TPU v7x, 32 devices: a whole 2x2x4 slice. The times are simulated.
32 devices in a mesh: wide: 8 (over y, x, core), narrow: 4 (over z).
Axes of the slice: x: 2, y: 2, z: 4, core: 2. Of those that a mesh axis runs over, the one named last changes fastest.
Arguments:
- tokens: bfloat16 [8192, 768], P('wide'), may hold values from -6 to 6
- segments: int32 [32, 256], P('wide'), may hold values from 0 to 1, never falling along the last dimension, each value on 1 to 200 neighbouring positions
- question: int32 [32], P('wide'), may hold values from 0 to 1, as said below
- answer_ids: int32 [2, 20], replicated, may hold values from 0 to 32127
- vocab_table: bfloat16 [32128, 768], P('wide'), may hold values from -6 to 6
- enc_gains: float32 [3, 768], replicated, may hold values from 0.5 to 1.5
- enc_inward: bfloat16 [768, 3, 768], P(None, None, 'narrow'), may hold values from -0.109375 to 0.109375
- encoder_bias: float32 [32, 12], P(None, 'narrow'), may hold values from -4 to 4
- enc_outward: bfloat16 [768, 768], P('narrow'), may hold values from -1.75 to 1.75
- enc_grow: bfloat16 [768, 3072], P(None, 'narrow'), may hold values from -0.21875 to 0.21875
- enc_shrink: bfloat16 [3072, 768], P('narrow'), may hold values from -0.109375 to 0.109375
- cross_key_value_weight: bfloat16 [768, 2, 768], P(None, None, 'narrow'), may hold values from -0.109375 to 0.109375
- dec_gains: float32 [3, 768], replicated, may hold values from 0.5 to 1.5
- dec_inward: bfloat16 [768, 3, 768], P(None, None, 'narrow'), may hold values from -0.109375 to 0.109375
- decoder_bias: float32 [32, 12], P(None, 'narrow'), may hold values from -4 to 4
- dec_outward: bfloat16 [768, 768], P('narrow'), may hold values from -1.75 to 1.75
- cross_query: bfloat16 [768, 768], P(None, 'narrow'), may hold values from -0.109375 to 0.109375
- cross_outward: bfloat16 [768, 768], P('narrow'), may hold values from -2.5 to 2.5
- dec_grow: bfloat16 [768, 3072], P(None, 'narrow'), may hold values from -0.21875 to 0.21875
- dec_shrink: bfloat16 [3072, 768], P('narrow'), may hold values from -0.109375 to 0.109375
- grad_memory: bfloat16 [8192, 768], P('wide'), may hold values from -6 to 6
- grad_output: bfloat16 [40, 768], replicated, may hold values from -6 to 6
Outputs:
- memory: bfloat16 [8192, 768], P('wide')
- output: bfloat16 [40, 768], replicated
- grad_tokens: bfloat16 [8192, 768], P('wide')
- grad_vocab_table: float32 [32128, 768], P('wide')
- grad_enc_gains: float32 [3, 768], replicated
- grad_enc_inward: float32 [768, 3, 768], P('wide', None, 'narrow')
- grad_enc_bias: float32 [32, 12], P(None, 'narrow')
- grad_enc_outward: float32 [768, 768], P('narrow', 'wide')
- grad_enc_grow: float32 [768, 3072], P('wide', 'narrow')
- grad_enc_shrink: float32 [3072, 768], P('narrow', 'wide')
- grad_cross_inward: float32 [768, 2, 768], P('wide', None, 'narrow')
- grad_dec_gains: float32 [3, 768], replicated
- grad_dec_inward: float32 [768, 3, 768], P(None, None, 'narrow')
- gradient_decoder_bias: float32 [32, 12], P(None, 'narrow')
- grad_dec_outward: float32 [768, 768], P('narrow')
- grad_cross_query: float32 [768, 768], P(None, 'narrow')
- grad_cross_outward: float32 [768, 768], P('narrow')
- grad_dec_grow: float32 [768, 3072], P(None, 'narrow')
- grad_dec_shrink: float32 [3072, 768], P('narrow')
Inputs may be any that keep to these rules, and one draw needn't show every extreme that they name: `segments`: along each row the passage ids never fall; each passage holds 1 to 200 tokens. Each aligned block of 2 rows holds every question id once, so every question owns exactly 16 rows; the first row's question also owns the last row.
All inputs are finite; a program needn't handle non-finite values.
Results may differ from a plain program's by a relative error of at most 0.024.
The roundings to bfloat16 on the way count: a program that leaves them out, or rounds other values in their place, can miss the bound.
Values may be sent and summed in bfloat16 or wider, within the bound.
No kernel may reach another device: no remote copies, remote signals or barrier semaphores. Data moves between devices by JAX's collectives and lax.ppermute only.
A program may use at most 192 MiB of HBM per device.

v0:
```python
import jax
import jax.numpy as jnp
from jax import lax
from jax.sharding import PartitionSpec as P

HD = 64


EPSILON = 1e-06
BOTH_EDGES = (12, 16, 23, 32, 46, 64, 91)
CAUSAL_EDGES = (19, 21, 24, 27, 31, 35, 40, 46, 52, 59, 67, 77, 87, 99, 113)
PRECISION_FULL = lax.Precision.HIGHEST
PRECISION_SINGLE = jnp.float32
BFLOAT = jnp.bfloat16
MASKED = -1e30


def merged(value, axis, join):
    pieces = jax.tree.map(lambda part: lax.all_gather(part, axis), value)
    head = jax.tree.map(lambda part: part[0], pieces)
    tail = jax.tree.map(lambda part: part[1:], pieces)
    total, _ = lax.scan(lambda total, piece: (join(total, piece), None), head, tail)
    return total


def bucket_both(length):
    places = jnp.arange(length, dtype=jnp.int32)
    offset = places[None, :] - places[:, None]
    spread = jnp.abs(offset)
    far_bucket = 8 + sum(((spread >= border).astype(jnp.int32) for border in BOTH_EDGES))
    near = jnp.where(spread < 8, spread, far_bucket)
    return jnp.where(offset > 0, 16, 0) + near


def causal_bucket_ids(length):
    places = jnp.arange(length, dtype=jnp.int32)
    spread = jnp.maximum(places[:, None] - places[None, :], 0)
    far_bucket = 16 + sum(((spread >= border).astype(jnp.int32) for border in CAUSAL_EDGES))
    return jnp.where(spread < 16, spread, far_bucket)


def bucket_lookup(buckets, bucket_count):
    return (jnp.arange(bucket_count, dtype=jnp.int32)[:, None, None] == buckets[None]).astype(
        PRECISION_SINGLE
    )


def smooth_gate(values):
    return jax.nn.gelu(values, approximate=True)


def smooth_gate_back(grown, upstream):
    _, pullback = jax.vjp(smooth_gate, grown)
    return pullback(upstream)[0]


def norm_rows(values, gain_row):
    inv_rms = lax.rsqrt(jnp.mean(values * values, axis=-1, keepdims=True) + EPSILON)
    return (values * inv_rms * gain_row, inv_rms)


def norm_back(gradient_normalized, values, inv_rms, gain_row):
    scaled = gradient_normalized * gain_row
    inv_cubed = inv_rms * inv_rms * inv_rms
    grad_values = inv_rms * scaled - values * inv_cubed * jnp.mean(
        scaled * values, axis=-1, keepdims=True
    )
    return (grad_values, gradient_normalized * values * inv_rms)


def merge_stats(first_pair, second_pair):
    first_max, first_total = first_pair
    second_max, second_total = second_pair
    highest = jnp.maximum(first_max, second_max)
    return (
        highest,
        first_total * jnp.exp(first_max - highest) + second_total * jnp.exp(second_max - highest),
    )


def attend_forward(normalized_rows, input_weight, outward, expanded_bias, allowed, head_size):
    row_total, length = (normalized_rows.shape[0], normalized_rows.shape[1])
    projection_output = jnp.einsum(
        "weq,qyb->yweb", normalized_rows, input_weight, preferred_element_type=PRECISION_SINGLE
    ).astype(BFLOAT)
    head_split = projection_output.reshape(3, row_total, length, -1, head_size)
    scores = (
        jnp.einsum(
            "rqhe,rkhe->rhqk", head_split[0], head_split[1], preferred_element_type=PRECISION_SINGLE
        )
        + expanded_bias[None]
    )
    masked = jnp.where(allowed, scores, MASKED)
    highest = jnp.max(masked, axis=-1, keepdims=True)
    exponent = jnp.exp(masked - highest)
    totals = jnp.sum(exponent, axis=-1, keepdims=True)
    weights = (exponent / totals).astype(BFLOAT)
    context = jnp.einsum(
        "rhqk,rkhe->rqhe", weights, head_split[2], preferred_element_type=PRECISION_SINGLE
    )
    context = context.reshape(row_total, length, -1).astype(BFLOAT)
    partial_value = jnp.einsum(
        "rli,id->rld", context, outward, preferred_element_type=PRECISION_SINGLE
    )
    return (partial_value, (projection_output, context, highest + jnp.log(totals)))


def attend_backward(
    grad_branch,
    normalized_rows,
    input_weight,
    outward,
    expanded_bias,
    allowed,
    saved_state,
    head_size,
):
    projection_output, context, logsum = saved_state
    row_total, length = (normalized_rows.shape[0], normalized_rows.shape[1])
    grad_outward = jnp.einsum(
        "rli,rld->id", context, grad_branch, preferred_element_type=PRECISION_SINGLE
    )
    grad_context = jnp.einsum(
        "rld,id->rli", grad_branch, outward, preferred_element_type=PRECISION_SINGLE
    ).astype(BFLOAT)
    head_split = projection_output.reshape(3, row_total, length, -1, head_size)
    grad_heads = grad_context.reshape(row_total, length, -1, head_size)
    scores = (
        jnp.einsum(
            "rqhe,rkhe->rhqk", head_split[0], head_split[1], preferred_element_type=PRECISION_SINGLE
        )
        + expanded_bias[None]
    )
    softmax_rows = jnp.exp(jnp.where(allowed, scores, MASKED) - logsum)
    grad_probs = jnp.einsum(
        "rqhe,rkhe->rhqk", grad_heads, head_split[2], preferred_element_type=PRECISION_SINGLE
    )
    grad_values = jnp.einsum(
        "rhqk,rqhe->rkhe",
        softmax_rows.astype(BFLOAT),
        grad_heads,
        preferred_element_type=PRECISION_SINGLE,
    )
    dot_term = jnp.sum(grad_probs * softmax_rows, axis=-1, keepdims=True)
    grad_scores = (softmax_rows * (grad_probs - dot_term)).astype(BFLOAT)
    grad_queries = jnp.einsum(
        "rhqk,rkhe->rqhe", grad_scores, head_split[1], preferred_element_type=PRECISION_SINGLE
    )
    grad_keys = jnp.einsum(
        "rhqk,rqhe->rkhe", grad_scores, head_split[0], preferred_element_type=PRECISION_SINGLE
    )
    gradient_projection_output = (
        jnp.stack([grad_queries, grad_keys, grad_values])
        .reshape(3, row_total, length, -1)
        .astype(BFLOAT)
    )
    gradient_input_weight = jnp.einsum(
        "sgq,psgb->qpb",
        normalized_rows,
        gradient_projection_output,
        preferred_element_type=PRECISION_SINGLE,
    )
    gradient_normalized = jnp.einsum(
        "pekj,apj->eka",
        gradient_projection_output,
        input_weight,
        preferred_element_type=PRECISION_SINGLE,
    )
    grad_bias = jnp.sum(grad_scores.astype(PRECISION_SINGLE), axis=0)
    return (gradient_normalized, gradient_input_weight, grad_outward, grad_bias)


def per_device(
    tokens,
    segments,
    question,
    answer_ids,
    vocab_table,
    enc_gains,
    enc_inward,
    encoder_bias,
    enc_outward,
    enc_grow,
    enc_shrink,
    cross_key_value_weight,
    dec_gains,
    dec_inward,
    decoder_bias,
    dec_outward,
    cross_query,
    cross_outward,
    dec_grow,
    dec_shrink,
    grad_memory,
    grad_output,
):
    row_count, row_length = segments.shape
    tok_count = tokens.shape[0]
    questions, answers = answer_ids.shape
    dec_count = questions * answers
    head_size = HD
    head_local = cross_query.shape[1] // head_size
    narrow_count = lax.axis_size("narrow")
    narrow_index = lax.axis_index("narrow")
    share_rows = tok_count // narrow_count
    share_start = narrow_index * share_rows

    def dec_sum(partial_value):
        return lax.psum(partial_value, "narrow")

    def to_rows(partial_value):
        return lax.psum(partial_value, "narrow")

    def gain_part(contrib):
        return jnp.sum(lax.dynamic_slice_in_dim(contrib, share_start, share_rows, 0), axis=0)

    encoder_bucket_indicator = bucket_lookup(bucket_both(row_length), encoder_bias.shape[0])
    encoder_bias_expanded = jnp.einsum(
        "uxe,uc->cxe", encoder_bucket_indicator, encoder_bias, precision=PRECISION_FULL
    )
    enc_allowed = (segments[:, :, None] == segments[:, None, :])[:, None]
    token_values = tokens.astype(PRECISION_SINGLE)
    first_values, first_inv = norm_rows(token_values, enc_gains[0])
    first_normed = first_values.astype(BFLOAT).reshape(row_count, row_length, -1)
    attn_partial, attn_saved = attend_forward(
        first_normed, enc_inward, enc_outward, encoder_bias_expanded, enc_allowed, head_size
    )
    hidden = token_values + to_rows(attn_partial.reshape(tok_count, -1))
    second_values, second_inv = norm_rows(hidden, enc_gains[1])
    second_normed = second_values.astype(BFLOAT)
    enc_grown = jnp.dot(second_normed, enc_grow, preferred_element_type=PRECISION_SINGLE)
    enc_act = smooth_gate(enc_grown).astype(BFLOAT)
    enc_summed = hidden + to_rows(
        jnp.dot(enc_act, enc_shrink, preferred_element_type=PRECISION_SINGLE)
    )
    final_values, final_inv = norm_rows(enc_summed, enc_gains[2])
    memory = final_values.astype(BFLOAT)
    cross_projected = jnp.einsum(
        "yo,ovw->vyw", memory, cross_key_value_weight, preferred_element_type=PRECISION_SINGLE
    ).astype(BFLOAT)
    cross_keys = cross_projected[0].reshape(tok_count, head_local, head_size)
    cross_values = cross_projected[1].reshape(tok_count, head_local, head_size)
    wide_index = lax.axis_index("wide")
    vocab_local = vocab_table.shape[0]
    flat_ids = answer_ids.reshape(-1)
    vocab_ids = wide_index * vocab_local + jnp.arange(vocab_local, dtype=jnp.int32)
    one_hot = (flat_ids[:, None] == vocab_ids[None, :]).astype(BFLOAT)
    embedded = lax.psum(
        jnp.dot(one_hot, vocab_table, preferred_element_type=PRECISION_SINGLE), "wide"
    )
    decoder_bucket_indicator = bucket_lookup(causal_bucket_ids(answers), decoder_bias.shape[0])
    decoder_bias_expanded = jnp.einsum(
        "uxe,uc->cxe", decoder_bucket_indicator, decoder_bias, precision=PRECISION_FULL
    )
    places = jnp.arange(answers, dtype=jnp.int32)
    dec_allowed = (places[:, None] >= places[None, :])[None, None]
    zero_values, zero_inv = norm_rows(embedded, dec_gains[0])
    dec_normed = zero_values.astype(BFLOAT).reshape(questions, answers, -1)
    self_partial, self_saved = attend_forward(
        dec_normed, dec_inward, dec_outward, decoder_bias_expanded, dec_allowed, head_size
    )
    dec_first = embedded + dec_sum(self_partial.reshape(dec_count, -1))
    cross_values_f, cross_inv = norm_rows(dec_first, dec_gains[1])
    cross_normed = cross_values_f.astype(BFLOAT)
    cross_queries = jnp.dot(
        cross_normed, cross_query, preferred_element_type=PRECISION_SINGLE
    ).astype(BFLOAT)
    query_heads = cross_queries.reshape(dec_count, head_local, head_size)
    token_question = jnp.repeat(question, row_length)
    dec_question = jnp.arange(dec_count, dtype=jnp.int32) // answers
    cross_allowed = (dec_question[:, None] == token_question[None, :])[None]
    cross_scores = jnp.einsum(
        "qhe,the->hqt", query_heads, cross_keys, preferred_element_type=PRECISION_SINGLE
    )
    cross_masked = jnp.where(cross_allowed, cross_scores, MASKED)
    local_max = jnp.max(cross_masked, axis=-1)
    local_total = jnp.sum(
        jnp.where(cross_allowed, jnp.exp(cross_masked - local_max[:, :, None]), 0.0), axis=-1
    )
    whole_max, whole_total = merged((local_max, local_total), "wide", merge_stats)
    cross_logsum = whole_max + jnp.log(whole_total)
    cross_probs = jnp.exp(cross_masked - cross_logsum[:, :, None])
    cross_weights = cross_probs.astype(BFLOAT)
    part_rounded = jnp.einsum(
        "hqt,the->qhe", cross_weights, cross_values, preferred_element_type=PRECISION_SINGLE
    )
    part_exact = jnp.einsum(
        "hqt,the->qhe", cross_probs, cross_values.astype(PRECISION_SINGLE), precision=PRECISION_FULL
    )
    cross_sums, cross_exact = lax.psum((part_rounded, part_exact), "wide")
    cross_context = cross_sums.reshape(dec_count, -1).astype(BFLOAT)
    dec_second = dec_first + dec_sum(
        jnp.dot(cross_context, cross_outward, preferred_element_type=PRECISION_SINGLE)
    )
    third_values, third_inv = norm_rows(dec_second, dec_gains[2])
    third_normed = third_values.astype(BFLOAT)
    dec_grown = jnp.dot(third_normed, dec_grow, preferred_element_type=PRECISION_SINGLE)
    dec_act = smooth_gate(dec_grown).astype(BFLOAT)
    output = dec_second + dec_sum(
        jnp.dot(dec_act, dec_shrink, preferred_element_type=PRECISION_SINGLE)
    )
    grad_out = grad_output.astype(PRECISION_SINGLE)
    grad_dec_shrink = jnp.einsum(
        "nf,nd->fd", dec_act, grad_output, preferred_element_type=PRECISION_SINGLE
    )
    grad_dec_act = jnp.einsum(
        "nd,fd->nf", grad_output, dec_shrink, preferred_element_type=PRECISION_SINGLE
    )
    grad_dec_grown = smooth_gate_back(dec_grown, grad_dec_act).astype(BFLOAT)
    grad_dec_grow = jnp.einsum(
        "nd,nf->df", third_normed, grad_dec_grown, preferred_element_type=PRECISION_SINGLE
    )
    third_part = dec_sum(
        jnp.einsum("nf,df->nd", grad_dec_grown, dec_grow, preferred_element_type=PRECISION_SINGLE)
    )
    grad_third, third_gain = norm_back(third_part, dec_second, third_inv, dec_gains[2])
    grad_dec_second = grad_out + grad_third
    grad_cbranch = grad_dec_second.astype(BFLOAT)
    grad_cross_outward = jnp.einsum(
        "qi,qd->id", cross_context, grad_cbranch, preferred_element_type=PRECISION_SINGLE
    )
    grad_cross_context = jnp.einsum(
        "qd,id->qi", grad_cbranch, cross_outward, preferred_element_type=PRECISION_SINGLE
    ).astype(BFLOAT)
    grad_cheads = grad_cross_context.reshape(dec_count, head_local, head_size)
    cross_delta = jnp.einsum(
        "qhe,qhe->hq", grad_cheads.astype(PRECISION_SINGLE), cross_exact, precision=PRECISION_FULL
    )
    grad_cprobs = jnp.einsum(
        "qhe,the->hqt", grad_cheads, cross_values, preferred_element_type=PRECISION_SINGLE
    )
    grad_cross_scores = (cross_probs * (grad_cprobs - cross_delta[:, :, None])).astype(BFLOAT)
    grad_kv_values = jnp.einsum(
        "hqt,qhe->the", cross_weights, grad_cheads, preferred_element_type=PRECISION_SINGLE
    )
    grad_kv_keys = jnp.einsum(
        "hqt,qhe->the", grad_cross_scores, query_heads, preferred_element_type=PRECISION_SINGLE
    )
    query_part = jnp.einsum(
        "hqt,the->qhe", grad_cross_scores, cross_keys, preferred_element_type=PRECISION_SINGLE
    )
    grad_cross_queries = lax.psum(query_part.reshape(dec_count, -1), "wide").astype(BFLOAT)
    grad_cross_query = jnp.einsum(
        "qd,qi->di", cross_normed, grad_cross_queries, preferred_element_type=PRECISION_SINGLE
    )
    gradient_cross_key_value = (
        jnp.stack([grad_kv_keys, grad_kv_values]).reshape(2, tok_count, -1).astype(BFLOAT)
    )
    grad_cross_inward = jnp.einsum(
        "ox,hoa->xha", memory, gradient_cross_key_value, preferred_element_type=PRECISION_SINGLE
    )
    memory_part = jnp.einsum(
        "pqa,ypa->qy",
        gradient_cross_key_value,
        cross_key_value_weight,
        preferred_element_type=PRECISION_SINGLE,
    )
    cross_part = dec_sum(
        jnp.einsum(
            "qi,di->qd", grad_cross_queries, cross_query, preferred_element_type=PRECISION_SINGLE
        )
    )
    grad_cross_norm, cross_gain = norm_back(cross_part, dec_first, cross_inv, dec_gains[1])
    grad_dec_first = grad_dec_second + grad_cross_norm
    grad_sbranch = grad_dec_first.astype(BFLOAT).reshape(questions, answers, -1)
    zero_part, grad_dec_inward, grad_dec_outward, decoder_bias_rows = attend_backward(
        grad_sbranch,
        dec_normed,
        dec_inward,
        dec_outward,
        decoder_bias_expanded,
        dec_allowed,
        self_saved,
        head_size,
    )
    grad_zero, zero_gain = norm_back(
        dec_sum(zero_part.reshape(dec_count, -1)), embedded, zero_inv, dec_gains[0]
    )
    grad_embedded = grad_dec_first + grad_zero
    grad_vocab_table = jnp.einsum(
        "qv,qd->vd", one_hot.astype(PRECISION_SINGLE), grad_embedded, precision=PRECISION_FULL
    )
    gradient_decoder_bias = jnp.einsum(
        "jia,xia->xj", decoder_bias_rows, decoder_bucket_indicator, precision=PRECISION_FULL
    )
    grad_dec_gains = jnp.stack(
        [jnp.sum(zero_gain, axis=0), jnp.sum(cross_gain, axis=0), jnp.sum(third_gain, axis=0)]
    )
    grad_final = to_rows(memory_part) + grad_memory.astype(PRECISION_SINGLE)
    grad_enc_summed, final_gain = norm_back(grad_final, enc_summed, final_inv, enc_gains[2])
    grad_branch_ffn = grad_enc_summed.astype(BFLOAT)
    grad_enc_shrink = jnp.einsum(
        "nf,nd->fd", enc_act, grad_branch_ffn, preferred_element_type=PRECISION_SINGLE
    )
    grad_enc_act = jnp.einsum(
        "nd,fd->nf", grad_branch_ffn, enc_shrink, preferred_element_type=PRECISION_SINGLE
    )
    grad_enc_grown = smooth_gate_back(enc_grown, grad_enc_act).astype(BFLOAT)
    grad_enc_grow = jnp.einsum(
        "nd,nf->df", second_normed, grad_enc_grown, preferred_element_type=PRECISION_SINGLE
    )
    second_part = to_rows(
        jnp.einsum("nf,df->nd", grad_enc_grown, enc_grow, preferred_element_type=PRECISION_SINGLE)
    )
    grad_second_norm, second_gain = norm_back(second_part, hidden, second_inv, enc_gains[1])
    grad_enc_hidden = grad_enc_summed + grad_second_norm
    grad_branch_attn = grad_enc_hidden.astype(BFLOAT).reshape(row_count, row_length, -1)
    first_part, grad_enc_inward, grad_enc_outward, encoder_bias_rows = attend_backward(
        grad_branch_attn,
        first_normed,
        enc_inward,
        enc_outward,
        encoder_bias_expanded,
        enc_allowed,
        attn_saved,
        head_size,
    )
    grad_first_norm, first_gain = norm_back(
        to_rows(first_part.reshape(tok_count, -1)), token_values, first_inv, enc_gains[0]
    )
    grad_tokens = (grad_enc_hidden + grad_first_norm).astype(BFLOAT)
    enc_gain_terms = jnp.stack(
        [gain_part(first_gain), gain_part(second_gain), gain_part(final_gain)]
    )
    enc_bias_local = jnp.einsum(
        "jia,xia->xj", encoder_bias_rows, encoder_bucket_indicator, precision=PRECISION_FULL
    )
    bias_padded = jnp.zeros((encoder_bias.shape[0], head_local * narrow_count), PRECISION_SINGLE)
    bias_padded = lax.dynamic_update_slice(
        bias_padded, enc_bias_local, (jnp.int32(0), narrow_index * head_local)
    )
    enc_gain_sums, enc_bias_sums = lax.psum((enc_gain_terms, bias_padded), ("wide", "narrow"))
    grad_enc_bias = lax.dynamic_slice_in_dim(
        enc_bias_sums, narrow_index * head_local, head_local, 1
    )
    sent_cross, sent_grow, sent_shrink, sent_inward, sent_outward = (
        lax.psum_scatter(grad_cross_inward, "wide", scatter_dimension=0, tiled=True),
        lax.psum_scatter(grad_enc_grow, "wide", scatter_dimension=0, tiled=True),
        lax.psum_scatter(grad_enc_shrink, "wide", scatter_dimension=1, tiled=True),
        lax.psum_scatter(grad_enc_inward, "wide", scatter_dimension=0, tiled=True),
        lax.psum_scatter(grad_enc_outward, "wide", scatter_dimension=1, tiled=True),
    )
    return (
        memory,
        output.astype(BFLOAT),
        grad_tokens,
        grad_vocab_table,
        enc_gain_sums,
        sent_inward,
        grad_enc_bias,
        sent_outward,
        sent_grow,
        sent_shrink,
        sent_cross,
        grad_dec_gains,
        grad_dec_inward,
        gradient_decoder_bias,
        grad_dec_outward,
        grad_cross_query,
        grad_cross_outward,
        grad_dec_grow,
        grad_dec_shrink,
    )


def solution(mesh):
    in_specs = (
        P("wide", None),
        P("wide", None),
        P("wide"),
        P(),
        P("wide", None),
        P(),
        P(None, None, "narrow"),
        P(None, "narrow"),
        P("narrow", None),
        P(None, "narrow"),
        P("narrow", None),
        P(None, None, "narrow"),
        P(),
        P(None, None, "narrow"),
        P(None, "narrow"),
        P("narrow", None),
        P(None, "narrow"),
        P("narrow", None),
        P(None, "narrow"),
        P("narrow", None),
        P("wide", None),
        P(),
    )
    out_specs = (
        P("wide", None),
        P(),
        P("wide", None),
        P("wide", None),
        P(),
        P("wide", None, "narrow"),
        P(None, "narrow"),
        P("narrow", "wide"),
        P("wide", "narrow"),
        P("narrow", "wide"),
        P("wide", None, "narrow"),
        P(),
        P(None, None, "narrow"),
        P(None, "narrow"),
        P("narrow", None),
        P(None, "narrow"),
        P("narrow", None),
        P(None, "narrow"),
        P("narrow", None),
    )
    return jax.shard_map(
        per_device, mesh=mesh, in_specs=in_specs, out_specs=out_specs, check_vma=False
    )
```

profile of v0, /device:TPU:0, one launch (start us, length us, event | category | flops | bytes accessed | tf_op | source)
XLA Modules:
  0.0 1090.0 jit_solution(13159831470264296454)
XLA Ops:
  8.7 4.6 fusion.43
  19.8 12.0 %copy.109 = pred[32,256,256]{2,0,1:T(32,128)(4,1)S(1)} copy(pred[32,256,256]{1,0,2:T(32,128)(4,1)S(1)} %iota_compare_fusion) | data formatting | bytes 4194304 | tf_op jit(solution)/shard_map/eq | solution.py:43
  31.8 3.1 convolution_bitcast_fusion.4
  34.9 2.4 copy.110
  37.3 2.0 fusion.156
  41.7 2.3 fusion.159
  45.9 22.5 %all-reduce.16.cloned.1.call-done = f32[40,768]{1,0:T(8,128)} async-done(((f32[40,768]{1,0:T(8,128)}), f32[40,768]{1,0:T(8,128)}) %all-reduce.16.cloned.1.call-update) | async-done | bytes 122896 | tf_op jit(solution)/shard_map/psum | solution.py:248
  74.9 117.8 %all-reduce.14.cloned.1.call-done = f32[1024,768]{1,0:T(8,128)} async-done(((f32[1024,768]{1,0:T(8,128)}), f32[1024,768]{1,0:T(8,128)}) %all-reduce.14.cloned.1.call-update) | async-done | bytes 3145744 | tf_op jit(solution)/shard_map/psum | solution.py:212
  192.6 2.5 multiply_reduce_fusion.4
  200.0 3.6 fusion.150
  204.5 123.8 %all-reduce.28.cloned.1.call-done = (f32[1024,768]{1,0:T(8,128)}, f32[40,768]{1,0:T(8,128)}) async-done(((f32[1024,768]{1,0:T(8,128)}, f32[40,768]{1,0:T(8,128)}), (f32[1024,768]{1,0:T(8,128)}, f32[40,768]{1,0:T(8,128)})) %all-reduce.28.cloned.1.call-update) | async-done | bytes 3268624 | tf_op jit(solution)/shard_map/psum | solution.py:212
  328.3 4.9 multiply_reduce_fusion.3
  334.8 2.2 multiply_convert_fusion.1
  337.1 2.3 fusion.161
  340.6 9.0 all-gather.2
  349.9 8.9 all-gather.3
  359.9 25.5 %all-reduce.1 = (bf16[40,3,64]{2,0,1:T(8,128)(2,1)}, f32[40,3,64]{2,0,1:T(8,128)}) all-reduce(f32[40,3,64]{2,0,1:T(8,128)S(1)} %convolution_bitcast_fusion.10, f32[40,3,64]{2,0,1:T(8,128)S(1)} %convolution_bitcast_fusion.8), channel_id=1, replica_groups=mesh['wide'=8,'narrow'=4] {'wide'}, use_global_device_ids=true, to_apply=%region_17.18 | all-reduce | flops 15360 | bytes 107520 | tf_op jit(solution)/shard_map/psum | solution.py:290
  388.1 2.4 fusion.163
  390.6 29.0 %all-reduce.18.cloned.1.call-done = f32[40,768]{1,0:T(8,128)} async-done(((f32[40,768]{1,0:T(8,128)}), f32[40,768]{1,0:T(8,128)}) %all-reduce.18.cloned.1.call-update) | async-done | bytes 122896 | tf_op jit(solution)/shard_map/psum | solution.py:209
  425.5 34.2 %all-reduce.20.cloned.1.call-done = f32[40,768]{1,0:T(8,128)} async-done(((f32[40,768]{1,0:T(8,128)}), f32[40,768]{1,0:T(8,128)}) %all-reduce.20.cloned.1.call-update) | async-done | bytes 122896 | tf_op jit(solution)/shard_map/psum | solution.py:209
  467.7 3.9 convolution_bitcast_fusion.1
  472.9 24.1 %psum.131 = bf16[40,192]{1,0:T(8,128)(2,1)S(1)} all-reduce(f32[40,192]{1,0:T(8,128)S(1)} %reshape.430), channel_id=1, replica_groups=mesh['wide'=8,'narrow'=4] {'wide'}, use_global_device_ids=true, to_apply=%region_31.32 | all-reduce | flops 7680 | bytes 46080 | tf_op jit(solution)/shard_map/psum | solution.py:342
  497.9 95.0 %all-reduce.22.cloned.1.call-done = f32[1024,768]{1,0:T(8,128)} async-done(((f32[1024,768]{1,0:T(8,128)}), f32[1024,768]{1,0:T(8,128)}) %all-reduce.22.cloned.1.call-update) | async-done | bytes 3145744 | tf_op jit(solution)/shard_map/psum | solution.py:212
  592.8 4.0 multiply_reduce_fusion.2
  599.9 3.0 fusion.16
  604.0 3.2 fusion.165
  609.5 3.3 fusion.21
  612.9 119.0 %all-reduce.26.cloned.1.call-done = (f32[1024,768]{1,0:T(8,128)}, f32[40,768]{1,0:T(8,128)}) async-done(((f32[1024,768]{1,0:T(8,128)}, f32[40,768]{1,0:T(8,128)}), (f32[1024,768]{1,0:T(8,128)}, f32[40,768]{1,0:T(8,128)})) %all-reduce.26.cloned.1.call-update) | async-done | bytes 3268624 | tf_op jit(solution)/shard_map/psum | solution.py:212
  745.7 2.3 multiply_reduce_fusion.1
  753.1 5.0 fusion.152
  762.2 2.1 convolution_convert_fusion.3
  775.7 3.1 convolution_bitcast_fusion
  779.0 6.0 fusion.51
  785.1 4.5 fusion.148
  789.7 3.3 convert_element_type.361
  797.6 2.8 fusion.146
  800.4 2.9 fusion.144
  804.0 2.0 fusion.104
  812.3 2.7 convolution_bitcast_fusion.3
  816.3 4.1 convolution_bitcast_fusion.13
  820.6 2.8 convolution_bitcast_fusion.2
  826.2 117.9 %all-reduce.24.cloned.1.call-done = (f32[40,768]{1,0:T(8,128)}, f32[1024,768]{1,0:T(8,128)}, f32[40,768]{1,0:T(8,128)}) async-done(((f32[40,768]{1,0:T(8,128)}, f32[1024,768]{1,0:T(8,128)}, f32[40,768]{1,0:T(8,128)}), (f32[40,768]{1,0:T(8,128)}, f32[1024,768]{1,0:T(8,128)}, f32[40,768]{1,0:T(8,128)})) %all-reduce.24.cloned.1.call-update) | async-done | bytes 3391504 | tf_op jit(solution)/shard_map/psum | solution.py:209
  946.9 39.7 %all-reduce = (f32[3,768]{1,0:T(4,128)}, f32[32,12]{0,1:T(8,128)S(1)}) all-reduce(f32[3,768]{1,0:T(4,128)S(1)} %pad_maximum_fusion.5, f32[32,12]{0,1:T(8,128)S(1)} %dynamic_update_slice.3), channel_id=1, replica_groups=mesh['wide'=8,'narrow'=4] {'wide','narrow'}, use_global_device_ids=true, to_apply=%region_40.41 | all-reduce | flops 2688 | bytes 21504 | tf_op jit(solution)/shard_map/psum | solution.py:432
  987.7 2.4 fusion.9
  990.8 3.4 fusion.8
  994.3 8.1 fusion.41
  1002.4 34.1 %reduce-scatter.10.cloned.1.call-done = f32[96,768]{1,0:T(8,128)} async-done(((f32[768,768]{1,0:T(8,128)}), f32[96,768]{1,0:T(8,128)}) %reduce-scatter.10.cloned.1.call-update) | async-done | bytes 294928 | tf_op jit(solution)/shard_map/reduce_scatter | solution.py:438
  1036.5 46.8 %reduce-scatter.8.cloned.1.call-done = f32[96,3,192]{2,0,1:T(8,128)} async-done(((f32[768,3,192]{2,0,1:T(8,128)}), f32[96,3,192]{2,0,1:T(8,128)}) %reduce-scatter.8.cloned.1.call-update) | async-done | bytes 221200 | tf_op jit(solution)/shard_map/reduce_scatter | solution.py:440
  (433 shorter events, 108.4 us)
Async XLA Ops:
  7.2 192.8 %copy-start = (bf16[768,768]{1,0:T(8,128)(2,1)S(1)}, bf16[768,768]{1,0:T(8,128)(2,1)}, u32[]{:S(2)}) copy-start(bf16[768,768]{1,0:T(8,128)(2,1)} %param.34) | copy-start | bytes 3538948
  7.2 61.2 %all-reduce.16.cloned.1.call-start = ((), (), s32[]{:S(2)}) async-start(), calls=%async_computation.6 | async-start | bytes 245760 | tf_op jit(solution)/shard_map/psum | solution.py:248
  13.3 179.3 %all-reduce.14.cloned.1.call-start = ((), (), s32[]{:S(2)}) async-start(), calls=%async_computation.5 | async-start | bytes 6291456 | tf_op jit(solution)/shard_map/psum | solution.py:212
  15.2 319.6 %copy-start.79 = (f32[768]{0:T(1024)}, f32[768]{0:T(1024)S(1)}, u32[]{:S(2)}) copy-start(f32[768]{0:T(1024)S(1)} %get-tuple-element.115) | copy-start | bytes 9220
  18.6 18.7 %copy-start.17 = (bf16[1,4,256,192]{2,3,0,1:T(8,128)(2,1)}, bf16[1,4,256,192]{2,3,0,1:T(8,128)(2,1)S(1)}, u32[]{:S(2)}) copy-start(bf16[1,4,256,192]{2,3,0,1:T(8,128)(2,1)S(1)} %get-tuple-element.159) | copy-start | bytes 1179652
  18.6 18.7 %copy-start.18 = (bf16[1,4,256,192]{2,3,0,1:T(8,128)(2,1)}, bf16[1,4,256,192]{2,3,0,1:T(8,128)(2,1)S(1)}, u32[]{:S(2)}) copy-start(bf16[1,4,256,192]{2,3,0,1:T(8,128)(2,1)S(1)} %get-tuple-element.160) | copy-start | bytes 1179652
  18.6 13.2 %copy-start.116 = (f32[32,3]{0,1:T(4,128)S(1)}, f32[32,3]{0,1:T(4,128)}, u32[]{:S(2)}) copy-start(f32[32,3]{0,1:T(4,128)} %param.31) | copy-start | bytes 1156
  44.0 30.1 %copy-start.43 = (bf16[192,768]{1,0:T(8,128)(2,1)S(1)}, bf16[192,768]{1,0:T(8,128)(2,1)}, u32[]{:S(2)}) copy-start(bf16[192,768]{1,0:T(8,128)(2,1)} %param.39) | copy-start | bytes 884740
  44.0 284.3 %all-reduce.28.cloned.1.call-start = ((), (), s32[]{:S(2)}) async-start(), calls=%async_computation.17 | async-start | bytes 6537216 | tf_op jit(solution)/shard_map/psum | solution.py:212
  44.3 25.7 %copy-start.86 = (s32[20,20]{0,1:T(8,128)}, s32[20,20]{0,1:T(8,128)S(1)}, u32[]{:S(2)}) copy-start(s32[20,20]{0,1:T(8,128)S(1)} %compare_select_fusion.1) | copy-start | bytes 4804
  45.9 149.2 %copy-start.83 = (f32[768]{0:T(1024)}, f32[768]{0:T(1024)S(1)}, u32[]{:S(2)}) copy-start(f32[768]{0:T(1024)S(1)} %get-tuple-element.113) | copy-start | bytes 9220
  71.0 124.1 %copy-start.49 = (bf16[2,20,768,1]{2,1,0,3:T(8,128)(2,1)}, bf16[2,20,768,1]{2,1,0,3:T(8,128)(2,1)S(1)}, u32[]{:S(2)}) copy-start(bf16[2,20,768,1]{2,1,0,3:T(8,128)(2,1)S(1)} %reshape.454) | copy-start | bytes 184324
  72.7 122.4 %copy-start.69 = (bf16[2,20,3,64]{3,2,1,0:T(4,128)(2,1)}, bf16[2,20,3,64]{3,2,1,0:T(4,128)(2,1)S(1)}, u32[]{:S(2)}) copy-start(bf16[2,20,3,64]{3,2,1,0:T(4,128)(2,1)S(1)} %reshape.482) | copy-start | bytes 46084
  72.9 122.2 %copy-start.60 = (bf16[2,20,3,64]{3,2,1,0:T(4,128)(2,1)}, bf16[2,20,3,64]{3,2,1,0:T(4,128)(2,1)S(1)}, u32[]{:S(2)}) copy-start(bf16[2,20,3,64]{3,2,1,0:T(4,128)(2,1)S(1)} %reshape.483) | copy-start | bytes 46084
  73.1 122.1 %copy-start.93 = (f32[2,3,20]{2,1,0:T(4,128)}, f32[2,3,20]{2,1,0:T(4,128)S(1)}, u32[]{:S(2)}) copy-start(f32[2,3,20]{2,1,0:T(4,128)S(1)} %get-tuple-element.181) | copy-start | bytes 1444
  73.7 121.5 %copy-start.103 = (f32[2,3,20]{2,1,0:T(4,128)}, f32[2,3,20]{2,1,0:T(4,128)S(1)}, u32[]{:S(2)}) copy-start(f32[2,3,20]{2,1,0:T(4,128)S(1)} %fusion.91) | copy-start | bytes 1444
  73.9 121.2 %copy-start.57 = (bf16[2,20,3,64]{3,2,1,0:T(4,128)(2,1)}, bf16[2,20,3,64]{3,2,1,0:T(4,128)(2,1)S(1)}, u32[]{:S(2)}) copy-start(bf16[2,20,3,64]{3,2,1,0:T(4,128)(2,1)S(1)} %copy.122) | copy-start | bytes 46084
  74.9 122.0 %copy-start.95 = (f32[768]{0:T(1024)S(1)}, f32[768]{0:T(1024)}, u32[]{:S(2)}) copy-start(f32[768]{0:T(1024)} %get-tuple-element.117) | copy-start | bytes 9220
  203.7 215.9 %all-reduce.18.cloned.1.call-start = ((), (), s32[]{:S(2)}) async-start(), calls=%async_computation.7 | async-start | bytes 245760 | tf_op jit(solution)/shard_map/psum | solution.py:209
  339.5 48.6 %copy-start.50 = (bf16[40,768]{1,0:T(8,128)(2,1)S(1)}, bf16[40,768]{1,0:T(8,128)(2,1)}, u32[]{:S(2)}) copy-start(bf16[40,768]{1,0:T(8,128)(2,1)} %param.45) | copy-start | bytes 184324
  340.3 81.4 %copy-start.15 = (bf16[768,768]{1,0:T(8,128)(2,1)S(1)}, bf16[768,768]{1,0:T(8,128)(2,1)}, u32[]{:S(2)}) copy-start(bf16[768,768]{1,0:T(8,128)(2,1)} %param.42) | copy-start | bytes 3538948
  388.1 71.6 %all-reduce.20.cloned.1.call-start = ((), (), s32[]{:S(2)}) async-start(), calls=%async_computation.8 | async-start | bytes 245760 | tf_op jit(solution)/shard_map/psum | solution.py:209
  425.4 167.4 %all-reduce.22.cloned.1.call-start = ((), (), s32[]{:S(2)}) async-start(), calls=%async_computation.9 | async-start | bytes 6291456 | tf_op jit(solution)/shard_map/psum | solution.py:212
  471.6 25.5 %copy-start.42 = (bf16[768,192]{0,1:T(8,128)(2,1)S(1)}, bf16[768,192]{0,1:T(8,128)(2,1)}, u32[]{:S(2)}) copy-start(bf16[768,192]{0,1:T(8,128)(2,1)} %param.40) | copy-start | bytes 884740
  471.6 121.3 %copy-start.80 = (f32[768]{0:T(1024)S(1)}, f32[768]{0:T(1024)}, u32[]{:S(2)}) copy-start(f32[768]{0:T(1024)} %copy-done.79) | copy-start | bytes 9220
  471.6 260.3 %all-reduce.26.cloned.1.call-start = ((), (), s32[]{:S(2)}) async-start(), calls=%async_computation.16 | async-start | bytes 6537216 | tf_op jit(solution)/shard_map/psum | solution.py:212
  497.0 99.8 %copy-start.68 = (bf16[40,192]{1,0:T(8,128)(2,1)}, bf16[40,192]{1,0:T(8,128)(2,1)S(1)}, u32[]{:S(2)}) copy-start(bf16[40,192]{1,0:T(8,128)(2,1)S(1)} %psum.131) | copy-start | bytes 46084
  497.9 99.0 %copy-start.91 = (f32[1024]{0:T(1024)S(1)}, f32[1024]{0:T(1024)}, u32[]{:S(2)}) copy-start(f32[1024]{0:T(1024)} %copy-done.90) | copy-start | bytes 12292
  497.9 99.0 %copy-start.100 = (f32[1024]{0:T(1024)S(1)}, f32[1024]{0:T(1024)}, u32[]{:S(2)}) copy-start(f32[1024]{0:T(1024)} %get-tuple-element.171) | copy-start | bytes 12292
  607.3 200.6 %reduce-scatter.14.cloned.1.call-start = ((), (), s32[]{:S(2)}) async-start(), calls=%async_computation.13 | async-start | bytes 1769472 | tf_op jit(solution)/shard_map/reduce_scatter | solution.py:437
  609.5 130.5 %copy-start.27 = (f32[2,3,20,20]{2,3,1,0:T(8,128)S(1)}, f32[2,3,20,20]{2,3,1,0:T(8,128)}, u32[]{:S(2)}) copy-start(f32[2,3,20,20]{2,3,1,0:T(8,128)} %copy-done.26) | copy-start | bytes 28804
  612.8 132.9 %copy-start.5 = (f32[1024,768]{1,0:T(8,128)S(1)}, f32[1024,768]{1,0:T(8,128)}, u32[]{:S(2)}) copy-start(f32[1024,768]{1,0:T(8,128)} %copy-done.4) | copy-start | bytes 9437188
  612.8 132.9 %copy-start.96 = (f32[768]{0:T(1024)S(1)}, f32[768]{0:T(1024)}, u32[]{:S(2)}) copy-start(f32[768]{0:T(1024)} %get-tuple-element.117) | copy-start | bytes 9220
  612.8 211.7 %reduce-scatter.16.cloned.1.call-start = ((), (), s32[]{:S(2)}) async-start(), calls=%async_computation.14 | async-start | bytes 884736
  772.0 172.2 %all-reduce.24.cloned.1.call-start = ((), (), s32[]{:S(2)}) async-start(), calls=%async_computation.15 | async-start | bytes 6782976 | tf_op jit(solution)/shard_map/psum | solution.py:209
  778.9 223.5 %reduce-scatter.12.cloned.1.call-start = ((), (), s32[]{:S(2)}) async-start(), calls=%async_computation.12 | async-start | bytes 2654208 | tf_op jit(solution)/shard_map/reduce_scatter | solution.py:439
  785.0 251.5 %reduce-scatter.10.cloned.1.call-start = ((), (), s32[]{:S(2)}) async-start(), calls=%async_computation.11 | async-start | bytes 2654208 | tf_op jit(solution)/shard_map/reduce_scatter | solution.py:438
  789.6 293.7 %reduce-scatter.8.cloned.1.call-start = ((), (), s32[]{:S(2)}) async-start(), calls=%async_computation.10 | async-start | bytes 2654208 | tf_op jit(solution)/shard_map/reduce_scatter | solution.py:440
  820.5 123.6 %copy-start.24 = (f32[40,768]{1,0:T(8,128)S(1)}, f32[40,768]{1,0:T(8,128)}, u32[]{:S(2)}) copy-start(f32[40,768]{1,0:T(8,128)} %all-reduce.16.cloned.1.call-done) | copy-start | bytes 368644
  820.5 123.6 %copy-start.84 = (f32[768]{0:T(1024)S(1)}, f32[768]{0:T(1024)}, u32[]{:S(2)}) copy-start(f32[768]{0:T(1024)} %copy-done.83) | copy-start | bytes 9220
  820.6 123.6 %copy-start.112 = (f32[40]{0:T(128)S(1)}, f32[40]{0:T(128)}, u32[]{:S(2)}) copy-start(f32[40]{0:T(128)} %copy-done.111) | copy-start | bytes 484
  820.6 124.7 %copy-start.113 = (f32[256]{0:T(256)S(1)}, f32[256]{0:T(256)}, u32[]{:S(2)}) copy-start(f32[256]{0:T(256)} %dynamic-slice) | copy-start | bytes 3076
  823.4 164.3 %copy-start.9 = (bf16[1024,768]{1,0:T(8,128)(2,1)S(1)}, bf16[1024,768]{1,0:T(8,128)(2,1)}, u32[]{:S(2)}) copy-start(bf16[1024,768]{1,0:T(8,128)(2,1)} %param.24) | copy-start | bytes 4718596
  823.4 164.3 %copy-start.78 = (f32[768]{0:T(1024)S(1)}, f32[768]{0:T(1024)}, u32[]{:S(2)}) copy-start(f32[768]{0:T(1024)} %copy-done.77) | copy-start | bytes 9220
  945.3 44.9 %copy-start.72 = (f32[40,768]{1,0:T(8,128)S(1)}, f32[40,768]{1,0:T(8,128)}, u32[]{:S(2)}) copy-start(f32[40,768]{1,0:T(8,128)} %get-tuple-element.132) | copy-start | bytes 368644
  945.3 45.5 %copy-start.89 = (f32[1024]{0:T(1024)S(1)}, f32[1024]{0:T(1024)}, u32[]{:S(2)}) copy-start(f32[1024]{0:T(1024)} %copy-done.88) | copy-start | bytes 12292
  945.3 45.5 %copy-start.99 = (f32[1024]{0:T(1024)S(1)}, f32[1024]{0:T(1024)}, u32[]{:S(2)}) copy-start(f32[1024]{0:T(1024)} %get-tuple-element.167) | copy-start | bytes 12292
  994.3 89.0 %copy-start.1 = (bf16[768,768]{1,0:T(8,128)(2,1)S(1)}, bf16[768,768]{1,0:T(8,128)(2,1)}, u32[]{:S(2)}) copy-start(bf16[768,768]{1,0:T(8,128)(2,1)} %param.34) | copy-start | bytes 3538948
  (92 other events, 355.5 us)
Sparse Core Ops, SparseCore 0:
  13.4 54.9 all-reduce.15
  71.5 121.1 all-reduce.13
  203.8 124.4 all-reduce.27
  388.2 31.2 all-reduce.17
  425.5 34.0 all-reduce.19
  471.7 121.0 all-reduce.21
  607.4 124.4 all-reduce.25
  735.5 37.4 reduce-scatter.13
  776.5 35.0 reduce-scatter.15
  814.2 129.8 all-reduce.23
  948.4 41.5 reduce-scatter.11
  993.8 42.6 reduce-scatter.9
  1040.8 42.4 reduce-scatter.7
where the time goes:
time: 1100 us; the launch traced here: 1090 us
  waiting for transfers between devices  740 us (67%)
  matrix products  114 us (10%)
  blocking collectives  107 us (10%)
  other arithmetic  58.5 us (5%)
  local copies, waits for them, and re-layouts  53.4 us (5%)
  between operations  15.5 us (1%)
    psum x4, waiting for transfers between devices, to_rows(): return lax.psum(partial_value, 'narrow')  456 us
    psum x3, waiting for transfers between devices, dec_sum(): return lax.psum(partial_value, 'narrow')  181 us
    reduce_scatter x1, waiting for transfers between devices, per_device(): lax.psum_scatter(grad_enc_inward, 'wide', scatter_dimension=0, tiled=True)  46.8 us
    psum x1, blocking collectives, per_device(): lax.psum((enc_gain_terms, bias_padded), ('wide', 'narrow'))  39.7 us
    reduce_scatter x1, waiting for transfers between devices, per_device(): lax.psum_scatter(grad_enc_grow, 'wide', scatter_dimension=0, tiled=True)  34.1 us
    psum x1, blocking collectives, per_device(): cross_sums, cross_exact = lax.psum((part_rounded, part_exact), 'wide')  25.5 us
    psum x1, blocking collectives, per_device(): lax.psum(query_part.reshape(dec_count, -1), 'wide').astype(BFLOAT)  24.1 us
    psum x1, waiting for transfers between devices, per_device(): lax.psum(jnp.dot(one_hot, vocab_table, preferred_element_type=PRECISION_S...  22.5 us
  transfers between devices with their start and end apart: 13, of which 10 were waited for; matrix products, arithmetic and copies ran while one was open for 14% of the time, Pallas kernels for 0%

commit v1 on v0

v1 whole, which is shorter than its diff:
```python
import jax
import jax.numpy as jnp
from jax import lax
from jax.experimental import pallas as pl
from jax.experimental.pallas import tpu as pltpu
from jax.sharding import PartitionSpec as P

HD = 64
EPSILON = 1e-06
BOTH_EDGES = (12, 16, 23, 32, 46, 64, 91)
CAUSAL_EDGES = (19, 21, 24, 27, 31, 35, 40, 46, 52, 59, 67, 77, 87, 99, 113)
FULL = lax.Precision.HIGHEST
F32 = jnp.float32
BF16 = jnp.bfloat16
MASKED = -1e30


def bits_of(count):
    return [1 << k for k in range(count.bit_length() - 1)]


def swap(value, axis, bit):
    count = lax.axis_size(axis)
    pairs = [(i, i ^ bit) for i in range(count)]
    return jax.tree.map(lambda part: lax.ppermute(part, axis, pairs), value)


def exchange_sum(value, axis):
    for bit in bits_of(lax.axis_size(axis)):
        value = jax.tree.map(jnp.add, value, swap(value, axis, bit))
    return value


def rounded_sum(*parts):
    return sum(part.astype(F32) for part in parts).astype(BF16)


def place(starts, jobs, shape):
    arrays = [array for array, _ in jobs]

    def kernel(starts_ref, *refs):
        pieces, out, sem = refs[: len(arrays)], refs[len(arrays)], refs[len(arrays) + 1]
        copies = []
        for piece, (_, targets) in zip(pieces, jobs):
            for source, index, first, rows in targets:
                z, w = starts_ref[index, 0], starts_ref[index, 1]
                if source is None:
                    copies.append((piece, out.at[z]))
                else:
                    copies.append((piece.at[source], out.at[z, w, pl.ds(first, rows)]))
        for number, (source, target) in enumerate(copies):
            pltpu.make_async_copy(source, target, sem.at[number]).start()
        for number, (source, target) in enumerate(copies):
            pltpu.make_async_copy(source, target, sem.at[number]).wait()

    count = sum(len(targets) for _, targets in jobs)
    return pl.pallas_call(
        kernel,
        out_shape=jax.ShapeDtypeStruct(shape, arrays[0].dtype),
        grid_spec=pltpu.PrefetchScalarGridSpec(
            num_scalar_prefetch=1,
            in_specs=[pl.BlockSpec(memory_space=pl.ANY)] * len(arrays),
            out_specs=pl.BlockSpec(memory_space=pl.ANY),
            grid=(1,),
            scratch_shapes=[pltpu.SemaphoreType.DMA((count,))],
        ),
    )(starts, *arrays)


def gather_weights(quarter):
    blocks, rows, lanes = quarter.shape
    parts = lax.axis_size("narrow")
    wide_at, narrow_at = lax.axis_index("wide"), lax.axis_index("narrow")
    mine = lax.dynamic_index_in_dim(quarter, wide_at, 0, keepdims=False)
    others = jnp.stack([swap(mine, "narrow", offset) for offset in range(1, parts)])
    pieces = [(0, 0, others)]
    bits = bits_of(blocks)[::-1]
    if len(bits) >= 3 and rows % 32 == 0:
        a, b = bits[:2]
        half = rows // 2
        over_a, over_b = swap(others, "wide", a), swap(others, "wide", b)
        far_a = swap(over_b[:, :half], "wide", a)
        far_b = swap(over_a[:, half:], "wide", b)
        pieces += [(a, 0, over_a), (b, 0, over_b), (a ^ b, 0, far_a), (a ^ b, half, far_b)]
        bits = bits[2:]
    for bit in bits:
        pieces += [(at ^ bit, first, swap(piece, "wide", bit)) for at, first, piece in pieces]
    jobs = [(quarter, [(None, 0, 0, rows)])]
    starts = [(narrow_at, jnp.int32(0))]
    for at, first, piece in pieces:
        targets = []
        for offset in range(1, parts):
            targets.append((offset - 1, len(starts), first, piece.shape[1]))
            starts.append((narrow_at ^ offset, wide_at ^ at))
        jobs.append((piece, targets))
    table = jnp.stack([jnp.stack(pair) for pair in starts]).astype(jnp.int32)
    return place(table, jobs, (parts, blocks, rows, lanes))


def scatter_sums(whole):
    parts, blocks, rows, lanes = whole.shape
    wide_at, narrow_at = lax.axis_index("wide"), lax.axis_index("narrow")

    def block(at):
        return lax.dynamic_index_in_dim(whole, wide_at ^ at, 1, keepdims=False)

    even = jnp.stack([block(at) for at in range(0, blocks, 2)])
    odd = jnp.stack([block(at) for at in range(1, blocks, 2)])
    held = rounded_sum(even, swap(odd, "wide", 1))
    bits = bits_of(blocks)[1:]
    if len(bits) == 2 and rows % 32 == 0:
        a, b = bits
        half = rows // 2
        far = held[3]
        from_a = swap(far[:, :half], "wide", a)
        from_b = swap(far[:, half:], "wide", b)
        send_b = jnp.concatenate([rounded_sum(held[2][:, :half], from_a), held[2][:, half:]], axis=1)
        send_a = jnp.concatenate([held[1][:, :half], rounded_sum(held[1][:, half:], from_b)], axis=1)
        total = rounded_sum(held[0], swap(send_a, "wide", a), swap(send_b, "wide", b))
    else:
        for bit in bits[::-1]:
            half = held.shape[0] // 2
            held = rounded_sum(held[:half], swap(held[half:], "wide", bit))
        total = held[0]

    def part(offset):
        return lax.dynamic_index_in_dim(total, narrow_at ^ offset, 0, keepdims=False)

    result = part(0).astype(F32)
    for offset in range(1, parts):
        result = result + swap(part(offset), "narrow", offset).astype(F32)
    return result


def spread_rows(mine):
    parts = lax.axis_size("narrow")
    narrow_at = lax.axis_index("narrow")
    whole = jnp.zeros((parts,) + mine.shape, mine.dtype)
    for offset in range(parts):
        piece = mine if offset == 0 else swap(mine, "narrow", offset)
        whole = lax.dynamic_update_index_in_dim(whole, piece, narrow_at ^ offset, 0)
    return whole.reshape((-1,) + mine.shape[1:])


def bucket_both(length):
    places = jnp.arange(length, dtype=jnp.int32)
    offset = places[None, :] - places[:, None]
    spread = jnp.abs(offset)
    far_bucket = 8 + sum(((spread >= border).astype(jnp.int32) for border in BOTH_EDGES))
    near = jnp.where(spread < 8, spread, far_bucket)
    return jnp.where(offset > 0, 16, 0) + near


def causal_bucket_ids(length):
    places = jnp.arange(length, dtype=jnp.int32)
    spread = jnp.maximum(places[:, None] - places[None, :], 0)
    far_bucket = 16 + sum(((spread >= border).astype(jnp.int32) for border in CAUSAL_EDGES))
    return jnp.where(spread < 16, spread, far_bucket)


def bucket_lookup(buckets, bucket_count):
    return (jnp.arange(bucket_count, dtype=jnp.int32)[:, None, None] == buckets[None]).astype(F32)


def smooth_gate(values):
    return jax.nn.gelu(values, approximate=True)


def smooth_gate_back(grown, upstream):
    _, pullback = jax.vjp(smooth_gate, grown)
    return pullback(upstream)[0]


def norm_rows(values, gain_row):
    inv_rms = lax.rsqrt(jnp.mean(values * values, axis=-1, keepdims=True) + EPSILON)
    return (values * inv_rms * gain_row, inv_rms)


def norm_back(gradient_normalized, values, inv_rms, gain_row):
    scaled = gradient_normalized * gain_row
    inv_cubed = inv_rms * inv_rms * inv_rms
    grad_values = inv_rms * scaled - values * inv_cubed * jnp.mean(
        scaled * values, axis=-1, keepdims=True
    )
    return (grad_values, gradient_normalized * values * inv_rms)


def dot(spec, left, right):
    return jnp.einsum(spec, left, right, preferred_element_type=F32)


def softmax_forward(queries, keys, values, bias, allowed):
    scores = dot("rqhe,rkhe->rhqk", queries, keys) + bias[None]
    masked = jnp.where(allowed, scores, MASKED)
    highest = jnp.max(masked, axis=-1, keepdims=True)
    exponent = jnp.exp(masked - highest)
    totals = jnp.sum(exponent, axis=-1, keepdims=True)
    weights = (exponent / totals).astype(BF16)
    context = dot("rhqk,rkhe->rqhe", weights, values).astype(BF16)
    return context, highest + jnp.log(totals)


def softmax_backward(queries, keys, values, bias, allowed, logsum, grad_context):
    scores = dot("rqhe,rkhe->rhqk", queries, keys) + bias[None]
    probs = jnp.exp(jnp.where(allowed, scores, MASKED) - logsum)
    grad_probs = dot("rqhe,rkhe->rhqk", grad_context, values)
    grad_values = dot("rhqk,rqhe->rkhe", probs.astype(BF16), grad_context)
    dot_term = jnp.sum(grad_probs * probs, axis=-1, keepdims=True)
    grad_scores = (probs * (grad_probs - dot_term)).astype(BF16)
    grad_queries = dot("rhqk,rkhe->rqhe", grad_scores, keys)
    grad_keys = dot("rhqk,rqhe->rkhe", grad_scores, queries)
    return [g.astype(BF16) for g in (grad_queries, grad_keys, grad_values)], jnp.sum(
        grad_scores.astype(F32), axis=0
    )


def merge_stats(first, second):
    first_max, first_total, first_sums = first
    second_max, second_total, second_sums = second
    ahead = first_max >= second_max
    high = jnp.where(ahead, first_max, second_max)
    scale = jnp.exp(jnp.where(ahead, second_max, first_max) - high)
    total = jnp.where(ahead, first_total, second_total) + scale * jnp.where(
        ahead, second_total, first_total
    )
    sums = jnp.where(ahead[..., None], first_sums, second_sums) + scale[..., None] * jnp.where(
        ahead[..., None], second_sums, first_sums
    )
    return high, total, sums


def per_device(
    tokens,
    segments,
    question,
    answer_ids,
    vocab_table,
    enc_gains,
    enc_inward,
    encoder_bias,
    enc_outward,
    enc_grow,
    enc_shrink,
    cross_key_value_weight,
    dec_gains,
    dec_inward,
    decoder_bias,
    dec_outward,
    cross_query,
    cross_outward,
    dec_grow,
    dec_shrink,
    grad_memory,
    grad_output,
):
    parts, blocks = lax.axis_size("narrow"), lax.axis_size("wide")
    wide_at, narrow_at = lax.axis_index("wide"), lax.axis_index("narrow")
    row_length = segments.shape[1]
    rows_here = segments.shape[0] // parts
    count = rows_here * row_length
    width = tokens.shape[1]
    slab = width // blocks
    inner_local = cross_query.shape[1]
    head_local = inner_local // HD
    heads = head_local * parts
    hidden_local = enc_grow.shape[1]
    questions, answers = answer_ids.shape
    dec_count = questions * answers

    def own_rows(array, size):
        return lax.dynamic_slice_in_dim(array, narrow_at * size, size, 0)

    tokens_here = own_rows(tokens, count).astype(F32)
    grad_memory_here = own_rows(grad_memory, count).astype(F32)
    segments_here = own_rows(segments, rows_here)
    question_here = own_rows(question, rows_here)

    def slabs(*matrices):
        return jnp.concatenate([m.reshape(width, -1) for m in matrices], axis=1).reshape(blocks, slab, -1)

    def joined(whole):
        return whole.reshape(parts, width, -1)

    attn_all = joined(gather_weights(slabs(enc_inward, enc_outward.T)))
    ffn_all = joined(
        gather_weights(
            jnp.concatenate(
                [
                    enc_grow.reshape(blocks, slab, hidden_local),
                    enc_shrink.reshape(blocks, -1, width),
                ],
                axis=-1,
            )
            if hidden_local == width
            else slabs(enc_grow, enc_shrink.T)
        )
    )
    cross_all = joined(gather_weights(slabs(cross_key_value_weight, cross_outward.T)))
    in_all, out_all = attn_all[:, :, : 3 * inner_local], attn_all[:, :, 3 * inner_local :]
    grow_all = ffn_all[:, :, :hidden_local]
    shrink_all = ffn_all[:, :, hidden_local:]
    kv_all, cross_out_all = cross_all[:, :, : 2 * inner_local], cross_all[:, :, 2 * inner_local :]

    table_all = spread_rows(encoder_bias.T)
    indicator = bucket_lookup(bucket_both(row_length), encoder_bias.shape[0])
    bias_all = jnp.einsum("uxe,cu->cxe", indicator, table_all, precision=FULL)
    allowed = (segments_here[:, :, None] == segments_here[:, None, :])[:, None]
    first_values, first_inv = norm_rows(tokens_here, enc_gains[0])
    first_normed = first_values.astype(BF16)

    def heads_of(projected, kinds):
        split = projected.reshape(rows_here, row_length, parts, kinds, head_local, HD)
        return [split[:, :, :, kind].reshape(rows_here, row_length, heads, HD) for kind in range(kinds)]

    projected = dot("td,zdf->tzf", first_normed, in_all).astype(BF16)
    queries, keys, values = heads_of(projected, 3)
    context, logsum = softmax_forward(queries, keys, values, bias_all, allowed)
    context_flat = context.reshape(count, parts, inner_local)
    hidden = tokens_here + dot("tzi,zdi->td", context_flat, out_all)
    second_values, second_inv = norm_rows(hidden, enc_gains[1])
    second_normed = second_values.astype(BF16)
    enc_grown = dot("td,zdf->tzf", second_normed, grow_all)
    enc_act = smooth_gate(enc_grown).astype(BF16)
    enc_summed = hidden + dot("tzf,zfd->td", enc_act, shrink_all)
    final_values, final_inv = norm_rows(enc_summed, enc_gains[2])
    memory = final_values.astype(BF16)
    kv = dot("td,zdf->tzf", memory, kv_all).astype(BF16)
    kv_split = kv.reshape(count, parts, 2, head_local, HD)
    cross_keys = kv_split[:, :, 0].reshape(count, heads, HD)
    cross_values = kv_split[:, :, 1].reshape(count, heads, HD)

    vocab_local = vocab_table.shape[0]
    vocab_ids = wide_at * vocab_local + jnp.arange(vocab_local, dtype=jnp.int32)
    one_hot = (answer_ids.reshape(-1)[:, None] == vocab_ids[None, :]).astype(BF16)
    embedded = exchange_sum(dot("qv,vd->qd", one_hot, vocab_table), "wide")
    dec_indicator = bucket_lookup(causal_bucket_ids(answers), decoder_bias.shape[0])
    dec_bias = jnp.einsum("uxe,uc->cxe", dec_indicator, decoder_bias, precision=FULL)
    places = jnp.arange(answers, dtype=jnp.int32)
    dec_allowed = (places[:, None] >= places[None, :])[None, None]
    zero_values, zero_inv = norm_rows(embedded, dec_gains[0])
    dec_normed = zero_values.astype(BF16)
    dec_projected = dot("td,dpf->ptf", dec_normed, dec_inward).astype(BF16)
    dec_queries, dec_keys, dec_values = [
        dec_projected[kind].reshape(questions, answers, head_local, HD) for kind in range(3)
    ]
    dec_context, dec_logsum = softmax_forward(dec_queries, dec_keys, dec_values, dec_bias, dec_allowed)
    dec_context = dec_context.reshape(dec_count, inner_local)
    dec_first = embedded + exchange_sum(dot("ti,id->td", dec_context, dec_outward), "narrow")
    cross_values_f, cross_inv = norm_rows(dec_first, dec_gains[1])
    cross_normed = cross_values_f.astype(BF16)
    cross_queries = dot("td,di->ti", cross_normed, cross_query).astype(BF16)
    queries_all = spread_rows(cross_queries[None])
    query_heads = queries_all.reshape(parts, dec_count, head_local, HD).transpose(1, 0, 2, 3)
    query_heads = query_heads.reshape(dec_count, heads, HD)

    token_question = jnp.repeat(question_here, row_length)
    dec_question = jnp.arange(dec_count, dtype=jnp.int32) // answers
    cross_allowed = (dec_question[:, None] == token_question[None, :])[None]
    cross_scores = dot("qhe,the->hqt", query_heads, cross_keys)
    cross_masked = jnp.where(cross_allowed, cross_scores, MASKED)
    local_max = jnp.max(cross_masked, axis=-1)
    exponent = jnp.where(cross_allowed, jnp.exp(cross_masked - local_max[:, :, None]), 0.0)
    high = exponent.astype(BF16)
    low = (exponent - high.astype(F32)).astype(BF16)
    local_sums = dot("hqt,the->hqe", high, cross_values) + dot("hqt,the->hqe", low, cross_values)
    stats = (local_max, jnp.sum(exponent, axis=-1), local_sums)
    for axis in ("wide", "narrow"):
        for bit in bits_of(lax.axis_size(axis)):
            stats = merge_stats(stats, swap(stats, axis, bit))
    whole_max, whole_total, whole_sums = stats
    cross_logsum = whole_max + jnp.log(whole_total)
    cross_exact = (whole_sums / whole_total[:, :, None]).transpose(1, 0, 2)
    cross_context = cross_exact.reshape(dec_count, -1).astype(BF16)
    cross_probs = jnp.where(cross_allowed, jnp.exp(cross_masked - cross_logsum[:, :, None]), 0.0)
    cross_weights = cross_probs.astype(BF16)

    dec_second = dec_first + dot("tzi,zdi->td", cross_context.reshape(dec_count, parts, -1), cross_out_all)
    third_values, third_inv = norm_rows(dec_second, dec_gains[2])
    third_normed = third_values.astype(BF16)
    dec_grown = dot("td,df->tf", third_normed, dec_grow)
    dec_act = smooth_gate(dec_grown).astype(BF16)
    grad_out = grad_output.astype(F32)
    grad_dec_grown = smooth_gate_back(dec_grown, dot("nd,fd->nf", grad_output, dec_shrink)).astype(BF16)
    third_part, output_part = exchange_sum(
        (dot("nf,df->nd", grad_dec_grown, dec_grow), dot("tf,fd->td", dec_act, dec_shrink)), "narrow"
    )
    output = (dec_second + output_part).astype(BF16)
    grad_dec_shrink = dot("nf,nd->fd", dec_act, grad_output)
    grad_dec_grow = dot("nd,nf->df", third_normed, grad_dec_grown)
    grad_third, third_gain = norm_back(third_part, dec_second, third_inv, dec_gains[2])
    grad_dec_second = grad_out + grad_third
    grad_cbranch = grad_dec_second.astype(BF16)
    grad_cross_context = dot("td,zdi->tzi", grad_cbranch, cross_out_all).astype(BF16)
    grad_cheads = grad_cross_context.reshape(dec_count, heads, HD)
    context_local = lax.dynamic_slice_in_dim(cross_context, narrow_at * inner_local, inner_local, 1)
    grad_cross_outward = dot("qi,qd->id", context_local, grad_cbranch)
    cross_delta = jnp.einsum("qhe,qhe->hq", grad_cheads.astype(F32), cross_exact, precision=FULL)
    grad_cprobs = dot("qhe,the->hqt", grad_cheads, cross_values)
    grad_cross_scores = (cross_probs * (grad_cprobs - cross_delta[:, :, None])).astype(BF16)
    grad_kv_values = dot("hqt,qhe->the", cross_weights, grad_cheads)
    grad_kv_keys = dot("hqt,qhe->the", grad_cross_scores, query_heads)
    query_part = dot("hqt,the->qhe", grad_cross_scores, cross_keys).reshape(dec_count, -1)
    grad_kv = jnp.stack(
        [g.reshape(count, parts, inner_local) for g in (grad_kv_keys, grad_kv_values)], axis=2
    ).astype(BF16)
    grad_kv = grad_kv.reshape(count, parts, 2 * inner_local)

    def scattered(whole):
        return scatter_sums(whole.astype(BF16).reshape(parts, blocks, slab, -1))

    memory_part = dot("tzf,zdf->td", grad_kv, kv_all)
    sent_cross = scattered(dot("td,tzf->zdf", memory, grad_kv))
    grad_final = memory_part + grad_memory_here
    grad_enc_summed, final_gain = norm_back(grad_final, enc_summed, final_inv, enc_gains[2])
    grad_branch_ffn = grad_enc_summed.astype(BF16)
    grad_enc_act = dot("td,zfd->tzf", grad_branch_ffn, shrink_all)
    grad_enc_grown = smooth_gate_back(enc_grown, grad_enc_act).astype(BF16)
    sent_ffn = scattered(
        jnp.concatenate(
            [
                dot("td,tzf->zdf", second_normed, grad_enc_grown),
                dot("td,tzf->zdf", grad_branch_ffn, enc_act),
            ],
            axis=-1,
        )
    )
    second_part = dot("tzf,zdf->td", grad_enc_grown, grow_all)
    grad_second_norm, second_gain = norm_back(second_part, hidden, second_inv, enc_gains[1])
    grad_enc_hidden = grad_enc_summed + grad_second_norm
    grad_branch_attn = grad_enc_hidden.astype(BF16)
    grad_context = dot("td,zdi->tzi", grad_branch_attn, out_all).astype(BF16)
    grad_heads = grad_context.reshape(rows_here, row_length, heads, HD)
    grad_qkv, bias_rows = softmax_backward(
        queries, keys, values, bias_all, allowed, logsum, grad_heads
    )
    grad_projected = jnp.stack([g.reshape(count, parts, inner_local) for g in grad_qkv], axis=2)
    grad_projected = grad_projected.reshape(count, parts, 3 * inner_local)
    sent_attn = scattered(
        jnp.concatenate(
            [
                dot("td,tzf->zdf", first_normed, grad_projected),
                dot("td,tzf->zdf", grad_branch_attn, context_flat),
            ],
            axis=-1,
        )
    )
    first_part = dot("tzf,zdf->td", grad_projected, in_all)
    grad_first_norm, first_gain = norm_back(first_part, tokens_here, first_inv, enc_gains[0])
    grad_tokens = spread_rows((grad_enc_hidden + grad_first_norm).astype(BF16))
    memory_out = spread_rows(memory)

    enc_gain_terms = jnp.stack([jnp.sum(g, axis=0) for g in (first_gain, second_gain, final_gain)])
    enc_bias_local = jnp.einsum("jia,xia->xj", bias_rows, indicator, precision=FULL)
    enc_gain_sums, enc_bias_sums = exchange_sum(
        exchange_sum((enc_gain_terms, enc_bias_local), "wide"), "narrow"
    )
    grad_enc_bias = lax.dynamic_slice_in_dim(enc_bias_sums, narrow_at * head_local, head_local, 1)

    grad_cross_queries_all = exchange_sum(exchange_sum(query_part, "wide"), "narrow").astype(BF16)
    grad_cross_queries = lax.dynamic_slice_in_dim(
        grad_cross_queries_all, narrow_at * inner_local, inner_local, 1
    )
    grad_cross_query = dot("qd,qi->di", cross_normed, grad_cross_queries)
    cross_part = exchange_sum(dot("qi,di->qd", grad_cross_queries, cross_query), "narrow")
    grad_cross_norm, cross_gain = norm_back(cross_part, dec_first, cross_inv, dec_gains[1])
    grad_dec_first = grad_dec_second + grad_cross_norm
    grad_sbranch = grad_dec_first.astype(BF16)
    grad_dec_outward = dot("ti,td->id", dec_context, grad_sbranch)
    grad_dec_heads = dot("td,id->ti", grad_sbranch, dec_outward).astype(BF16)
    grad_dec_qkv, dec_bias_rows = softmax_backward(
        dec_queries,
        dec_keys,
        dec_values,
        dec_bias,
        dec_allowed,
        dec_logsum,
        grad_dec_heads.reshape(questions, answers, head_local, HD),
    )
    grad_dec_projected = jnp.stack([g.reshape(dec_count, inner_local) for g in grad_dec_qkv])
    grad_dec_inward = dot("td,ptf->dpf", dec_normed, grad_dec_projected)
    zero_part = exchange_sum(dot("ptf,dpf->td", grad_dec_projected, dec_inward), "narrow")
    grad_zero, zero_gain = norm_back(zero_part, embedded, zero_inv, dec_gains[0])
    grad_embedded = grad_dec_first + grad_zero
    grad_vocab_table = jnp.einsum("qv,qd->vd", one_hot.astype(F32), grad_embedded, precision=FULL)
    gradient_decoder_bias = jnp.einsum("jia,xia->xj", dec_bias_rows, dec_indicator, precision=FULL)
    grad_dec_gains = jnp.stack([jnp.sum(g, axis=0) for g in (zero_gain, cross_gain, third_gain)])

    sent_inward = sent_attn[:, : 3 * inner_local].reshape(slab, 3, inner_local)
    sent_outward = sent_attn[:, 3 * inner_local :].T
    sent_grow = sent_ffn[:, :hidden_local]
    sent_shrink = sent_ffn[:, hidden_local:].T
    return (
        memory_out,
        output,
        grad_tokens,
        grad_vocab_table,
        enc_gain_sums,
        sent_inward,
        grad_enc_bias,
        sent_outward,
        sent_grow,
        sent_shrink,
        sent_cross.reshape(slab, 2, inner_local),
        grad_dec_gains,
        grad_dec_inward,
        gradient_decoder_bias,
        grad_dec_outward,
        grad_cross_query,
        grad_cross_outward,
        grad_dec_grow,
        grad_dec_shrink,
    )


def solution(mesh):
    in_specs = (
        P("wide", None),
        P("wide", None),
        P("wide"),
        P(),
        P("wide", None),
        P(),
        P(None, None, "narrow"),
        P(None, "narrow"),
        P("narrow", None),
        P(None, "narrow"),
        P("narrow", None),
        P(None, None, "narrow"),
        P(),
        P(None, None, "narrow"),
        P(None, "narrow"),
        P("narrow", None),
        P(None, "narrow"),
        P("narrow", None),
        P(None, "narrow"),
        P("narrow", None),
        P("wide", None),
        P(),
    )
    out_specs = (
        P("wide", None),
        P(),
        P("wide", None),
        P("wide", None),
        P(),
        P("wide", None, "narrow"),
        P(None, "narrow"),
        P("narrow", "wide"),
        P("wide", "narrow"),
        P("narrow", "wide"),
        P("wide", None, "narrow"),
        P(),
        P(None, None, "narrow"),
        P(None, "narrow"),
        P("narrow", None),
        P(None, "narrow"),
        P("narrow", None),
        P(None, "narrow"),
        P("narrow", None),
    )
    return jax.shard_map(
        per_device, mesh=mesh, in_specs=in_specs, out_specs=out_specs, check_vma=False
    )
```

time: 1100 us -> 1150 us (1.045)
  Pallas kernels: 0 us -> 555 us
  waiting for transfers between devices: 740 us -> 197 us
  starting transfers between devices: 1.12 us -> 120 us
  blocking collectives: 107 us -> 0 us
  local copies, waits for them, and re-layouts: 53.4 us -> 93.5 us
  other arithmetic: 58.5 us -> 79.8 us
  matrix products: 114 us -> 94.8 us
    psum x8 -> x0, waiting for transfers between devices: 659 us -> none  [the longest x4 456 us: to_rows(): return lax.psum(partial_value, 'narrow')]
    pallas_call x0 -> x3, Pallas kernels: none -> 555 us  [place(): pl.pallas_call(kernel, out_shape=jax.ShapeDtypeStruct(shape, arrays[0].dt...]
    ppermute x0 -> x115, waiting for transfers between devices: none -> 197 us  [swap(): return jax.tree.map(lambda part: lax.ppermute(part, axis, pairs), value)]
    ppermute x0 -> x115, starting transfers between devices: none -> 120 us  [swap(): return jax.tree.map(lambda part: lax.ppermute(part, axis, pairs), value)]
    psum x3 -> x0, blocking collectives: 89.3 us -> none  [the longest x1 39.7 us: per_device(): lax.psum((enc_gain_terms, bias_padded), ('wide', 'narrow'))]
    reduce_scatter x4 -> x0, waiting for transfers between devices: 80.9 us -> none  [the longest x1 46.8 us: per_device(): lax.psum_scatter(grad_enc_inward, 'wide', scatter_dimension=0, tiled=True)]
    another operation x2 -> x27, other arithmetic: 0.63 us -> 24.1 us  [the longest x13 8.32 us: gather_weights(): table = jnp.stack([jnp.stack(pair) for pair in starts]).astype(jnp.int32)]
    all_gather x2 -> x0, blocking collectives: 17.9 us -> none  [merged(): pieces = jax.tree.map(lambda part: lax.all_gather(part, axis), value)]
  transfers between devices with their start and end apart: 13 -> 115, of which waited for: 10 -> 38; matrix products, arithmetic and copies ran while one was open for 14% -> 18% of each run, Pallas kernels for 0% -> 23%
where the time goes in v1:
time: 1150 us; the launch traced here: 1140 us
  Pallas kernels  555 us (48%)
  waiting for transfers between devices  197 us (17%)
  starting transfers between devices  120 us (10%)
  matrix products  94.8 us (8%)
  local copies, waits for them, and re-layouts  93.5 us (8%)
  other arithmetic  79.8 us (7%)
    pallas_call x3, Pallas kernels, place(): pl.pallas_call(kernel, out_shape=jax.ShapeDtypeStruct(shape, arrays[0].dt...  555 us
    ppermute x115, waiting for transfers between devices, swap(): return jax.tree.map(lambda part: lax.ppermute(part, axis, pairs), value)  197 us
    ppermute x115, starting transfers between devices, swap(): return jax.tree.map(lambda part: lax.ppermute(part, axis, pairs), value)  120 us
    dot_general x52, matrix products, dot(): return jnp.einsum(spec, left, right, preferred_element_type=F32)  77.7 us
  transfers between devices with their start and end apart: 115, of which 38 were waited for; matrix products, arithmetic and copies ran while one was open for 18% of the time, Pallas kernels for 23%

profile of v1, /device:TPU:0, one launch (start us, length us, event | category | flops | bytes accessed | tf_op | source)
XLA Modules:
  0.0 1143.8 jit_solution(16255414805947313119)
XLA Ops:
  0.7 3.1 collective-permute-start.12
  7.1 3.8 fusion.108
  16.3 3.8 collective-permute-start.40
  28.1 2.9 pad_maximum_fusion.1.refs_0_
  42.2 3.4 iota_compare_fusion
  56.9 13.1 %copy.280 = pred[32,256,256]{2,0,1:T(32,128)(4,1)} copy(pred[32,256,256]{1,0,2:T(32,128)(4,1)} %iota_compare_fusion) | data formatting | bytes 4194304 | tf_op jit(solution)/shard_map/eq | solution.py:162
  86.2 3.5 collective-permute-start.2
  108.4 4.3 fusion.289
  112.7 5.4 copy.281
  127.3 21.1 %collective-permute-done.34 = f32[40,768]{1,0:T(8,128)S(1)} collective-permute-done((f32[40,768]{1,0:T(8,128)S(1)}, f32[40,768]{1,0:T(8,128)S(1)}, u32[]{:S(2)}, u32[]{:S(2)}) %collective-permute-start.34) | collective-permute-done | bytes 122912 | tf_op jit(solution)/shard_map/ppermute | solution.py:25
  153.6 7.9 collective-permute-done.3.refs_2_
  168.4 2.9 collective-permute-start.37
  176.6 5.3 collective-permute-done.5.refs_4_
  183.4 121.5 %shard_map.359 = bf16[4,8,96,576]{3,2,1,0:T(8,128)(2,1)} custom-call(s32[31,2]{1,0:T(8,128)} %stack.295.starts_ref, bf16[8,96,576]{2,1,0:T(8,128)(2,1)} %pad_maximum_fusion.8.refs_0_, bf16[3,96,576]{2,1,0:T(8,128)(2,1)} %pad_maximum_fusion.14.refs_1_, bf16[3,96,576]{2,1,0:T(8,128)(2,1)} %collective-permute-done.41.refs_2_, ...), custom_call_target="tpu_custom_call" | custom-call | tf_op jit(solution)/shard_map/pallas_call | solution.py:57
  306.3 145.3 %shard_map.357 = bf16[4,8,96,768]{3,2,1,0:T(8,128)(2,1)} custom-call(s32[31,2]{1,0:T(8,128)} %stack.295.starts_ref, bf16[8,96,768]{2,1,0:T(8,128)(2,1)} %pad_maximum_fusion.3.refs_0_, bf16[3,96,768]{2,1,0:T(8,128)(2,1)} %copy-done.49, bf16[3,96,768]{2,1,0:T(8,128)(2,1)} %collective-permute-done.3.refs_2_, ...), custom_call_target="tpu_custom_call" | custom-call | tf_op jit(solution)/shard_map/pallas_call | solution.py:57
  451.6 3.9 fusion.35
  465.5 7.5 collective-permute-done.20.refs_4_
  475.1 2.9 multiply_reduce_fusion.6
  479.4 288.2 %shard_map.358 = bf16[4,8,96,1536]{3,2,1,0:T(8,128)(2,1)} custom-call(s32[31,2]{1,0:T(8,128)} %stack.295.starts_ref, bf16[8,96,1536]{2,1,0:T(8,128)(2,1)} %pad_maximum_fusion.1.refs_0_, bf16[3,96,1536]{2,1,0:T(8,128)(2,1)} %copy-done.34, bf16[3,96,1536]{2,1,0:T(8,128)(2,1)} %collective-permute-done.18.refs_2_, ...), custom_call_target="tpu_custom_call" | custom-call | tf_op jit(solution)/shard_map/pallas_call | solution.py:57
  767.6 3.8 fusion.6
  771.4 5.5 multiply_reduce_fusion.5
  804.0 12.2 %collective-permute-done.63 = f32[12,40]{1,0:T(8,128)S(1)} collective-permute-done((f32[12,40]{1,0:T(8,128)S(1)}, f32[12,40]{1,0:T(8,128)S(1)}, u32[]{:S(2)}, u32[]{:S(2)}) %collective-permute-start.63) | collective-permute-done | bytes 1952 | tf_op jit(solution)/shard_map/ppermute | solution.py:25
  816.3 3.2 collective-permute-start.54
  821.0 7.0 collective-permute-done.54
  829.5 4.8 collective-permute-done.56
  836.2 4.5 collective-permute-done.57
  841.2 7.4 collective-permute-done.58
  849.9 8.0 collective-permute-done.59
  865.8 3.8 collective-permute-done.67
  887.3 5.2 fusion.18
  909.0 2.9 convert_bitcast_fusion
  913.8 3.8 convolution_convert_fusion
  917.7 3.7 convolution_convert_fusion.1
  925.9 6.0 copy.323
  972.7 15.0 %collective-permute-done.85 = f32[3,768]{1,0:T(4,128)S(1)} collective-permute-done((f32[3,768]{1,0:T(4,128)S(1)}, f32[3,768]{1,0:T(4,128)S(1)}, u32[]{:S(2)}, u32[]{:S(2)}) %collective-permute-start.85) | collective-permute-done | bytes 9248 | tf_op jit(solution)/shard_map/ppermute | solution.py:25
  990.0 4.1 collective-permute-done.75
  996.0 7.3 collective-permute-done.76
  1003.7 5.2 collective-permute-done.77
  1010.8 6.2 collective-permute-done.78
  1034.0 4.6 collective-permute-done.108
  1052.4 3.3 add_convert_fusion
  1063.1 11.2 collective-permute-done.102
  1076.7 11.5 %collective-permute-done.100 = bf16[4,48,1536]{2,1,0:T(8,128)(2,1)S(1)} collective-permute-done((bf16[4,48,1536]{2,1,0:T(8,128)(2,1)S(1)}, bf16[4,48,1536]{2,1,0:T(8,128)(2,1)S(1)}, u32[]{:S(2)}, u32[]{:S(2)}) %collective-permute-start.100) | collective-permute-done | bytes 589856 | tf_op jit(solution)/shard_map/ppermute | solution.py:25
  1091.3 8.1 fusion.106
  1102.4 2.8 collective-permute-done.112
  1117.2 5.9 collective-permute-start.104
  1123.1 8.9 collective-permute-done.92
  1134.0 7.5 collective-permute-done.105
  (849 shorter events, 306.4 us)
Async XLA Ops:
  0.7 74.5 %collective-permute-start.12 = (f32[3,32]{1,0:T(4,128)}, f32[3,32]{1,0:T(4,128)}, u32[]{:S(2)}, u32[]{:S(2)}) collective-permute-start(f32[3,32]{1,0:T(4,128)} %bitcast.528), channel_id=1, source_target_pairs={{0,1},{1,0},{2,3},{3,2},{4,5},{5,4},{6,7},{7,6},{8,9},{9,8},{10,11... | collective-permute-start | bytes 1160 | tf_op jit(solution)/shard_map/ppermute | solution.py:25
  3.8 77.5 %collective-permute-start.13 = (f32[3,32]{1,0:T(4,128)}, f32[3,32]{1,0:T(4,128)}, u32[]{:S(2)}, u32[]{:S(2)}) collective-permute-start(f32[3,32]{1,0:T(4,128)} %bitcast.529), channel_id=1, source_target_pairs={{0,2},{1,3},{2,0},{3,1},{4,6},{5,7},{6,4},{7,5},{8,10},{9,11},{10,... | collective-permute-start | bytes 1160 | tf_op jit(solution)/shard_map/ppermute | solution.py:25
  6.4 91.0 %collective-permute-start.14 = (f32[3,32]{1,0:T(4,128)}, f32[3,32]{1,0:T(4,128)}, u32[]{:S(2)}, u32[]{:S(2)}) collective-permute-start(f32[3,32]{1,0:T(4,128)} %bitcast.530), channel_id=1, source_target_pairs={{0,3},{1,2},{2,1},{3,0},{4,7},{5,6},{6,5},{7,4},{8,11},{9,10},{10,... | collective-permute-start | bytes 1160 | tf_op jit(solution)/shard_map/ppermute | solution.py:25
  11.0 63.2 %collective-permute-start.30 = (f32[40,768]{1,0:T(8,128)S(1)}, f32[40,768]{1,0:T(8,128)}, u32[]{:S(2)}, u32[]{:S(2)}) collective-permute-start(f32[40,768]{1,0:T(8,128)S(1)} %fusion.108), channel_id=1, source_target_pairs={{0,4},{4,0},{8,12},{12,8},{16,20},{20,16},{24,28},{28,24},{1,5},{5... | collective-permute-start | bytes 368648 | tf_op jit(solution)/shard_map/ppermute | solution.py:25
  16.3 83.8 %collective-permute-start.40 = (bf16[96,576]{1,0:T(8,128)(2,1)}, bf16[96,576]{1,0:T(8,128)(2,1)}, u32[]{:S(2)}, u32[]{:S(2)}) collective-permute-start(bf16[96,576]{1,0:T(8,128)(2,1)} %fusion.205), channel_id=1, source_target_pairs={{0,3},{1,2},{2,1},{3,0},{4,7},{5,6},{6,5},{7,4},{8,11},{9,10},{10,... | collective-permute-start | bytes 331784 | tf_op jit(solution)/shard_map/ppermute | solution.py:25
  74.2 26.7 %collective-permute-start.39 = (bf16[96,576]{1,0:T(8,128)(2,1)}, bf16[96,576]{1,0:T(8,128)(2,1)}, u32[]{:S(2)}, u32[]{:S(2)}) collective-permute-start(bf16[96,576]{1,0:T(8,128)(2,1)} %fusion.205), channel_id=1, source_target_pairs={{0,2},{1,3},{2,0},{3,1},{4,6},{5,7},{6,4},{7,5},{8,10},{9,11},{10,... | collective-permute-start | bytes 331784 | tf_op jit(solution)/shard_map/ppermute | solution.py:25
  80.6 21.5 %collective-permute-start.38 = (bf16[96,576]{1,0:T(8,128)(2,1)}, bf16[96,576]{1,0:T(8,128)(2,1)}, u32[]{:S(2)}, u32[]{:S(2)}) collective-permute-start(bf16[96,576]{1,0:T(8,128)(2,1)} %fusion.205), channel_id=1, source_target_pairs={{0,1},{1,0},{2,3},{3,2},{4,5},{5,4},{6,7},{7,6},{8,9},{9,8},{10,11... | collective-permute-start | bytes 331784 | tf_op jit(solution)/shard_map/ppermute | solution.py:25
  86.2 32.9 %collective-permute-start.2 = (bf16[96,768]{1,0:T(8,128)(2,1)}, bf16[96,768]{1,0:T(8,128)(2,1)}, u32[]{:S(2)}, u32[]{:S(2)}) collective-permute-start(bf16[96,768]{1,0:T(8,128)(2,1)} %fusion.191), channel_id=1, source_target_pairs={{0,3},{1,2},{2,1},{3,0},{4,7},{5,6},{6,5},{7,4},{8,11},{9,10},{10,... | collective-permute-start | bytes 442376 | tf_op jit(solution)/shard_map/ppermute | solution.py:25
  100.0 20.0 %collective-permute-start.1 = (bf16[96,768]{1,0:T(8,128)(2,1)}, bf16[96,768]{1,0:T(8,128)(2,1)}, u32[]{:S(2)}, u32[]{:S(2)}) collective-permute-start(bf16[96,768]{1,0:T(8,128)(2,1)} %fusion.191), channel_id=1, source_target_pairs={{0,2},{1,3},{2,0},{3,1},{4,6},{5,7},{6,4},{7,5},{8,10},{9,11},{10,... | collective-permute-start | bytes 442376 | tf_op jit(solution)/shard_map/ppermute | solution.py:25
  100.9 19.8 %collective-permute-start = (bf16[96,768]{1,0:T(8,128)(2,1)}, bf16[96,768]{1,0:T(8,128)(2,1)}, u32[]{:S(2)}, u32[]{:S(2)}) collective-permute-start(bf16[96,768]{1,0:T(8,128)(2,1)} %fusion.191), channel_id=1, source_target_pairs={{0,1},{1,0},{2,3},{3,2},{4,5},{5,4},{6,7},{7,6},{8,9},{9,8},{10,11... | collective-permute-start | bytes 442376 | tf_op jit(solution)/shard_map/ppermute | solution.py:25
  103.9 22.3 %collective-permute-start.41 = (bf16[3,96,576]{2,1,0:T(8,128)(2,1)}, bf16[3,96,576]{2,1,0:T(8,128)(2,1)}, u32[]{:S(2)}, u32[]{:S(2)}) collective-permute-start(bf16[3,96,576]{2,1,0:T(8,128)(2,1)} %pad_maximum_fusion.14.refs_1_), channel_id=1, source_target_pairs={{0,16},{4,20},{8,24},{12,28},{16,0},{20,4},{24,8},{28,12},{1,17},{... | collective-permute-start | bytes 995336 | tf_op jit(solution)/shard_map/ppermute | solution.py:25
  119.1 29.9 %collective-permute-start.17 = (bf16[96,1536]{1,0:T(8,128)(2,1)S(1)}, bf16[96,1536]{1,0:T(8,128)(2,1)S(1)}, u32[]{:S(2)}, u32[]{:S(2)}) collective-permute-start(bf16[96,1536]{1,0:T(8,128)(2,1)S(1)} %copy-done.84), channel_id=1, source_target_pairs={{0,3},{1,2},{2,1},{3,0},{4,7},{5,6},{6,5},{7,4},{8,11},{9,10},{10,... | collective-permute-start | bytes 884744 | tf_op jit(solution)/shard_map/ppermute | solution.py:25
  120.1 30.1 %collective-permute-start.16 = (bf16[96,1536]{1,0:T(8,128)(2,1)S(1)}, bf16[96,1536]{1,0:T(8,128)(2,1)S(1)}, u32[]{:S(2)}, u32[]{:S(2)}) collective-permute-start(bf16[96,1536]{1,0:T(8,128)(2,1)S(1)} %copy-done.84), channel_id=1, source_target_pairs={{0,2},{1,3},{2,0},{3,1},{4,6},{5,7},{6,4},{7,5},{8,10},{9,11},{10,... | collective-permute-start | bytes 884744 | tf_op jit(solution)/shard_map/ppermute | solution.py:25
  120.7 27.7 %collective-permute-start.34 = (f32[40,768]{1,0:T(8,128)S(1)}, f32[40,768]{1,0:T(8,128)S(1)}, u32[]{:S(2)}, u32[]{:S(2)}) collective-permute-start(f32[40,768]{1,0:T(8,128)S(1)} %add.715), channel_id=1, source_target_pairs={{0,2},{1,3},{2,0},{3,1},{4,6},{5,7},{6,4},{7,5},{8,10},{9,11},{10,... | collective-permute-start | bytes 368648 | tf_op jit(solution)/shard_map/ppermute | solution.py:25
  124.1 27.9 %collective-permute-start.15 = (bf16[96,1536]{1,0:T(8,128)(2,1)S(1)}, bf16[96,1536]{1,0:T(8,128)(2,1)S(1)}, u32[]{:S(2)}, u32[]{:S(2)}) collective-permute-start(bf16[96,1536]{1,0:T(8,128)(2,1)S(1)} %copy-done.84), channel_id=1, source_target_pairs={{0,1},{1,0},{2,3},{3,2},{4,5},{5,4},{6,7},{7,6},{8,9},{9,8},{10,11... | collective-permute-start | bytes 884744 | tf_op jit(solution)/shard_map/ppermute | solution.py:25
  126.3 27.3 %collective-permute-start.45 = (bf16[3,96,576]{2,1,0:T(8,128)(2,1)}, bf16[3,96,576]{2,1,0:T(8,128)(2,1)S(1)}, u32[]{:S(2)}, u32[]{:S(2)}) collective-permute-start(bf16[3,96,576]{2,1,0:T(8,128)(2,1)} %pad_maximum_fusion.14.refs_1_), channel_id=1, source_target_pairs={{0,4},{4,0},{8,12},{12,8},{16,20},{20,16},{24,28},{28,24},{1,5},{5... | collective-permute-start | bytes 995336 | tf_op jit(solution)/shard_map/ppermute | solution.py:25
  153.6 20.4 %collective-permute-start.46 = (bf16[3,96,576]{2,1,0:T(8,128)(2,1)}, bf16[3,96,576]{2,1,0:T(8,128)(2,1)S(1)}, u32[]{:S(2)}, u32[]{:S(2)}) collective-permute-start(bf16[3,96,576]{2,1,0:T(8,128)(2,1)} %collective-permute-done.41.refs_2_), channel_id=1, source_target_pairs={{0,4},{4,0},{8,12},{12,8},{16,20},{20,16},{24,28},{28,24},{1,5},{5... | collective-permute-start | bytes 995336 | tf_op jit(solution)/shard_map/ppermute | solution.py:25
  174.0 130.9 %collective-permute-start.7 = (bf16[3,96,768]{2,1,0:T(8,128)(2,1)S(1)}, bf16[3,96,768]{2,1,0:T(8,128)(2,1)}, u32[]{:S(2)}, u32[]{:S(2)}) collective-permute-start(bf16[3,96,768]{2,1,0:T(8,128)(2,1)S(1)} %pad_maximum_fusion.13.refs_1_), channel_id=1, source_target_pairs={{0,4},{4,0},{8,12},{12,8},{16,20},{20,16},{24,28},{28,24},{1,5},{5... | collective-permute-start | bytes 1327112 | tf_op jit(solution)/shard_map/ppermute | solution.py:25
  176.1 129.6 %collective-permute-start.8 = (bf16[3,96,768]{2,1,0:T(8,128)(2,1)}, bf16[3,96,768]{2,1,0:T(8,128)(2,1)}, u32[]{:S(2)}, u32[]{:S(2)}) collective-permute-start(bf16[3,96,768]{2,1,0:T(8,128)(2,1)} %collective-permute-done.3.refs_2_), channel_id=1, source_target_pairs={{0,4},{4,0},{8,12},{12,8},{16,20},{20,16},{24,28},{28,24},{1,5},{5... | collective-permute-start | bytes 1327112 | tf_op jit(solution)/shard_map/ppermute | solution.py:25
  176.1 130.1 %collective-permute-start.9 = (bf16[3,96,768]{2,1,0:T(8,128)(2,1)}, bf16[3,96,768]{2,1,0:T(8,128)(2,1)}, u32[]{:S(2)}, u32[]{:S(2)}) collective-permute-start(bf16[3,96,768]{2,1,0:T(8,128)(2,1)} %collective-permute-done.4.refs_3_), channel_id=1, source_target_pairs={{0,4},{4,0},{8,12},{12,8},{16,20},{20,16},{24,28},{28,24},{1,5},{5... | collective-permute-start | bytes 1327112 | tf_op jit(solution)/shard_map/ppermute | solution.py:25
  181.9 124.4 %collective-permute-start.10 = (bf16[3,48,768]{2,1,0:T(8,128)(2,1)}, bf16[3,48,768]{2,1,0:T(8,128)(2,1)}, u32[]{:S(2)}, u32[]{:S(2)}) collective-permute-start(bf16[3,48,768]{2,1,0:T(8,128)(2,1)} %collective-permute-done.5.refs_4_), channel_id=1, source_target_pairs={{0,4},{4,0},{8,12},{12,8},{16,20},{20,16},{24,28},{28,24},{1,5},{5... | collective-permute-start | bytes 663560 | tf_op jit(solution)/shard_map/ppermute | solution.py:25
  183.2 123.1 %collective-permute-start.11 = (bf16[3,48,768]{2,1,0:T(8,128)(2,1)}, bf16[3,48,768]{2,1,0:T(8,128)(2,1)}, u32[]{:S(2)}, u32[]{:S(2)}) collective-permute-start(bf16[3,48,768]{2,1,0:T(8,128)(2,1)} %collective-permute-done.6.refs_5_), channel_id=1, source_target_pairs={{0,4},{4,0},{8,12},{12,8},{16,20},{20,16},{24,28},{28,24},{1,5},{5... | collective-permute-start | bytes 663560 | tf_op jit(solution)/shard_map/ppermute | solution.py:25
  304.9 156.8 %collective-permute-start.18 = (bf16[3,96,1536]{2,1,0:T(8,128)(2,1)S(1)}, bf16[3,96,1536]{2,1,0:T(8,128)(2,1)}, u32[]{:S(2)}, u32[]{:S(2)}) collective-permute-start(bf16[3,96,1536]{2,1,0:T(8,128)(2,1)S(1)} %pad_maximum_fusion.9.refs_1_), channel_id=1, source_target_pairs={{0,16},{4,20},{8,24},{12,28},{16,0},{20,4},{24,8},{28,12},{1,17},{... | collective-permute-start | bytes 2654216 | tf_op jit(solution)/shard_map/ppermute | solution.py:25
  305.7 153.2 %collective-permute-start.19 = (bf16[3,96,1536]{2,1,0:T(8,128)(2,1)S(1)}, bf16[3,96,1536]{2,1,0:T(8,128)(2,1)}, u32[]{:S(2)}, u32[]{:S(2)}) collective-permute-start(bf16[3,96,1536]{2,1,0:T(8,128)(2,1)S(1)} %pad_maximum_fusion.9.refs_1_), channel_id=1, source_target_pairs={{0,8},{4,12},{8,0},{12,4},{16,24},{20,28},{24,16},{28,20},{1,9},{5... | collective-permute-start | bytes 2654216 | tf_op jit(solution)/shard_map/ppermute | solution.py:25
  306.3 172.2 %collective-permute-start.22 = (bf16[3,96,1536]{2,1,0:T(8,128)(2,1)S(1)}, bf16[3,96,1536]{2,1,0:T(8,128)(2,1)}, u32[]{:S(2)}, u32[]{:S(2)}) collective-permute-start(bf16[3,96,1536]{2,1,0:T(8,128)(2,1)S(1)} %pad_maximum_fusion.9.refs_1_), channel_id=1, source_target_pairs={{0,4},{4,0},{8,12},{12,8},{16,20},{20,16},{24,28},{28,24},{1,5},{5... | collective-permute-start | bytes 2654216 | tf_op jit(solution)/shard_map/ppermute | solution.py:25
  790.4 50.7 %collective-permute-start.27 = (bf16[256,768]{1,0:T(8,128)(2,1)}, bf16[256,768]{1,0:T(8,128)(2,1)S(1)}, u32[]{:S(2)}, u32[]{:S(2)}) collective-permute-start(bf16[256,768]{1,0:T(8,128)(2,1)} %copy-done.58), channel_id=1, source_target_pairs={{0,1},{1,0},{2,3},{3,2},{4,5},{5,4},{6,7},{7,6},{8,9},{9,8},{10,11... | collective-permute-start | bytes 1179656 | tf_op jit(solution)/shard_map/ppermute | solution.py:25
  790.4 50.7 %collective-permute-start.28 = (bf16[256,768]{1,0:T(8,128)(2,1)}, bf16[256,768]{1,0:T(8,128)(2,1)S(1)}, u32[]{:S(2)}, u32[]{:S(2)}) collective-permute-start(bf16[256,768]{1,0:T(8,128)(2,1)} %copy-done.58), channel_id=1, source_target_pairs={{0,2},{1,3},{2,0},{3,1},{4,6},{5,7},{6,4},{7,5},{8,10},{9,11},{10,... | collective-permute-start | bytes 1179656 | tf_op jit(solution)/shard_map/ppermute | solution.py:25
  793.0 56.9 %collective-permute-start.29 = (bf16[256,768]{1,0:T(8,128)(2,1)}, bf16[256,768]{1,0:T(8,128)(2,1)S(1)}, u32[]{:S(2)}, u32[]{:S(2)}) collective-permute-start(bf16[256,768]{1,0:T(8,128)(2,1)} %copy-done.58), channel_id=1, source_target_pairs={{0,3},{1,2},{2,1},{3,0},{4,7},{5,6},{6,5},{7,4},{8,11},{9,10},{10,... | collective-permute-start | bytes 1179656 | tf_op jit(solution)/shard_map/ppermute | solution.py:25
  904.8 84.0 %collective-permute-start.69 = (bf16[256,768]{1,0:T(8,128)(2,1)}, bf16[256,768]{1,0:T(8,128)(2,1)}, u32[]{:S(2)}, u32[]{:S(2)}) collective-permute-start(bf16[256,768]{1,0:T(8,128)(2,1)} %get-tuple-element.116), channel_id=1, source_target_pairs={{0,1},{1,0},{2,3},{3,2},{4,5},{5,4},{6,7},{7,6},{8,9},{9,8},{10,11... | collective-permute-start | bytes 1179656 | tf_op jit(solution)/shard_map/ppermute | solution.py:25
  906.7 87.5 %collective-permute-start.70 = (bf16[256,768]{1,0:T(8,128)(2,1)}, bf16[256,768]{1,0:T(8,128)(2,1)}, u32[]{:S(2)}, u32[]{:S(2)}) collective-permute-start(bf16[256,768]{1,0:T(8,128)(2,1)} %get-tuple-element.116), channel_id=1, source_target_pairs={{0,2},{1,3},{2,0},{3,1},{4,6},{5,7},{6,4},{7,5},{8,10},{9,11},{10,... | collective-permute-start | bytes 1179656 | tf_op jit(solution)/shard_map/ppermute | solution.py:25
  924.6 35.5 %collective-permute-start.72 = (f32[40,768]{1,0:T(8,128)}, f32[40,768]{1,0:T(8,128)}, u32[]{:S(2)}, u32[]{:S(2)}) collective-permute-start(f32[40,768]{1,0:T(8,128)} %reshape.589), channel_id=1, source_target_pairs={{0,4},{4,0},{8,12},{12,8},{16,20},{20,16},{24,28},{28,24},{1,5},{5... | collective-permute-start | bytes 368648 | tf_op jit(solution)/shard_map/ppermute | solution.py:25
  924.7 23.6 %collective-permute-start.81 = (f32[3,768]{1,0:T(4,128)S(1)}, f32[3,768]{1,0:T(4,128)S(1)}, u32[]{:S(2)}, u32[]{:S(2)}) collective-permute-start(f32[3,768]{1,0:T(4,128)S(1)} %pad_maximum_fusion.17), channel_id=1, source_target_pairs={{0,4},{4,0},{8,12},{12,8},{16,20},{20,16},{24,28},{28,24},{1,5},{5... | collective-permute-start | bytes 27656 | tf_op jit(solution)/shard_map/ppermute | solution.py:25
  966.9 21.4 %collective-permute-start.74 = (f32[40,768]{1,0:T(8,128)S(1)}, f32[40,768]{1,0:T(8,128)S(1)}, u32[]{:S(2)}, u32[]{:S(2)}) collective-permute-start(f32[40,768]{1,0:T(8,128)S(1)} %add.746), channel_id=1, source_target_pairs={{0,16},{4,20},{8,24},{12,28},{16,0},{20,4},{24,8},{28,12},{1,17},{... | collective-permute-start | bytes 368648 | tf_op jit(solution)/shard_map/ppermute | solution.py:25
  969.9 33.8 %collective-permute-start.71 = (bf16[256,768]{1,0:T(8,128)(2,1)}, bf16[256,768]{1,0:T(8,128)(2,1)S(1)}, u32[]{:S(2)}, u32[]{:S(2)}) collective-permute-start(bf16[256,768]{1,0:T(8,128)(2,1)} %get-tuple-element.116), channel_id=1, source_target_pairs={{0,3},{1,2},{2,1},{3,0},{4,7},{5,6},{6,5},{7,4},{8,11},{9,10},{10,... | collective-permute-start | bytes 1179656 | tf_op jit(solution)/shard_map/ppermute | solution.py:25
  987.7 60.0 %collective-permute-start.86 = (bf16[4,4,96,768]{3,2,1,0:T(8,128)(2,1)}, bf16[4,4,96,768]{3,2,1,0:T(8,128)(2,1)}, u32[]{:S(2)}, u32[]{:S(2)}) collective-permute-start(bf16[4,4,96,768]{3,2,1,0:T(8,128)(2,1)} %pad_maximum_fusion.2), channel_id=1, source_target_pairs={{0,4},{4,0},{8,12},{12,8},{16,20},{20,16},{24,28},{28,24},{1,5},{5... | collective-permute-start | bytes 7077896 | tf_op jit(solution)/shard_map/ppermute | solution.py:25
  988.3 64.1 %collective-permute-start.99 = (bf16[4,4,96,1536]{3,2,1,0:T(8,128)(2,1)}, bf16[4,4,96,1536]{3,2,1,0:T(8,128)(2,1)}, u32[]{:S(2)}, u32[]{:S(2)}) collective-permute-start(bf16[4,4,96,1536]{3,2,1,0:T(8,128)(2,1)} %pad_maximum_fusion), channel_id=1, source_target_pairs={{0,4},{4,0},{8,12},{12,8},{16,20},{20,16},{24,28},{28,24},{1,5},{5... | collective-permute-start | bytes 14155784 | tf_op jit(solution)/shard_map/ppermute | solution.py:25
  994.1 30.6 %collective-permute-start.107 = (bf16[4,4,96,384]{3,2,1,0:T(8,128)(2,1)}, bf16[4,4,96,384]{3,2,1,0:T(8,128)(2,1)}, u32[]{:S(2)}, u32[]{:S(2)}) collective-permute-start(bf16[4,4,96,384]{3,2,1,0:T(8,128)(2,1)} %pad_maximum_fusion.7), channel_id=1, source_target_pairs={{0,4},{4,0},{8,12},{12,8},{16,20},{20,16},{24,28},{28,24},{1,5},{5... | collective-permute-start | bytes 3538952 | tf_op jit(solution)/shard_map/ppermute | solution.py:25
  1045.7 44.9 %collective-permute-start.114 = (bf16[96,384]{1,0:T(8,128)(2,1)S(1)}, bf16[96,384]{1,0:T(8,128)(2,1)S(1)}, u32[]{:S(2)}, u32[]{:S(2)}) collective-permute-start(bf16[96,384]{1,0:T(8,128)(2,1)S(1)} %get-tuple-element.197), channel_id=1, source_target_pairs={{0,3},{1,2},{2,1},{3,0},{4,7},{5,6},{6,5},{7,4},{8,11},{9,10},{10,... | collective-permute-start | bytes 221192 | tf_op jit(solution)/shard_map/ppermute | solution.py:25
  1047.7 51.7 %collective-permute-start.113 = (bf16[96,384]{1,0:T(8,128)(2,1)S(1)}, bf16[96,384]{1,0:T(8,128)(2,1)S(1)}, u32[]{:S(2)}, u32[]{:S(2)}) collective-permute-start(bf16[96,384]{1,0:T(8,128)(2,1)S(1)} %get-tuple-element.198), channel_id=1, source_target_pairs={{0,2},{1,3},{2,0},{3,1},{4,6},{5,7},{6,4},{7,5},{8,10},{9,11},{10,... | collective-permute-start | bytes 221192 | tf_op jit(solution)/shard_map/ppermute | solution.py:25
  1059.6 46.5 %collective-permute-start.90 = (bf16[4,96,768]{2,1,0:T(8,128)(2,1)}, bf16[4,96,768]{2,1,0:T(8,128)(2,1)}, u32[]{:S(2)}, u32[]{:S(2)}) collective-permute-start(bf16[4,96,768]{2,1,0:T(8,128)(2,1)} %pad_maximum_fusion.12), channel_id=1, source_target_pairs={{0,16},{4,20},{8,24},{12,28},{16,0},{20,4},{24,8},{28,12},{1,17},{... | collective-permute-start | bytes 1769480 | tf_op jit(solution)/shard_map/ppermute | solution.py:25
  1061.7 44.4 %collective-permute-start.88 = (bf16[4,96,768]{2,1,0:T(8,128)(2,1)}, bf16[4,96,768]{2,1,0:T(8,128)(2,1)}, u32[]{:S(2)}, u32[]{:S(2)}) collective-permute-start(bf16[4,96,768]{2,1,0:T(8,128)(2,1)} %pad_maximum_fusion.11), channel_id=1, source_target_pairs={{0,8},{4,12},{8,0},{12,4},{16,24},{20,28},{24,16},{28,20},{1,9},{5... | collective-permute-start | bytes 1769480 | tf_op jit(solution)/shard_map/ppermute | solution.py:25
  1088.2 23.8 %collective-permute-start.103 = (bf16[4,96,1536]{2,1,0:T(8,128)(2,1)}, bf16[4,96,1536]{2,1,0:T(8,128)(2,1)}, u32[]{:S(2)}, u32[]{:S(2)}) collective-permute-start(bf16[4,96,1536]{2,1,0:T(8,128)(2,1)} %pad_maximum_fusion.6), channel_id=1, source_target_pairs={{0,16},{4,20},{8,24},{12,28},{16,0},{20,4},{24,8},{28,12},{1,17},{... | collective-permute-start | bytes 3538952 | tf_op jit(solution)/shard_map/ppermute | solution.py:25
  1090.6 21.4 %collective-permute-start.101 = (bf16[4,96,1536]{2,1,0:T(8,128)(2,1)}, bf16[4,96,1536]{2,1,0:T(8,128)(2,1)}, u32[]{:S(2)}, u32[]{:S(2)}) collective-permute-start(bf16[4,96,1536]{2,1,0:T(8,128)(2,1)} %pad_maximum_fusion.5), channel_id=1, source_target_pairs={{0,8},{4,12},{8,0},{12,4},{16,24},{20,28},{24,16},{28,20},{1,9},{5... | collective-permute-start | bytes 3538952 | tf_op jit(solution)/shard_map/ppermute | solution.py:25
  1109.4 22.5 %collective-permute-start.92 = (bf16[96,768]{1,0:T(8,128)(2,1)S(1)}, bf16[96,768]{1,0:T(8,128)(2,1)S(1)}, u32[]{:S(2)}, u32[]{:S(2)}) collective-permute-start(bf16[96,768]{1,0:T(8,128)(2,1)S(1)} %get-tuple-element.193), channel_id=1, source_target_pairs={{0,2},{1,3},{2,0},{3,1},{4,6},{5,7},{6,4},{7,5},{8,10},{9,11},{10,... | collective-permute-start | bytes 442376 | tf_op jit(solution)/shard_map/ppermute | solution.py:25
  1110.1 21.9 %collective-permute-start.91 = (bf16[96,768]{1,0:T(8,128)(2,1)S(1)}, bf16[96,768]{1,0:T(8,128)(2,1)S(1)}, u32[]{:S(2)}, u32[]{:S(2)}) collective-permute-start(bf16[96,768]{1,0:T(8,128)(2,1)S(1)} %get-tuple-element.191), channel_id=1, source_target_pairs={{0,1},{1,0},{2,3},{3,2},{4,5},{5,4},{6,7},{7,6},{8,9},{9,8},{10,11... | collective-permute-start | bytes 442376 | tf_op jit(solution)/shard_map/ppermute | solution.py:25
  1115.4 18.6 %collective-permute-start.106 = (bf16[96,1536]{1,0:T(8,128)(2,1)}, bf16[96,1536]{1,0:T(8,128)(2,1)}, u32[]{:S(2)}, u32[]{:S(2)}) collective-permute-start(bf16[96,1536]{1,0:T(8,128)(2,1)} %get-tuple-element.180), channel_id=1, source_target_pairs={{0,3},{1,2},{2,1},{3,0},{4,7},{5,6},{6,5},{7,4},{8,11},{9,10},{10,... | collective-permute-start | bytes 884744 | tf_op jit(solution)/shard_map/ppermute | solution.py:25
  1117.2 24.3 %collective-permute-start.105 = (bf16[96,1536]{1,0:T(8,128)(2,1)}, bf16[96,1536]{1,0:T(8,128)(2,1)}, u32[]{:S(2)}, u32[]{:S(2)}) collective-permute-start(bf16[96,1536]{1,0:T(8,128)(2,1)} %get-tuple-element.181), channel_id=1, source_target_pairs={{0,2},{1,3},{2,0},{3,1},{4,6},{5,7},{6,4},{7,5},{8,10},{9,11},{10,... | collective-permute-start | bytes 884744 | tf_op jit(solution)/shard_map/ppermute | solution.py:25
  1117.2 24.3 %collective-permute-start.104 = (bf16[96,1536]{1,0:T(8,128)(2,1)S(1)}, bf16[96,1536]{1,0:T(8,128)(2,1)}, u32[]{:S(2)}, u32[]{:S(2)}) collective-permute-start(bf16[96,1536]{1,0:T(8,128)(2,1)S(1)} %get-tuple-element.179), channel_id=1, source_target_pairs={{0,1},{1,0},{2,3},{3,2},{4,5},{5,4},{6,7},{7,6},{8,9},{9,8},{10,11... | collective-permute-start | bytes 884744 | tf_op jit(solution)/shard_map/ppermute | solution.py:25
  (252 other events, 7240.4 us)

commit v2 on v1

v2 whole, which is shorter than its diff:
```python
import functools
import jax
import jax.numpy as jnp
import numpy as np
from jax import lax
from jax.experimental import pallas as pl
from jax.experimental.pallas import tpu as pltpu
from jax.sharding import PartitionSpec as P

HD = 64
SLABS = 8
EPSILON = 1e-06
BOTH_EDGES = (12, 16, 23, 32, 46, 64, 91)
CAUSAL_EDGES = (19, 21, 24, 27, 31, 35, 40, 46, 52, 59, 67, 77, 87, 99, 113)
FULL = lax.Precision.HIGHEST
F32 = jnp.float32
BF16 = jnp.bfloat16
I32 = jnp.int32
MASKED = -1e30
MIB = 1 << 20


def bits_of(count):
    return [1 << k for k in range(count.bit_length() - 1)]


def swap(value, axis, bit):
    count = lax.axis_size(axis)
    return lax.ppermute(value, axis, [(i, i ^ bit) for i in range(count)])


def exchange_sum(value, axis):
    for bit in bits_of(lax.axis_size(axis)):
        value = value + swap(value, axis, bit)
    return value


def exchange_pair(value, axis):
    bits = bits_of(lax.axis_size(axis))
    for bit in bits[:-1]:
        value = value + swap(value, axis, bit)
    return value, swap(value, axis, bits[-1])


def rounded_sum(*parts):
    return sum(part.astype(F32) for part in parts).astype(BF16)


def spread_rows(mine):
    parts = lax.axis_size("narrow")
    narrow_at = lax.axis_index("narrow")
    whole = jnp.zeros((parts,) + mine.shape, mine.dtype)
    for offset in range(parts):
        piece = mine if offset == 0 else swap(mine, "narrow", offset)
        whole = lax.dynamic_update_index_in_dim(whole, piece, narrow_at ^ offset, 0)
    return whole.reshape((-1,) + mine.shape[1:])


def slab_bits():
    low = lax.axis_size("wide") // SLABS
    return [low * bit for bit in bits_of(SLABS)], lax.axis_index("wide") // low


def gather_pieces(mine):
    parts = lax.axis_size("narrow")
    (low, a, b), _ = slab_bits()
    others = jnp.stack([swap(mine, "narrow", offset) for offset in range(1, parts)])
    half = mine.shape[0] // 2
    over_a, over_b = swap(others, "wide", a), swap(others, "wide", b)
    far_a = swap(over_b[:, :half], "wide", a)
    far_b = swap(over_a[:, half:], "wide", b)
    pieces = [(0, 0, others), (2, 0, over_a), (4, 0, over_b), (6, 0, far_a), (6, half, far_b)]
    return pieces + [(at ^ 1, first, swap(piece, "wide", low)) for at, first, piece in pieces]


def scatter_sums(far, rest, keep):
    (low, a, b), _ = slab_bits()
    got_far, got = swap(far, "wide", low), swap(rest, "wide", low)
    half = far.shape[0] // 2
    from_a = swap(rounded_sum(keep[3, :half], got_far[:half]), "wide", a)
    from_b = swap(rounded_sum(keep[3, half:], got_far[half:]), "wide", b)
    send_b = jnp.concatenate(
        [rounded_sum(keep[2, :half], got[2, :half], from_a), rounded_sum(keep[2, half:], got[2, half:])]
    )
    send_a = jnp.concatenate(
        [rounded_sum(keep[1, :half], got[1, :half]), rounded_sum(keep[1, half:], got[1, half:], from_b)]
    )
    got_a, got_b = swap(send_a, "wide", a), swap(send_b, "wide", b)
    result = sum(part.astype(F32) for part in (keep[0, 0], got[0, 0], got_a[0], got_b[0]))
    for offset in range(1, far.shape[0]):
        term = rounded_sum(keep[0, offset], got[0, offset], got_a[offset], got_b[offset])
        result = result + swap(term, "narrow", offset).astype(F32)
    wide_at, slab = lax.axis_index("wide"), result.shape[0]
    for bit in bits_of(low)[::-1]:
        result = result.reshape(2, -1, result.shape[-1])
        upper = (wide_at & bit) // bit
        held = lax.dynamic_index_in_dim(result, upper, 0, keepdims=False)
        sent = lax.dynamic_index_in_dim(result, 1 - upper, 0, keepdims=False)
        result = held + swap(sent, "wide", bit)
    return result


def mm(left, right):
    return lax.dot_general(left, right, (((1,), (0,)), ((), ())), preferred_element_type=F32)


def mm_t(left, right):
    return lax.dot_general(left, right, (((1,), (1,)), ((), ())), preferred_element_type=F32)


def t_mm(left, right):
    return lax.dot_general(left, right, (((0,), (0,)), ((), ())), preferred_element_type=F32)


def exact_mm(left, right):
    return lax.dot_general(
        left, right, (((1,), (0,)), ((), ())), precision=FULL, preferred_element_type=F32
    )


def norm(values, gain):
    inv = lax.rsqrt(jnp.mean(values * values, axis=-1, keepdims=True) + EPSILON)
    return values * inv * gain, inv


def norm_back(upstream, values, gain):
    inv = lax.rsqrt(jnp.mean(values * values, axis=-1, keepdims=True) + EPSILON)
    scaled = upstream * gain
    pull = jnp.mean(scaled * values, axis=-1, keepdims=True)
    return inv * scaled - values * (inv * inv * inv) * pull, jnp.sum(
        upstream * values * inv, axis=0, keepdims=True
    )


def gelu_both(x):
    scale = np.float32(np.sqrt(2.0 / np.pi))
    square = x * x
    bent = jnp.tanh(scale * (x + 0.044715 * square * x))
    half = 0.5 * (1.0 + bent)
    slope = half + 0.5 * x * (1.0 - bent * bent) * scale * (1.0 + 3 * 0.044715 * square)
    return x * half, slope


def toeplitz(row, rows):
    spread = jnp.broadcast_to(row, (rows, row.shape[1]))
    return pltpu.roll(spread, 0, 1, stride=1, stride_axis=0)


def diagonal_sums(matrix, lanes):
    rows, columns = matrix.shape
    flip = lax.broadcasted_iota(I32, (rows, rows), 0) + lax.broadcasted_iota(I32, (rows, rows), 1)
    turned = mm(jnp.where(flip == rows - 1, 1.0, 0.0).astype(BF16), matrix)
    if columns < lanes:
        turned = jnp.concatenate([turned, jnp.zeros((rows, lanes - columns), F32)], axis=1)
    turned = pltpu.roll(turned, 0, 1, stride=1, stride_axis=0)
    return jnp.sum(turned, axis=0, keepdims=True)


class In:
    def __init__(self, array, space=pltpu.VMEM):
        self.array = array
        self.spec = pl.BlockSpec(memory_space=space)


def smem(array):
    return In(array, pltpu.SMEM)


def anywhere(array):
    return In(array, pl.ANY)


def call(kernel, name, inputs, outs, scratch=(), vmem=24, us=2):
    inputs = [i if isinstance(i, In) else In(i) for i in inputs]
    return pl.pallas_call(
        kernel,
        out_shape=[jax.ShapeDtypeStruct(shape, dtype) for shape, dtype in outs],
        in_specs=[i.spec for i in inputs],
        out_specs=[pl.BlockSpec(memory_space=pltpu.VMEM)] * len(outs),
        scratch_shapes=list(scratch),
        compiler_params=pltpu.CompilerParams(vmem_limit_bytes=vmem * MIB),
        cost_estimate=pl.CostEstimate(flops=int(us * 1.1e9), bytes_accessed=0, transcendentals=0),
        name=name,
    )(*[i.array for i in inputs])


class Weights:
    def __init__(self, local, pieces, parts):
        self.local, self.pieces, self.parts = local, pieces, parts
        self.blocks = 1 + max(block for _, block, _ in local)
        self.rows = local[0][0].shape[1]
        self.slab = self.rows // SLABS
        self.inputs = [anywhere(array) for array, _, _ in local]
        self.inputs += [anywhere(piece) for _, _, piece in pieces]
        per_piece = sum(len(self.targets(first, piece.shape[1])) for _, first, piece in pieces)
        self.count = len(local) + (parts - 1) * per_piece
        self.scratch = [
            pltpu.VMEM((parts, self.blocks, self.rows, local[0][0].shape[1]), BF16),
            pltpu.SemaphoreType.DMA((self.count,)),
        ]

    def targets(self, first, rows):
        if rows < self.slab:
            return [(0, 0, first, rows)]
        return [
            (at, (first + at) // self.slab, 0, self.slab) for at in range(0, rows, self.slab)
        ]

    def start(self, where, refs, held, sem):
        slab, narrow_at = where[0], where[1]
        groups = [[] for _ in range(self.parts)]
        for (array, block, first), ref in zip(self.local, refs):
            groups[0].append((ref, held.at[narrow_at, block, pl.ds(first, array.shape[0])]))
        for offset in range(1, self.parts):
            for (at, first, piece), ref in zip(self.pieces, refs[len(self.local) :]):
                for source, block, row, rows in self.targets(first, piece.shape[1]):
                    target = pl.multiple_of((slab ^ at) * self.slab + row, 16)
                    groups[offset].append(
                        (
                            ref.at[offset - 1, pl.ds(source, rows)],
                            held.at[narrow_at ^ offset, block, pl.ds(target, rows)],
                        )
                    )
        made, number = [], 0
        for group in groups:
            copies = []
            for source, target in group:
                copies.append(pltpu.make_async_copy(source, target, sem.at[number]))
                copies[-1].start()
                number += 1
            made.append(copies)
        return made


def fetch_rows(weights, first, held, sem):
    copy = pltpu.make_async_copy(weights.at[:, 0, pl.ds(first, held.shape[1])], held, sem)
    copy.start()
    return copy


def wait_all(copies):
    for copy in copies:
        copy.wait()


def embed_rows(where, ids, table):
    count, (rows, width) = ids.shape[0], table.shape

    def kernel(where_ref, ids_ref, table_ref, out_ref, tiles, sums, sem):
        base = where_ref[3] * rows

        def tile_of(i):
            local = jnp.clip(ids_ref[i] - base, 0, rows - 1)
            return pl.multiple_of((local >> 4) << 4, 16)

        def copy(i):
            return pltpu.make_async_copy(
                table_ref.at[pl.ds(tile_of(i), 16)], tiles.at[i], sem.at[i]
            )

        @pl.loop(0, count)
        def _(i):
            copy(i).start()

        @pl.loop(0, count)
        def _(i):
            copy(i).wait()
            local = ids_ref[i] - base
            wanted = jnp.where((local >= 0) & (local < rows), local & 15, 16)
            match = lax.broadcasted_iota(I32, (16, width), 0) == wanted
            row = jnp.sum(jnp.where(match, tiles[i].astype(F32), 0.0), axis=0, keepdims=True)
            sums[pl.ds(i, 1), :] = row

        out_ref[...] = sums[...].astype(BF16)

    return call(
        kernel,
        "embed_rows",
        [smem(where), smem(ids), anywhere(table)],
        [((count, width), BF16)],
        [pltpu.VMEM((count, 16, width), BF16), pltpu.VMEM((count, width), F32), pltpu.SemaphoreType.DMA((count,))],
    )[0]


def causal_mask(count, answers):
    query = lax.broadcasted_iota(I32, (count, count), 0)
    key = lax.broadcasted_iota(I32, (count, count), 1)
    return (query // answers == key // answers) & (key <= query)


def masked_softmax(scores, allowed):
    masked = jnp.where(allowed, scores, MASKED)
    exponent = jnp.exp(masked - jnp.max(masked, axis=-1, keepdims=True))
    return exponent / jnp.sum(exponent, axis=-1, keepdims=True)


def decoder_self(embedded, gains, inward, outward, bias_line, answers):
    count, width = embedded.shape
    inner = outward.shape[0]

    def kernel(x_ref, gains_ref, in_ref, out_w_ref, line_ref, normed_ref, proj_ref, ctx_ref, part_ref):
        x = x_ref[...].astype(F32)
        normed = norm(x, gains_ref[0:1])[0].astype(BF16)
        normed_ref[...] = normed
        proj = mm_t(normed, in_ref[...]).astype(BF16)
        proj_ref[...] = proj
        allowed = causal_mask(count, answers)
        contexts = []
        for h in range(inner // HD):
            q, k, v = [proj[:, s * inner + h * HD : s * inner + (h + 1) * HD] for s in range(3)]
            scores = mm_t(q, k) + toeplitz(line_ref[h : h + 1], count)[:, :count]
            contexts.append(mm(masked_softmax(scores, allowed).astype(BF16), v).astype(BF16))
        context = jnp.concatenate(contexts, axis=1)
        ctx_ref[...] = context
        part_ref[...] = mm(context, out_w_ref[...])

    return call(
        kernel,
        "decoder_self",
        [embedded, gains, inward, outward, bias_line],
        [((count, width), BF16), ((count, 3 * inner), BF16), ((count, inner), BF16), ((count, width), F32)],
    )


def encoder_attention(where, tokens, segments, gains, bias_line, weights):
    length, width = segments.shape[1], tokens.shape[1]
    inner = bias_line.shape[1] * HD
    parts = weights.parts

    def kernel(where_ref, tokens_ref, seg_ref, gains_ref, line_ref, *refs):
        pieces, refs = refs[: len(weights.inputs)], refs[len(weights.inputs) :]
        hidden_ref, normed_ref, qkv_ref, ctx_ref, held, sem, own, own_sem = refs
        narrow_at = where_ref[1]
        fetch = pltpu.make_async_copy(
            tokens_ref.at[pl.ds(pl.multiple_of(narrow_at * length, 16), length)], own, own_sem
        )
        fetch.start()
        loads = weights.start(where_ref, pieces, held, sem)
        allowed = same_segment(seg_ref[pl.ds(narrow_at, 1), :])
        fetch.wait()
        x = own[...].astype(F32)
        normed = norm(x, gains_ref[0:1])[0].astype(BF16)
        normed_ref[...] = normed
        hidden_ref[...] = x
        for copies in loads:
            wait_all(copies)

        @pl.loop(0, parts)
        def _(z):
            proj = mm_t(normed, held[z, 0, : 3 * inner]).astype(BF16)
            qkv_ref[z] = proj
            contexts = []
            for h in range(inner // HD):
                q, k, v = [proj[:, s * inner + h * HD : s * inner + (h + 1) * HD] for s in range(3)]
                line = line_ref[z ^ narrow_at, h : h + 1]
                scores = mm_t(q, k) + toeplitz(line, length)[:, :length]
                contexts.append(mm(masked_softmax(scores, allowed).astype(BF16), v).astype(BF16))
            context = jnp.concatenate(contexts, axis=1)
            ctx_ref[z] = context
            hidden_ref[...] += mm(context, held[z, 0, 3 * inner :])

    return call(
        kernel,
        "encoder_attention",
        [smem(where), anywhere(tokens), segments, gains, bias_line] + weights.inputs,
        [
            ((length, width), F32),
            ((length, width), BF16),
            ((parts, length, 3 * inner), BF16),
            ((parts, length, inner), BF16),
        ],
        weights.scratch + [pltpu.VMEM((length, width), BF16), pltpu.SemaphoreType.DMA],
        vmem=32,
        us=15,
    )


def same_segment(row):
    length = row.shape[1]
    across = jnp.broadcast_to(row.astype(F32), (length, length))
    diagonal = lax.broadcasted_iota(I32, (length, length), 0) == lax.broadcasted_iota(
        I32, (length, length), 1
    )
    down = jnp.sum(jnp.where(diagonal, across, 0.0), axis=1, keepdims=True)
    return across == down


def encoder_ffn(where, hidden, gains, weights):
    length, width = hidden.shape
    parts = weights.parts
    units = weights.rows

    def kernel(where_ref, hidden_ref, gains_ref, *refs):
        pieces, refs = refs[: len(weights.inputs)], refs[len(weights.inputs) :]
        normed_ref, act_ref, slope_ref, summed_ref, memory_ref, held, sem = refs
        loads = weights.start(where_ref, pieces, held, sem)
        narrow_at = where_ref[1]
        x = hidden_ref[...]
        normed = norm(x, gains_ref[1:2])[0].astype(BF16)
        normed_ref[...] = normed
        total = x
        for offset in range(parts):
            z = narrow_at ^ offset
            wait_all(loads[offset])
            act, slope = gelu_both(mm(normed, held[z, 1]))
            act = act.astype(BF16)
            act_ref[z] = act
            slope_ref[z] = slope
            total = total + mm(act, held[z, 0])
        summed_ref[...] = total
        memory_ref[...] = norm(total, gains_ref[2:3])[0].astype(BF16)

    return call(
        kernel,
        "encoder_ffn",
        [smem(where), hidden, gains] + weights.inputs,
        [
            ((length, width), BF16),
            ((parts, length, units), BF16),
            ((parts, length, units), F32),
            ((length, width), F32),
            ((length, width), BF16),
        ],
        weights.scratch,
        vmem=40,
        us=17,
    )


def cross_forward(where, memory, embedded, self_sums, gains, weights, answers, inner):
    length, width = memory.shape
    count = embedded.shape[0]
    parts = weights.parts
    heads = inner // HD

    def kernel(where_ref, memory_ref, embedded_ref, one_ref, two_ref, gains_ref, *refs):
        pieces, refs = refs[: len(weights.inputs)], refs[len(weights.inputs) :]
        first_ref, normed_ref, q_ref, kv_ref, stats_ref, held, sem = refs
        loads = weights.start(where_ref, pieces, held, sem)
        narrow_at = where_ref[1]
        first = embedded_ref[...].astype(F32) + (one_ref[...] + two_ref[...])
        first_ref[...] = first
        normed = norm(first, gains_ref[1:2])[0].astype(BF16)
        normed_ref[...] = normed
        memory = memory_ref[...]
        mine = lax.broadcasted_iota(I32, (count, 1), 0) // answers == where_ref[2]
        lane = lax.broadcasted_iota(I32, (count, 128), 1)
        stats = jnp.where(lane < 64, MASKED, 0.0)
        for copies in loads:
            wait_all(copies)
        sums = []
        for z in range(parts):
            kv = mm_t(memory, held[z, 0, : 2 * inner]).astype(BF16)
            kv_ref[z] = kv
            queries = mm_t(normed, held[z, 0, 3 * inner :]).astype(BF16)
            q_ref[z] = queries
            for h in range(heads):
                k, v = [kv[:, s * inner + h * HD : s * inner + (h + 1) * HD] for s in range(2)]
                scores = mm_t(queries[:, h * HD : (h + 1) * HD], k)
                largest = jnp.max(scores, axis=-1, keepdims=True)
                exponent = jnp.where(mine, jnp.exp(scores - largest), 0.0)
                high = exponent.astype(BF16)
                low = (exponent - high.astype(F32)).astype(BF16)
                sums.append(mm(high, v) + mm(low, v))
                at = z * heads + h
                stats = jnp.where(lane == at, jnp.where(mine, largest, MASKED), stats)
                stats = jnp.where(lane == 64 + at, jnp.sum(exponent, axis=-1, keepdims=True), stats)
        stats_ref[...] = jnp.concatenate(sums + [stats], axis=1)

    return call(
        kernel,
        "cross_forward",
        [smem(where), memory, embedded, *self_sums, gains] + weights.inputs,
        [
            ((count, width), F32),
            ((count, width), BF16),
            ((parts, count, inner), BF16),
            ((parts, length, 2 * inner), BF16),
            ((count, width + 128), F32),
            (weights.scratch[0].shape, BF16),
        ],
        weights.scratch[1:],
        vmem=32,
        us=9,
    )


def spread_heads(stats, first, heads):
    count = stats.shape[0]
    return jnp.concatenate(
        [jnp.broadcast_to(stats[:, first + h : first + h + 1], (count, HD)) for h in range(heads)], axis=1
    )


def merge(one, two):
    width = one.shape[1] - 128
    heads = width // HD
    stats_one, stats_two = one[:, width:], two[:, width:]

    def join(largest_one, largest_two, value_one, value_two):
        ahead = largest_one >= largest_two
        scale = jnp.exp(
            jnp.where(ahead, largest_two, largest_one) - jnp.where(ahead, largest_one, largest_two)
        )
        return jnp.where(ahead, value_one, value_two) + scale * jnp.where(ahead, value_two, value_one)

    sums = join(
        spread_heads(stats_one, 0, heads), spread_heads(stats_two, 0, heads), one[:, :width], two[:, :width]
    )
    totals = join(stats_one[:, :64], stats_two[:, :64], stats_one[:, 64:], stats_two[:, 64:])
    stats = jnp.concatenate([jnp.maximum(stats_one[:, :64], stats_two[:, :64]), totals], axis=1)
    return sums, stats


def merge_stats(one, two):
    def kernel(one_ref, two_ref, out_ref):
        sums, stats = merge(one_ref[...], two_ref[...])
        out_ref[...] = jnp.concatenate([sums, stats], axis=1)

    return call(kernel, "merge_stats", [one, two], [(one.shape, F32)])[0]


def decoder_middle(one, two, first, cross_weights, gains, grow, shrink, grad_output, inner):
    count, width = first.shape
    parts = width // inner
    heads = width // HD

    def kernel(one_ref, two_ref, first_ref, out_w_ref, gains_ref, grow_ref, shrink_ref, up_ref, *refs):
        exact_ref, stats_ref, ctx_ref, second_ref, normed_ref, act_ref, back_ref, part_ref, out_ref, held, sem = refs
        fetch = fetch_rows(out_w_ref, 2 * inner, held, sem)
        sums, stats = merge(one_ref[...], two_ref[...])
        stats_ref[...] = stats
        exact = sums / spread_heads(stats, 64, heads)
        exact_ref[...] = exact
        context = exact.astype(BF16)
        ctx_ref[...] = context
        fetch.wait()
        branch = mm(context[:, :inner], held[0])
        for z in range(1, parts):
            branch = branch + mm(context[:, z * inner : (z + 1) * inner], held[z])
        second = first_ref[...] + branch
        second_ref[...] = second
        normed = norm(second, gains_ref[2:3])[0].astype(BF16)
        normed_ref[...] = normed
        act, slope = gelu_both(mm(normed, grow_ref[...]))
        act = act.astype(BF16)
        act_ref[...] = act
        back = (mm_t(up_ref[...], shrink_ref[...]) * slope).astype(BF16)
        back_ref[...] = back
        part_ref[...] = mm_t(back, grow_ref[...])
        out_ref[...] = mm(act, shrink_ref[...])

    units = grow.shape[1]
    return call(
        kernel,
        "decoder_middle",
        [
            one,
            two,
            first,
            anywhere(cross_weights),
            gains,
            grow,
            shrink,
            grad_output,
        ],
        [
            ((count, width), F32),
            ((count, 128), F32),
            ((count, width), BF16),
            ((count, width), F32),
            ((count, width), BF16),
            ((count, units), BF16),
            ((count, units), BF16),
            ((count, width), F32),
            ((count, width), F32),
        ],
        [pltpu.VMEM((parts, inner, width), BF16), pltpu.SemaphoreType.DMA],
    )


def cross_backward(
    where, third_sums, second, gains, grad_output, cross_weights, kv, queries, stats, exact,
    grad_memory, summed, enc_gains, answers,
):
    count, width = second.shape
    parts, length, inner = kv.shape[0], kv.shape[1], kv.shape[2] // 2
    heads = inner // HD

    def kernel(where_ref, one_ref, two_ref, second_ref, gains_ref, up_ref, weights_ref, kv_ref, q_ref, *refs):
        stats_ref, exact_ref, memory_ref, summed_ref, enc_gains_ref = refs[:5]
        grad_second_ref, branch_ref, grad_kv_ref, query_ref, grad_ref, low_ref, gain_ref, own, sem = refs[5:14]
        kv_held, kv_sem, out_held, out_sem = refs[14:]
        out_fetch = fetch_rows(weights_ref, 2 * inner, out_held, out_sem)
        kv_fetch = fetch_rows(weights_ref, 0, kv_held, kv_sem)
        fetch = pltpu.make_async_copy(
            memory_ref.at[pl.ds(pl.multiple_of(where_ref[1] * length, 16), length)], own, sem
        )
        fetch.start()
        grad_third, third_gain = norm_back(one_ref[...] + two_ref[...], second_ref[...], gains_ref[2:3])
        grad_second = up_ref[...].astype(F32) + grad_third
        grad_second_ref[...] = grad_second
        branch = grad_second.astype(BF16)
        branch_ref[...] = branch
        mine = lax.broadcasted_iota(I32, (count, 1), 0) // answers == where_ref[2]
        stats = stats_ref[...]
        logsum = stats[:, :64] + jnp.log(stats[:, 64:])
        exact = exact_ref[...]
        fetch.wait()
        total = own[...].astype(F32)
        out_fetch.wait()
        kv_fetch.wait()
        query_parts = []
        for z in range(parts):
            context = mm_t(branch, out_held[z]).astype(BF16)
            deltas = context.astype(F32) * exact[:, z * inner : (z + 1) * inner]
            grad_keys, grad_values = [], []
            for h in range(heads):
                at = z * heads + h
                k, v = [kv_ref[z, :, s * inner + h * HD : s * inner + (h + 1) * HD] for s in range(2)]
                q = q_ref[z, :, h * HD : (h + 1) * HD]
                up = context[:, h * HD : (h + 1) * HD]
                probs = jnp.where(mine, jnp.exp(mm_t(q, k) - logsum[:, at : at + 1]), 0.0)
                delta = jnp.sum(deltas[:, h * HD : (h + 1) * HD], axis=-1, keepdims=True)
                grad_scores = (probs * (mm_t(up, v) - delta)).astype(BF16)
                query_parts.append(mm(grad_scores, k))
                grad_keys.append(t_mm(grad_scores, q).astype(BF16))
                grad_values.append(t_mm(probs.astype(BF16), up).astype(BF16))
            grad_kv = jnp.concatenate(grad_keys + grad_values, axis=1)
            grad_kv_ref[z] = grad_kv
            total = total + mm(grad_kv, kv_held[z])
        query_ref[...] = jnp.concatenate(query_parts, axis=1)
        grad, gain = norm_back(total, summed_ref[...], enc_gains_ref[2:3])
        grad_ref[...] = grad
        low_ref[...] = grad.astype(BF16)
        gain_ref[...] = jnp.concatenate([gain, third_gain], axis=0)

    return call(
        kernel,
        "cross_backward",
        [
            smem(where),
            *third_sums,
            second,
            gains,
            grad_output,
            anywhere(cross_weights),
            kv,
            queries,
            stats,
            exact,
            anywhere(grad_memory),
            summed,
            enc_gains,
        ],
        [
            ((count, width), F32),
            ((count, width), BF16),
            (kv.shape, BF16),
            ((count, width), F32),
            ((length, width), F32),
            ((length, width), BF16),
            ((2, width), F32),
        ],
        [
            pltpu.VMEM((length, width), BF16),
            pltpu.SemaphoreType.DMA,
            pltpu.VMEM((parts, 2 * inner, width), BF16),
            pltpu.SemaphoreType.DMA,
            pltpu.VMEM((parts, inner, width), BF16),
            pltpu.SemaphoreType.DMA,
        ],
        vmem=32,
        us=9,
    )


def ffn_backward(where, grad_summed, slope, hidden, gains, weights):
    length, width = hidden.shape
    parts = weights.parts

    def kernel(where_ref, grad_ref, slope_ref, hidden_ref, gains_ref, *refs):
        pieces, refs = refs[: len(weights.inputs)], refs[len(weights.inputs) :]
        grown_ref, out_ref, gain_ref, held, sem = refs
        loads = weights.start(where_ref, pieces, held, sem)
        narrow_at = where_ref[1]
        grad = grad_ref[...]
        branch = grad.astype(BF16)
        total = jnp.zeros((length, width), F32)
        for offset in range(parts):
            z = narrow_at ^ offset
            wait_all(loads[offset])
            grown = (mm_t(branch, held[z, 0]) * slope_ref[z]).astype(BF16)
            grown_ref[z] = grown
            total = total + mm_t(grown, held[z, 1])
        pulled, gain = norm_back(total, hidden_ref[...], gains_ref[1:2])
        out_ref[...] = grad + pulled
        gain_ref[...] = gain

    return call(
        kernel,
        "ffn_backward",
        [smem(where), grad_summed, slope, hidden, gains] + weights.inputs,
        [(slope.shape, BF16), ((length, width), F32), ((1, width), F32)],
        weights.scratch,
        vmem=40,
        us=17,
    )


def weight_grads(where, pairs, name):
    parts, (length, width) = pairs[0][1].shape[0], pairs[0][0].shape
    lanes = sum(right.shape[-1] for _, right in pairs)
    rows = width // SLABS
    lefts = []
    for left, _ in pairs:
        if not any(left is known for known in lefts):
            lefts.append(left)

    def kernel(where_ref, *refs):
        left_refs, refs = refs[: len(lefts)], refs[len(lefts) :]
        right_refs, refs = refs[: len(pairs)], refs[len(pairs) :]
        far_ref, rest_ref, keep_ref, held = refs
        slab, narrow_at = where_ref[0], where_ref[1]
        turned = [ref[...].T for ref in left_refs]
        for offset in range(parts):
            first = 0
            for (left, right), ref in zip(pairs, right_refs):
                which = [number for number, known in enumerate(lefts) if known is left][0]
                last = first + right.shape[-1]
                held[:, first:last] = mm(turned[which], ref[narrow_at ^ offset]).astype(BF16)
                first = last
            for at in range(SLABS):
                block = held[pl.ds(pl.multiple_of((slab ^ at) * rows, 16), rows), :]
                if at == 7:
                    far_ref[offset] = block
                elif at & 1:
                    rest_ref[at >> 1, offset] = block
                else:
                    keep_ref[at >> 1, offset] = block

    return call(
        kernel,
        name,
        [smem(where)] + lefts + [right for _, right in pairs],
        [
            ((parts, rows, lanes), BF16),
            ((3, parts, rows, lanes), BF16),
            ((4, parts, rows, lanes), BF16),
        ],
        [pltpu.VMEM((width, lanes), BF16)],
        vmem=40,
        us=6,
    )


def attention_backward(
    where, grad_hidden, hidden_gains, normed, qkv, tokens, segments, gains, bias_line, buckets, weights
):
    length, width = grad_hidden.shape
    inner = bias_line.shape[1] * HD
    heads = inner // HD
    parts = weights.parts
    lanes, bucket_count = buckets.shape

    def kernel(where_ref, grad_ref, known_ref, second_ref, qkv_ref, tokens_ref, seg_ref, gains_ref, line_ref, buckets_ref, *refs):
        pieces, refs = refs[: len(weights.inputs)], refs[len(weights.inputs) :]
        branch_ref, dqkv_ref, out_ref, shared_ref, held, sem, own, own_sem, sums, total = refs
        narrow_at = where_ref[1]
        loads = weights.start(where_ref, pieces, held, sem)
        fetch = pltpu.make_async_copy(
            tokens_ref.at[pl.ds(pl.multiple_of(narrow_at * length, 16), length)], own, own_sem
        )
        fetch.start()
        allowed = same_segment(seg_ref[pl.ds(narrow_at, 1), :])
        grad = grad_ref[...]
        branch = grad.astype(BF16)
        branch_ref[...] = branch
        total[...] = jnp.zeros((length, width), F32)
        sums[...] = jnp.zeros(sums.shape, F32)
        for copies in loads:
            wait_all(copies)

        @pl.loop(0, parts)
        def _(z):
            context = mm_t(branch, held[z, 0, 3 * inner :]).astype(BF16)
            proj = qkv_ref[z]
            grads = [[], [], []]
            for h in range(heads):
                q, k, v = [proj[:, s * inner + h * HD : s * inner + (h + 1) * HD] for s in range(3)]
                up = context[:, h * HD : (h + 1) * HD]
                line = line_ref[z ^ narrow_at, h : h + 1]
                scores = mm_t(q, k) + toeplitz(line, length)[:, :length]
                probs = masked_softmax(scores, allowed)
                grad_probs = mm_t(up, v)
                delta = jnp.sum(grad_probs * probs, axis=-1, keepdims=True)
                grad_scores = (probs * (grad_probs - delta)).astype(BF16)
                sums[z, h : h + 1, :] = diagonal_sums(grad_scores, lanes)
                grads[0].append(mm(grad_scores, k).astype(BF16))
                grads[1].append(t_mm(grad_scores, q).astype(BF16))
                grads[2].append(t_mm(probs.astype(BF16), up).astype(BF16))
            dqkv = jnp.concatenate(grads[0] + grads[1] + grads[2], axis=1)
            dqkv_ref[z] = dqkv
            total[...] += mm(dqkv, held[z, 0, : 3 * inner])

        fetch.wait()
        pulled, gain = norm_back(total[...], own[...].astype(F32), gains_ref[0:1])
        out_ref[...] = (grad_ref[...] + pulled).astype(BF16)
        tables = [exact_mm(sums[z], buckets_ref[...]) for z in range(parts)]
        blank = jnp.zeros((8, width - parts * bucket_count), F32)
        first_rows = jnp.concatenate([gain, second_ref[...], known_ref[0:1], jnp.zeros((5, width), F32)], axis=0)
        shared_ref[...] = jnp.concatenate(
            [first_rows, jnp.concatenate(tables + [blank], axis=1)], axis=0
        )

    return call(
        kernel,
        "attention_backward",
        [smem(where), grad_hidden, *hidden_gains, qkv, anywhere(tokens), segments, gains, bias_line, buckets]
        + weights.inputs,
        [((length, width), BF16), (qkv.shape, BF16), ((length, width), BF16), ((16, width), F32)],
        weights.scratch
        + [
            pltpu.VMEM((length, width), BF16),
            pltpu.SemaphoreType.DMA,
            pltpu.VMEM((parts, 8, lanes), F32),
            pltpu.VMEM((length, width), F32),
        ],
        vmem=40,
        us=15,
    )


def decoder_weights(where, context, branch, normed, back, act, grad_output, inner):
    count, width = context.shape
    parts = width // inner

    def kernel(where_ref, ctx_ref, branch_ref, normed_ref, back_ref, act_ref, up_ref, outward_ref, grow_ref, shrink_ref):
        mine = jnp.zeros((count, inner), BF16)
        for z in range(parts):
            mine = jnp.where(where_ref[1] == z, ctx_ref[:, z * inner : (z + 1) * inner], mine)
        outward_ref[...] = t_mm(mine, branch_ref[...])
        grow_ref[...] = t_mm(normed_ref[...], back_ref[...])
        shrink_ref[...] = t_mm(act_ref[...], up_ref[...])

    return call(
        kernel,
        "decoder_weights",
        [smem(where), context, branch, normed, back, act, grad_output],
        [((inner, width), F32), ((width, back.shape[1]), F32), ((act.shape[1], width), F32)],
    )


def decoder_backward(
    where, query_sums, cross_weights, cross_normed, first, grad_second, gains, outward, inward, context,
    normed, proj, bias_line, buckets, answers,
):
    count, width = first.shape
    inner = outward.shape[0]
    heads = inner // HD
    parts = width // inner
    lanes, bucket_count = buckets.shape

    def kernel(where_ref, one_ref, two_ref, query_w_ref, cross_normed_ref, first_ref, grad_second_ref, gains_ref, *refs):
        outward_ref, inward_ref, ctx_ref, normed_ref, proj_ref, line_ref, buckets_ref = refs[:7]
        first_out, query_out, outward_out, inward_out, part_out, bias_out, gain_out, held, sem = refs[7:]
        fetch = fetch_rows(query_w_ref, 3 * inner, held, sem)
        grad_queries = (one_ref[...] + two_ref[...]).astype(BF16)
        mine = jnp.zeros((count, inner), BF16)
        total = jnp.zeros((count, width), F32)
        fetch.wait()
        for z in range(parts):
            block = grad_queries[:, z * inner : (z + 1) * inner]
            mine = jnp.where(where_ref[1] == z, block, mine)
            total = total + mm(block, held[z])
        query_out[...] = t_mm(mine, cross_normed_ref[...])
        pulled, gain = norm_back(total, first_ref[...], gains_ref[1:2])
        gain_out[...] = gain
        grad_first = grad_second_ref[...] + pulled
        first_out[...] = grad_first
        branch = grad_first.astype(BF16)
        outward_out[...] = t_mm(ctx_ref[...], branch)
        up_all = mm_t(branch, outward_ref[...]).astype(BF16)
        proj = proj_ref[...]
        allowed = causal_mask(count, answers)
        grads, bias_rows = [[], [], []], []
        for h in range(heads):
            q, k, v = [proj[:, s * inner + h * HD : s * inner + (h + 1) * HD] for s in range(3)]
            up = up_all[:, h * HD : (h + 1) * HD]
            scores = mm_t(q, k) + toeplitz(line_ref[h : h + 1], count)[:, :count]
            probs = masked_softmax(scores, allowed)
            grad_probs = mm_t(up, v)
            delta = jnp.sum(grad_probs * probs, axis=-1, keepdims=True)
            grad_scores = (probs * (grad_probs - delta)).astype(BF16)
            bias_rows.append(diagonal_sums(grad_scores, lanes))
            grads[0].append(mm(grad_scores, k).astype(BF16))
            grads[1].append(t_mm(grad_scores, q).astype(BF16))
            grads[2].append(t_mm(probs.astype(BF16), up).astype(BF16))
        dqkv = jnp.concatenate(grads[0] + grads[1] + grads[2], axis=1)
        inward_out[...] = t_mm(dqkv, normed_ref[...])
        part_out[...] = mm(dqkv, inward_ref[...])
        bias_out[...] = exact_mm(jnp.concatenate(bias_rows, axis=0), buckets_ref[...])

    return call(
        kernel,
        "decoder_backward",
        [
            smem(where),
            *query_sums,
            anywhere(cross_weights),
            cross_normed,
            first,
            grad_second,
            gains,
            outward,
            inward,
            context,
            normed,
            proj,
            bias_line,
            buckets,
        ],
        [
            ((count, width), F32),
            ((inner, width), F32),
            ((inner, width), F32),
            ((3 * inner, width), F32),
            ((count, width), F32),
            ((heads, bucket_count), F32),
            ((1, width), F32),
        ],
        [pltpu.VMEM((parts, inner, width), BF16), pltpu.SemaphoreType.DMA],
    )


def vocabulary_grads(where, ids, zero_sums, embedded, gains, grad_first, second, cross_gain, known_gains, rows):
    count, width = embedded.shape

    def kernel(where_ref, ids_ref, one_ref, two_ref, embedded_ref, gains_ref, first_ref, second_ref, *refs):
        cross_ref, known_ref, table_ref, output_ref, gain_ref, grads = refs
        sums = one_ref[...] + two_ref[...]
        output_ref[...] = (second_ref[...] + sums[count:]).astype(BF16)
        pulled, gain = norm_back(sums[:count], embedded_ref[...].astype(F32), gains_ref[0:1])
        gain_ref[...] = jnp.concatenate([gain, cross_ref[...], known_ref[1:2]], axis=0)
        grads[...] = first_ref[...] + pulled
        table_ref[...] = jnp.zeros(table_ref.shape, F32)
        base = where_ref[3] * rows

        @pl.loop(0, count)
        def _(i):
            local = ids_ref[i] - base

            @pl.when((local >= 0) & (local < rows))
            def _():
                table_ref[pl.ds(local, 1), :] += grads[pl.ds(i, 1), :]

    return call(
        kernel,
        "vocabulary_grads",
        [smem(where), smem(ids), *zero_sums, embedded, gains, grad_first, second, cross_gain, known_gains],
        [((rows, width), F32), ((count, width), BF16), ((3, width), F32)],
        [pltpu.VMEM((count, width), F32)],
        vmem=32,
    )


def both_bucket(offset):
    spread = np.abs(offset)
    far = 8 + sum((spread >= edge).astype(np.int32) for edge in BOTH_EDGES)
    return np.where(offset > 0, 16, 0) + np.where(spread < 8, spread, far)


def causal_bucket(offset):
    back = np.maximum(-offset, 0)
    far = 16 + sum((back >= edge).astype(np.int32) for edge in CAUSAL_EDGES)
    return np.where(back < 16, back, far)


def bucket_lines(bucket, count, buckets):
    lanes = 128
    while lanes < 2 * count:
        lanes *= 2
    place = np.arange(lanes)
    turning = bucket(np.where(place < lanes // 2, place, place - lanes))
    straight = bucket(place - (count - 1))
    rows = np.arange(buckets)
    return (
        (rows[:, None] == turning[None]).astype(np.float32),
        (straight[:, None] == rows[None]).astype(np.float32),
    )


def per_device(
    tokens,
    segments,
    question,
    answer_ids,
    vocab_table,
    enc_gains,
    enc_inward,
    encoder_bias,
    enc_outward,
    enc_grow,
    enc_shrink,
    cross_key_value_weight,
    dec_gains,
    dec_inward,
    decoder_bias,
    dec_outward,
    cross_query,
    cross_outward,
    dec_grow,
    dec_shrink,
    grad_memory,
    grad_output,
):
    parts = lax.axis_size("narrow")
    narrow_at = lax.axis_index("narrow")
    bits, slab = slab_bits()
    low = bits[0]
    length = segments.shape[1]
    width = tokens.shape[1]
    inner = enc_outward.shape[0]
    heads = inner // HD
    questions, answers = answer_ids.shape
    count = questions * answers
    ids = answer_ids.reshape(-1)
    own_question = lax.dynamic_index_in_dim(question, narrow_at, 0, keepdims=False)
    where = jnp.stack([slab, narrow_at, own_question, lax.axis_index("wide")]).astype(I32)

    def turned(weight):
        return jnp.transpose(weight, (1, 2, 0)).reshape(-1, width)

    enc_in, dec_in, cross_kv = turned(enc_inward), turned(dec_inward), turned(cross_key_value_weight)
    cross_q = cross_query.T

    def own_slab(*matrices):
        whole = matrices[0] if len(matrices) == 1 else jnp.concatenate(matrices)
        rows = whole.shape[0] // SLABS
        return lax.dynamic_slice_in_dim(whole, slab * rows, rows, 0)

    attn_pieces = gather_pieces(own_slab(enc_in, enc_outward))
    ffn_pieces = gather_pieces(jnp.concatenate([own_slab(enc_shrink), own_slab(enc_grow)]))
    cross_pieces = gather_pieces(own_slab(cross_kv, cross_outward, cross_q))
    attn_weights = Weights([(enc_in, 0, 0), (enc_outward, 0, 3 * inner)], attn_pieces, parts)
    ffn_weights = Weights([(enc_shrink, 0, 0), (enc_grow, 1, 0)], ffn_pieces, parts)
    cross_weights = Weights(
        [(cross_kv, 0, 0), (cross_outward, 0, 2 * inner), (cross_q, 0, 3 * inner)], cross_pieces, parts
    )

    table = encoder_bias.T
    tables = jnp.stack([table] + [swap(table, "narrow", offset) for offset in range(1, parts)])
    both, both_sums = bucket_lines(both_bucket, length, table.shape[1])
    causal, causal_sums = bucket_lines(causal_bucket, count, table.shape[1])
    enc_line = jnp.einsum("zhb,bt->zht", tables, both, precision=FULL)
    dec_line = jnp.einsum("bh,bt->ht", decoder_bias, causal, precision=FULL)

    vocab_local = vocab_table.shape[0]
    if vocab_local % 16 == 0:
        embedded = embed_rows(where, ids, vocab_table)
    else:
        local_ids = where[3] * vocab_local + jnp.arange(vocab_local, dtype=I32)
        one_hot = (ids[:, None] == local_ids[None, :]).astype(BF16)
        embedded = jnp.dot(one_hot, vocab_table, preferred_element_type=F32).astype(BF16)
    embedded = exchange_sum(embedded, "wide")
    dec_normed, dec_proj, dec_context, self_part = decoder_self(
        embedded, dec_gains, dec_in, dec_outward, dec_line, answers
    )
    self_sums = exchange_pair(self_part, "narrow")

    hidden, first_normed, qkv, context = encoder_attention(
        where, tokens, segments, enc_gains, enc_line, attn_weights
    )
    second_normed, act, slope, summed, memory = encoder_ffn(where, hidden, enc_gains, ffn_weights)

    dec_first, cross_normed, queries, kv, stats, cross_all = cross_forward(
        where, memory, embedded, self_sums, dec_gains, cross_weights, answers, inner
    )
    steps = [("wide", bit) for bit in bits_of(lax.axis_size("wide"))]
    steps += [("narrow", bit) for bit in bits_of(parts)]
    for axis, bit in steps[:-1]:
        stats = merge_stats(stats, swap(stats, axis, bit))
    exact, stats, cross_context, dec_second, third_normed, dec_act, dec_back, third_part, output_part = decoder_middle(
        stats, swap(stats, *steps[-1]), dec_first, cross_all, dec_gains, dec_grow, dec_shrink, grad_output, inner
    )
    third_sums = exchange_pair(third_part, "narrow")
    grad_dec_second, cross_branch, grad_kv, query_part, grad_summed, ffn_branch, known_gains = cross_backward(
        where, third_sums, dec_second, dec_gains, grad_output, cross_all, kv, queries, stats, exact,
        grad_memory, summed, enc_gains, answers,
    )

    sent_early = scatter_sums(*weight_grads(where, [(ffn_branch, act), (memory, grad_kv)], "shrink_weight_grads"))
    grad_grown, grad_hidden, second_gain = ffn_backward(
        where, grad_summed, slope, hidden, enc_gains, ffn_weights
    )
    sent_grow = scatter_sums(*weight_grads(where, [(second_normed, grad_grown)], "grow_weight_grads"))
    attn_branch, grad_qkv, own_grad_tokens, shared = attention_backward(
        where, grad_hidden, (known_gains, second_gain), first_normed, qkv, tokens, segments, enc_gains,
        enc_line, jnp.asarray(both_sums), attn_weights,
    )
    sent_attn = scatter_sums(
        *weight_grads(where, [(first_normed, grad_qkv), (attn_branch, context)], "attention_weight_grads")
    )
    grad_tokens = spread_rows(own_grad_tokens)
    memory_out = spread_rows(memory)
    shared = exchange_sum(exchange_sum(shared, "wide"), "narrow")

    grad_cross_outward, grad_dec_grow, grad_dec_shrink = decoder_weights(
        where, cross_context, cross_branch, third_normed, dec_back, dec_act, grad_output, inner
    )
    query_sums = exchange_pair(exchange_sum(query_part, "wide"), "narrow")
    grad_dec_first, grad_cross_q, grad_dec_outward, grad_dec_in, zero_part, dec_bias_grads, cross_gain = decoder_backward(
        where, query_sums, cross_all, cross_normed, dec_first, grad_dec_second, dec_gains, dec_outward, dec_in,
        dec_context, dec_normed, dec_proj, dec_line, jnp.asarray(causal_sums), answers,
    )
    zero_sums = exchange_pair(jnp.concatenate([zero_part, output_part]), "narrow")
    grad_vocab_table, output, grad_dec_gains = vocabulary_grads(
        where, ids, zero_sums, embedded, dec_gains, grad_dec_first, dec_second, cross_gain, known_gains, vocab_local
    )

    units = enc_grow.shape[1]
    sent_shrink, sent_cross = sent_early[:, :units], sent_early[:, units:]
    own_bias = lax.dynamic_slice(shared, (8, narrow_at * table.shape[1]), (heads, table.shape[1]))
    rows = sent_attn.shape[0]
    return (
        memory_out,
        output,
        grad_tokens,
        grad_vocab_table,
        shared[:3],
        sent_attn[:, : 3 * inner].reshape(rows, 3, inner),
        own_bias.T,
        sent_attn[:, 3 * inner :].T,
        sent_grow,
        sent_shrink.T,
        sent_cross.reshape(rows, 2, inner),
        grad_dec_gains,
        jnp.transpose(grad_dec_in.reshape(3, inner, width), (2, 0, 1)),
        dec_bias_grads.T,
        grad_dec_outward,
        grad_cross_q.T,
        grad_cross_outward,
        grad_dec_grow,
        grad_dec_shrink,
    )


def solution(mesh):
    in_specs = (
        P("wide", None),
        P("wide", None),
        P("wide"),
        P(),
        P("wide", None),
        P(),
        P(None, None, "narrow"),
        P(None, "narrow"),
        P("narrow", None),
        P(None, "narrow"),
        P("narrow", None),
        P(None, None, "narrow"),
        P(),
        P(None, None, "narrow"),
        P(None, "narrow"),
        P("narrow", None),
        P(None, "narrow"),
        P("narrow", None),
        P(None, "narrow"),
        P("narrow", None),
        P("wide", None),
        P(),
    )
    out_specs = (
        P("wide", None),
        P(),
        P("wide", None),
        P("wide", None),
        P(),
        P("wide", None, "narrow"),
        P(None, "narrow"),
        P("narrow", "wide"),
        P("wide", "narrow"),
        P("narrow", "wide"),
        P("wide", None, "narrow"),
        P(),
        P(None, None, "narrow"),
        P(None, "narrow"),
        P("narrow", None),
        P(None, "narrow"),
        P("narrow", None),
        P(None, "narrow"),
        P("narrow", None),
    )
    return jax.shard_map(
        per_device, mesh=mesh, in_specs=in_specs, out_specs=out_specs, check_vma=False
    )
```

time: 1150 us -> 469 us (0.41)
  Pallas kernels: 555 us -> 117 us
  matrix products: 94.8 us -> 0.31 us
  other arithmetic: 79.8 us -> 13.2 us
  local copies, waits for them, and re-layouts: 93.5 us -> 28.4 us
  starting transfers between devices: 120 us -> 108 us
    pallas_call x3 -> x19, Pallas kernels: 555 us -> 117 us  [call(): pl.pallas_call(kernel, out_shape=[jax.ShapeDtypeStruct(shape, dtype) for...]
    dot_general x57 -> x2, matrix products: 94.3 us -> 0.31 us  [the longest x1 0.18 us: per_device(): enc_line = jnp.einsum('zhb,bt->zht', tables, both, precision=FULL)]
    another operation x27 -> x5, other arithmetic: 24.1 us -> 0.93 us  [the longest x1 0.72 us: per_device(): jnp.stack([slab, narrow_at, own_question, lax.axis_index('wide')])]
    eq x2 -> x0, local copies, waits for them, and re-layouts: 13.9 us -> none  [the longest x1 13.1 us: bucket_lookup(): jnp.arange(bucket_count, dtype=jnp.int32)[:, None, None] == buckets[None]]
    ppermute x115 -> x96, starting transfers between devices: 120 us -> 108 us  [swap(): return lax.ppermute(value, axis, [(i, i ^ bit) for i in range(count)])]
    ppermute x115 -> x96, waiting for transfers between devices: 197 us -> 189 us  [swap(): return lax.ppermute(value, axis, [(i, i ^ bit) for i in range(count)])]
  transfers between devices with their start and end apart: 115 -> 96, of which waited for: 38 -> 39; matrix products, arithmetic and copies ran while one was open for 18% -> 5% of each run, Pallas kernels for 23% -> 14%
where the time goes in v2:
time: 469 us; the launch traced here: 460 us
  waiting for transfers between devices  189 us (40%)
  Pallas kernels  117 us (25%)
  starting transfers between devices  108 us (23%)
  local copies, waits for them, and re-layouts  28.4 us (6%)
  other arithmetic  13.2 us (3%)
    ppermute x96, waiting for transfers between devices, swap(): return lax.ppermute(value, axis, [(i, i ^ bit) for i in range(count)])  189 us
    pallas_call x19, Pallas kernels, call(): pl.pallas_call(kernel, out_shape=[jax.ShapeDtypeStruct(shape, dtype) for...  117 us
    ppermute x96, starting transfers between devices, swap(): return lax.ppermute(value, axis, [(i, i ^ bit) for i in range(count)])  108 us
    unnamed x253, local copies, waits for them, and re-layouts  19.7 us
  transfers between devices with their start and end apart: 96, of which 39 were waited for; matrix products, arithmetic and copies ran while one was open for 5% of the time, Pallas kernels for 14%

profile of v2, /device:TPU:0, one launch (start us, length us, event | category | flops | bytes accessed | tf_op | source)
XLA Modules:
  0.0 459.6 jit_solution(10728528445968476356)
XLA Ops:
  1.7 4.1 collective-permute-start.4
  12.0 2.7 copy-done.22
  14.7 3.7 embed_rows.1
  28.6 2.4 collective-permute-start.2
  32.2 5.0 %collective-permute-done = f32[3,32]{1,0:T(4,128)S(1)} collective-permute-done((f32[3,32]{1,0:T(4,128)S(1)}, f32[3,32]{1,0:T(4,128)S(1)}, u32[]{:S(2)}, u32[]{:S(2)}) %collective-permute-start) | collective-permute-done | bytes 416 | tf_op jit(solution)/shard_map/ppermute | solution.py:29
  37.2 3.0 collective-permute-start.36
  40.2 14.8 %collective-permute-start.35 = (bf16[96,768]{1,0:T(8,128)(2,1)S(1)}, bf16[96,768]{1,0:T(8,128)(2,1)S(1)}, u32[]{:S(2)}, u32[]{:S(2)}) collective-permute-start(bf16[96,768]{1,0:T(8,128)(2,1)S(1)} %fusion.37), channel_id=1, source_target_pairs={{0,1},{1,0},{2,3},{3,2},{4,5},{5,4},{6,7},{7,6},{8,9},{9,8},{10,11... | collective-permute-start | bytes 442376 | tf_op jit(solution)/shard_map/ppermute | solution.py:29
  60.9 2.7 collective-permute-done.35
  68.5 4.2 collective-permute-done.6.refs_3_
  72.7 22.6 %collective-permute-done.39.refs_5_ = bf16[3,96,768]{2,1,0:T(8,128)(2,1)S(1)} collective-permute-done((bf16[3,96,768]{2,1,0:T(8,128)(2,1)S(1)}, bf16[3,96,768]{2,1,0:T(8,128)(2,1)S(1)}, u32[]{:S(2)}, u32[]{:S(2)}) %collective-permute-start.39) | collective-permute-done | bytes 442400 | tf_op jit(solution)/shard_map/ppermute | solution.py:29
  95.8 3.4 collective-permute-done.38.refs_4_
  101.2 3.8 collective-permute-done.34.two_ref
  108.0 3.2 collective-permute-done.9.refs_6_
  116.5 7.2 %collective-permute-done.20.refs_5_ = bf16[3,96,768]{2,1,0:T(8,128)(2,1)S(1)} collective-permute-done((bf16[3,96,768]{2,1,0:T(8,128)(2,1)S(1)}, bf16[3,96,768]{2,1,0:T(8,128)(2,1)S(1)}, u32[]{:S(2)}, u32[]{:S(2)}) %collective-permute-start.20) | collective-permute-done | bytes 442400 | tf_op jit(solution)/shard_map/ppermute | solution.py:29
  124.4 13.7 %encoder_attention.1 = (f32[256,768]{1,0:T(8,128)S(1)}, bf16[256,768]{1,0:T(8,128)(2,1)S(1)}, bf16[4,256,576]{2,1,0:T(8,128)(2,1)S(1)}, bf16[4,256,192]{2,1,0:T(8,128)(2,1)S(1)}) custom-call(s32[4]{0:T(128)S(1)} %pad_add_fusion.where_ref, bf16[1024,768]{1,0:T(8,128)(2,1)S(1)} %copy-done.24, s32[4,256]{1,0:T(4,128)S(1)} %copy-done.64, ...), custom_call_target="tpu_custom_call" | custom-call | flops 16499999744 | tf_op jit(solution)/shard_map/encoder_attention/pallas_call | solution.py:175
  142.4 17.5 %encoder_ffn.1 = (bf16[256,768]{1,0:T(8,128)(2,1)S(1)}, bf16[4,256,768]{2,1,0:T(8,128)(2,1)S(1)}, f32[4,256,768]{2,1,0:T(8,128)}, f32[256,768]{1,0:T(8,128)S(1)}, bf16[256,768]{1,0:T(8,128)(2,1)S(1)}) custom-call(s32[4]{0:T(128)S(1)} %pad_add_fusion.where_ref, f32[256,768]{1,0:T(8,128)S(1)} %get-tuple-element.83.hidden_ref, f32[3,768]{1,0:T(4,128)S(1)} %copy-done.61, ...), custom_call_target="tpu_custom_call" | custom-call | flops 18699999232 | tf_op jit(solution)/shard_map/encoder_ffn/pallas_call | solution.py:175
  160.1 11.8 %cross_forward.1 = (f32[40,768]{1,0:T(8,128)S(1)}, bf16[40,768]{1,0:T(8,128)(2,1)S(1)}, bf16[4,40,192]{2,1,0:T(8,128)(2,1)S(1)}, bf16[4,256,384]{2,1,0:T(8,128)(...) custom-call(s32[4]{0:T(128)S(1)} %pad_add_fusion.where_ref, ...), custom_call_target="tpu_custom_call" | custom-call | flops 9900000256 | tf_op jit(solution)/shard_map/cross_forward/pallas_call | solution.py:175
  175.5 4.6 %collective-permute-done.48.two_ref = f32[40,896]{1,0:T(8,128)S(1)} collective-permute-done((f32[40,896]{1,0:T(8,128)S(1)}, f32[40,896]{1,0:T(8,128)S(1)}, u32[]{:S(2)}, u32[]{:S(2)}) %collective-permute-start.48) | collective-permute-done | bytes 143392 | tf_op jit(solution)/shard_map/ppermute | solution.py:29
  181.6 2.8 collective-permute-start.29
  188.6 23.8 %collective-permute-done.50.two_ref = f32[40,896]{1,0:T(8,128)S(1)} collective-permute-done((f32[40,896]{1,0:T(8,128)S(1)}, f32[40,896]{1,0:T(8,128)S(1)}, u32[]{:S(2)}, u32[]{:S(2)}) %collective-permute-start.50) | collective-permute-done | bytes 143392 | tf_op jit(solution)/shard_map/ppermute | solution.py:29
  214.4 9.0 %collective-permute-done.51.two_ref = f32[40,896]{1,0:T(8,128)S(1)} collective-permute-done((f32[40,896]{1,0:T(8,128)S(1)}, f32[40,896]{1,0:T(8,128)S(1)}, u32[]{:S(2)}, u32[]{:S(2)}) %collective-permute-start.51) | collective-permute-done | bytes 143392 | tf_op jit(solution)/shard_map/ppermute | solution.py:29
  225.8 4.8 %collective-permute-done.52 = f32[40,768]{1,0:T(8,128)S(1)} collective-permute-done((f32[40,768]{1,0:T(8,128)S(1)}, f32[40,768]{1,0:T(8,128)S(1)}, u32[]{:S(2)}, u32[]{:S(2)}) %collective-permute-start.52) | collective-permute-done | bytes 122912 | tf_op jit(solution)/shard_map/ppermute | solution.py:29
  230.8 6.5 %collective-permute-done.53.two_ref = f32[40,768]{1,0:T(8,128)S(1)} collective-permute-done((f32[40,768]{1,0:T(8,128)S(1)}, f32[40,768]{1,0:T(8,128)S(1)}, u32[]{:S(2)}, u32[]{:S(2)}) %collective-permute-start.53) | collective-permute-done | bytes 122912 | tf_op jit(solution)/shard_map/ppermute | solution.py:29
  237.3 2.3 copy-done.71
  239.7 6.7 %cross_backward.1 = (f32[40,768]{1,0:T(8,128)S(1)}, bf16[40,768]{1,0:T(8,128)(2,1)S(1)}, bf16[4,256,384]{2,1,0:T(8,128)(2,1)S(1)}, f32[40,768]{1,0:T(8,128)S(1)}...) custom-call(s32[4]{0:T(128)S(1)} %pad_add_fusion.where_ref, ...), custom_call_target="tpu_custom_call" | custom-call | flops 9900000256 | tf_op jit(solution)/shard_map/cross_backward/pallas_call | solution.py:175
  248.9 16.9 %ffn_backward.1 = (bf16[4,256,768]{2,1,0:T(8,128)(2,1)S(1)}, f32[256,768]{1,0:T(8,128)S(1)}, f32[1,768]{1,0:T(1,128)S(1)}) custom-call(s32[4]{0:T(128)S(1)} %pad_add_fusion.where_ref, f32[256,768]{1,0:T(8,128)S(1)} %get-tuple-element.108.grad_ref, f32[4,256,768]{2,1,0:T(8,128)} %get-tuple-element.109.slope_ref, f32[256,768]{1,0:T(8,128)S(1)} %copy-done.109, ...), custom_call_target="tpu_custom_call" | custom-call | flops 18699999232 | tf_op jit(solution)/shard_map/ffn_backward/pallas_call | solution.py:175
  265.9 17.4 %attention_backward.1 = (bf16[256,768]{1,0:T(8,128)(2,1)S(1)}, bf16[4,256,576]{2,1,0:T(8,128)(2,1)S(1)}, bf16[256,768]{1,0:T(8,128)(2,1)S(1)}, f32[16,768]{1,0:T(8,128)S(1)}) custom-call(s32[4]{0:T(128)S(1)} %pad_add_fusion.where_ref, f32[256,768]{1,0:T(8,128)S(1)} %get-tuple-element.110.grad_ref, f32[2,768]{1,0:T(2,128)S(1)} %get-tuple-element.106.refs_1_.known_ref, ...), custom_call_target="tpu_custom_call" | custom-call | flops 16499999744 | tf_op jit(solution)/shard_map/attention_backward/pallas_call | solution.py:175
  285.9 2.9 collective-permute-start.61
  290.8 2.4 grow_weight_grads.1
  294.4 3.4 shrink_weight_grads.1
  301.9 2.9 attention_weight_grads.1
  305.5 4.0 collective-permute-done.67
  309.5 3.4 collective-permute-start.68
  313.2 3.7 decoder_weights.1
  320.7 8.2 %collective-permute-done.58.two_ref = f32[40,768]{1,0:T(8,128)S(1)} collective-permute-done((f32[40,768]{1,0:T(8,128)S(1)}, f32[40,768]{1,0:T(8,128)S(1)}, u32[]{:S(2)}, u32[]{:S(2)}) %collective-permute-start.58) | collective-permute-done | bytes 122912 | tf_op jit(solution)/shard_map/ppermute | solution.py:29
  329.0 4.8 %decoder_backward.1 = (f32[40,768]{1,0:T(8,128)S(1)}, f32[192,768]{1,0:T(8,128)}, f32[192,768]{1,0:T(8,128)}, f32[576,768]{1,0:T(8,128)}, f32[40,768]{1,0:T(8,12...) custom-call(s32[4]{0:T(128)S(1)} %pad_add_fusion.where_ref, f32[40,768]{1,0:T(8,128)S(1)} %add.354.one_ref, ...), custom_call_target="tpu_custom_call" | custom-call | flops 2200000000 | tf_op jit(solution)/shard_map/decoder_backward/pallas_call | solution.py:175
  334.6 7.7 %collective-permute-done.59 = f32[80,768]{1,0:T(8,128)S(1)} collective-permute-done((f32[80,768]{1,0:T(8,128)S(1)}, f32[80,768]{1,0:T(8,128)S(1)}, u32[]{:S(2)}, u32[]{:S(2)}) %collective-permute-start.59) | collective-permute-done | bytes 245792 | tf_op jit(solution)/shard_map/ppermute | solution.py:29
  343.1 2.4 collective-permute-start.71
  345.4 11.4 %collective-permute-done.60.two_ref = f32[80,768]{1,0:T(8,128)S(1)} collective-permute-done((f32[80,768]{1,0:T(8,128)S(1)}, f32[80,768]{1,0:T(8,128)S(1)}, u32[]{:S(2)}, u32[]{:S(2)}) %collective-permute-start.60) | collective-permute-done | bytes 245792 | tf_op jit(solution)/shard_map/ppermute | solution.py:29
  358.6 6.8 %vocabulary_grads.1 = (f32[4016,768]{1,0:T(8,128)}, bf16[40,768]{1,0:T(8,128)(2,1)}, f32[3,768]{1,0:T(4,128)}) custom-call(s32[4]{0:T(128)S(1)} %pad_add_fusion.where_ref, s32[40]{0:T(128)S(1)} %copy-done.68, f32[80,768]{1,0:T(8,128)S(1)} %add.355.one_ref, f32[80,768]{1,0:T(8,128)S(1)} %collective-permute-done.60.two_ref, bf16[40,768]{1,0:T(8,128)(2,1)S(1)} %copy-done.17, ...), custom_call_target="tpu_custom_call" | custom-call | flops 2200000000 | tf_op jit(solution)/shard_map/vocabulary_grads/pallas_call | solution.py:175
  369.7 5.5 %collective-permute-done.80 = bf16[2,96,768]{2,1,0:T(8,128)(2,1)S(1)} collective-permute-done((bf16[2,96,768]{2,1,0:T(8,128)(2,1)S(1)}, bf16[2,96,768]{2,1,0:T(8,128)(2,1)S(1)}, u32[]{:S(2)}, u32[]{:S(2)}) %collective-permute-start.80) | collective-permute-done | bytes 294944 | tf_op jit(solution)/shard_map/ppermute | solution.py:29
  379.7 4.9 %collective-permute-done.89 = bf16[2,96,1152]{2,1,0:T(8,128)(2,1)S(1)} collective-permute-done((bf16[2,96,1152]{2,1,0:T(8,128)(2,1)S(1)}, bf16[2,96,1152]{2,1,0:T(8,128)(2,1)S(1)}, u32[]{:S(2)}, u32[]{:S(2)}) %collective-permute-start.89) | collective-permute-done | bytes 442400 | tf_op jit(solution)/shard_map/ppermute | solution.py:29
  398.1 2.8 collective-permute-done.72
  401.2 8.7 %collective-permute-done.83 = bf16[4,96,768]{2,1,0:T(8,128)(2,1)S(1)} collective-permute-done((bf16[4,96,768]{2,1,0:T(8,128)(2,1)S(1)}, bf16[4,96,768]{2,1,0:T(8,128)(2,1)S(1)}, u32[]{:S(2)}, u32[]{:S(2)}) %collective-permute-start.83) | collective-permute-done | bytes 589856 | tf_op jit(solution)/shard_map/ppermute | solution.py:29
  420.0 6.3 %collective-permute-done.76 = bf16[96,768]{1,0:T(8,128)(2,1)S(1)} collective-permute-done((bf16[96,768]{1,0:T(8,128)(2,1)S(1)}, bf16[96,768]{1,0:T(8,128)(2,1)S(1)}, u32[]{:S(2)}, u32[]{:S(2)}) %collective-permute-start.76) | collective-permute-done | bytes 147488 | tf_op jit(solution)/shard_map/ppermute | solution.py:29
  435.2 5.5 %collective-permute-start.93 = (bf16[96,1152]{1,0:T(8,128)(2,1)S(1)}, bf16[96,1152]{1,0:T(8,128)(2,1)S(1)}, u32[]{:S(2)}, u32[]{:S(2)}) collective-permute-start(bf16[96,1152]{1,0:T(8,128)(2,1)S(1)} %get-tuple-element.185), channel_id=1, source_target_pairs={{0,1},{1,0},{2,3},{3,2},{4,5},{5,4},{6,7},{7,6},{8,9},{9,8},{10,11... | collective-permute-start | bytes 663560 | tf_op jit(solution)/shard_map/ppermute | solution.py:29
  446.3 3.1 collective-permute-done.95
  449.4 7.1 %collective-permute-done.94 = bf16[96,1152]{1,0:T(8,128)(2,1)S(1)} collective-permute-done((bf16[96,1152]{1,0:T(8,128)(2,1)S(1)}, bf16[96,1152]{1,0:T(8,128)(2,1)S(1)}, u32[]{:S(2)}, u32[]{:S(2)}) %collective-permute-start.94) | collective-permute-done | bytes 221216 | tf_op jit(solution)/shard_map/ppermute | solution.py:29
  (495 shorter events, 128.3 us)
Async XLA Ops:
  1.7 23.9 %collective-permute-start.4 = (bf16[96,768]{1,0:T(8,128)(2,1)S(1)}, bf16[96,768]{1,0:T(8,128)(2,1)S(1)}, u32[]{:S(2)}, u32[]{:S(2)}) collective-permute-start(bf16[96,768]{1,0:T(8,128)(2,1)S(1)} %fusion.38), channel_id=1, source_target_pairs={{0,2},{1,3},{2,0},{3,1},{4,6},{5,7},{6,4},{7,5},{8,10},{9,11},{10,... | collective-permute-start | bytes 442376 | tf_op jit(solution)/shard_map/ppermute | solution.py:29
  5.8 21.6 %collective-permute-start.3 = (bf16[96,768]{1,0:T(8,128)(2,1)S(1)}, bf16[96,768]{1,0:T(8,128)(2,1)S(1)}, u32[]{:S(2)}, u32[]{:S(2)}) collective-permute-start(bf16[96,768]{1,0:T(8,128)(2,1)S(1)} %fusion.38), channel_id=1, source_target_pairs={{0,1},{1,0},{2,3},{3,2},{4,5},{5,4},{6,7},{7,6},{8,9},{9,8},{10,11... | collective-permute-start | bytes 442376 | tf_op jit(solution)/shard_map/ppermute | solution.py:29
  7.4 21.3 %collective-permute-start.5 = (bf16[96,768]{1,0:T(8,128)(2,1)S(1)}, bf16[96,768]{1,0:T(8,128)(2,1)S(1)}, u32[]{:S(2)}, u32[]{:S(2)}) collective-permute-start(bf16[96,768]{1,0:T(8,128)(2,1)S(1)} %fusion.38), channel_id=1, source_target_pairs={{0,3},{1,2},{2,1},{3,0},{4,7},{5,6},{6,5},{7,4},{8,11},{9,10},{10,... | collective-permute-start | bytes 442376 | tf_op jit(solution)/shard_map/ppermute | solution.py:29
  7.4 14.1 %collective-permute-start.1 = (f32[3,32]{1,0:T(4,128)}, f32[3,32]{1,0:T(4,128)S(1)}, u32[]{:S(2)}, u32[]{:S(2)}) collective-permute-start(f32[3,32]{1,0:T(4,128)} %bitcast.284), channel_id=1, source_target_pairs={{0,2},{1,3},{2,0},{3,1},{4,6},{5,7},{6,4},{7,5},{8,10},{9,11},{10,... | collective-permute-start | bytes 1160 | tf_op jit(solution)/shard_map/ppermute | solution.py:29
  21.4 33.5 %collective-permute-start.17 = (bf16[192,768]{1,0:T(8,128)(2,1)S(1)}, bf16[192,768]{1,0:T(8,128)(2,1)S(1)}, u32[]{:S(2)}, u32[]{:S(2)}) collective-permute-start(bf16[192,768]{1,0:T(8,128)(2,1)S(1)} %pad_maximum_fusion.9), channel_id=1, source_target_pairs={{0,3},{1,2},{2,1},{3,0},{4,7},{5,6},{6,5},{7,4},{8,11},{9,10},{10,... | collective-permute-start | bytes 884744 | tf_op jit(solution)/shard_map/ppermute | solution.py:29
  24.1 32.7 %collective-permute-start.16 = (bf16[192,768]{1,0:T(8,128)(2,1)S(1)}, bf16[192,768]{1,0:T(8,128)(2,1)S(1)}, u32[]{:S(2)}, u32[]{:S(2)}) collective-permute-start(bf16[192,768]{1,0:T(8,128)(2,1)S(1)} %pad_maximum_fusion.9), channel_id=1, source_target_pairs={{0,2},{1,3},{2,0},{3,1},{4,6},{5,7},{6,4},{7,5},{8,10},{9,11},{10,... | collective-permute-start | bytes 884744 | tf_op jit(solution)/shard_map/ppermute | solution.py:29
  31.1 28.9 %collective-permute-start.15 = (bf16[192,768]{1,0:T(8,128)(2,1)S(1)}, bf16[192,768]{1,0:T(8,128)(2,1)S(1)}, u32[]{:S(2)}, u32[]{:S(2)}) collective-permute-start(bf16[192,768]{1,0:T(8,128)(2,1)S(1)} %pad_maximum_fusion.9), channel_id=1, source_target_pairs={{0,1},{1,0},{2,3},{3,2},{4,5},{5,4},{6,7},{7,6},{8,9},{9,8},{10,11... | collective-permute-start | bytes 884744 | tf_op jit(solution)/shard_map/ppermute | solution.py:29
  37.2 23.6 %collective-permute-start.36 = (bf16[96,768]{1,0:T(8,128)(2,1)S(1)}, bf16[96,768]{1,0:T(8,128)(2,1)S(1)}, u32[]{:S(2)}, u32[]{:S(2)}) collective-permute-start(bf16[96,768]{1,0:T(8,128)(2,1)S(1)} %fusion.37), channel_id=1, source_target_pairs={{0,2},{1,3},{2,0},{3,1},{4,6},{5,7},{6,4},{7,5},{8,10},{9,11},{10,... | collective-permute-start | bytes 442376 | tf_op jit(solution)/shard_map/ppermute | solution.py:29
  40.2 23.5 %collective-permute-start.35 = (bf16[96,768]{1,0:T(8,128)(2,1)S(1)}, bf16[96,768]{1,0:T(8,128)(2,1)S(1)}, u32[]{:S(2)}, u32[]{:S(2)}) collective-permute-start(bf16[96,768]{1,0:T(8,128)(2,1)S(1)} %fusion.37), channel_id=1, source_target_pairs={{0,1},{1,0},{2,3},{3,2},{4,5},{5,4},{6,7},{7,6},{8,9},{9,8},{10,11... | collective-permute-start | bytes 442376 | tf_op jit(solution)/shard_map/ppermute | solution.py:29
  63.6 43.7 %collective-permute-start.19 = (bf16[3,192,768]{2,1,0:T(8,128)(2,1)S(1)}, bf16[3,192,768]{2,1,0:T(8,128)(2,1)S(1)}, u32[]{:S(2)}, u32[]{:S(2)}) collective-permute-start(bf16[3,192,768]{2,1,0:T(8,128)(2,1)S(1)} %pad_maximum_fusion.refs_2_), channel_id=1, source_target_pairs={{0,16},{4,20},{8,24},{12,28},{16,0},{20,4},{24,8},{28,12},{1,17},{... | collective-permute-start | bytes 2654216 | tf_op jit(solution)/shard_map/ppermute | solution.py:29
  64.9 42.5 %collective-permute-start.18 = (bf16[3,192,768]{2,1,0:T(8,128)(2,1)S(1)}, bf16[3,192,768]{2,1,0:T(8,128)(2,1)S(1)}, u32[]{:S(2)}, u32[]{:S(2)}) collective-permute-start(bf16[3,192,768]{2,1,0:T(8,128)(2,1)S(1)} %pad_maximum_fusion.refs_2_), channel_id=1, source_target_pairs={{0,8},{4,12},{8,0},{12,4},{16,24},{20,28},{24,16},{28,20},{1,9},{5... | collective-permute-start | bytes 2654216 | tf_op jit(solution)/shard_map/ppermute | solution.py:29
  66.4 28.9 %collective-permute-start.39 = (bf16[3,96,768]{2,1,0:T(8,128)(2,1)S(1)}, bf16[3,96,768]{2,1,0:T(8,128)(2,1)S(1)}, u32[]{:S(2)}, u32[]{:S(2)}) collective-permute-start(bf16[3,96,768]{2,1,0:T(8,128)(2,1)S(1)} %pad_maximum_fusion.8.refs_3_), channel_id=1, source_target_pairs={{0,16},{4,20},{8,24},{12,28},{16,0},{20,4},{24,8},{28,12},{1,17},{... | collective-permute-start | bytes 1327112 | tf_op jit(solution)/shard_map/ppermute | solution.py:29
  67.9 31.3 %collective-permute-start.38 = (bf16[3,96,768]{2,1,0:T(8,128)(2,1)S(1)}, bf16[3,96,768]{2,1,0:T(8,128)(2,1)S(1)}, u32[]{:S(2)}, u32[]{:S(2)}) collective-permute-start(bf16[3,96,768]{2,1,0:T(8,128)(2,1)S(1)} %pad_maximum_fusion.8.refs_3_), channel_id=1, source_target_pairs={{0,8},{4,12},{8,0},{12,4},{16,24},{20,28},{24,16},{28,20},{1,9},{5... | collective-permute-start | bytes 1327112 | tf_op jit(solution)/shard_map/ppermute | solution.py:29
  72.6 33.5 %collective-permute-start.10 = (bf16[3,96,768]{2,1,0:T(8,128)(2,1)S(1)}, bf16[3,96,768]{2,1,0:T(8,128)(2,1)S(1)}, u32[]{:S(2)}, u32[]{:S(2)}) collective-permute-start(bf16[3,96,768]{2,1,0:T(8,128)(2,1)S(1)} %pad_maximum_fusion.7.refs_2_), channel_id=1, source_target_pairs={{0,4},{4,0},{8,12},{12,8},{16,20},{20,16},{24,28},{28,24},{1,5},{5... | collective-permute-start | bytes 1327112 | tf_op jit(solution)/shard_map/ppermute | solution.py:29
  114.8 26.1 %collective-permute-start.22 = (bf16[3,192,768]{2,1,0:T(8,128)(2,1)S(1)}, bf16[3,192,768]{2,1,0:T(8,128)(2,1)S(1)}, u32[]{:S(2)}, u32[]{:S(2)}) collective-permute-start(bf16[3,192,768]{2,1,0:T(8,128)(2,1)S(1)} %pad_maximum_fusion.refs_2_), channel_id=1, source_target_pairs={{0,4},{4,0},{8,12},{12,8},{16,20},{20,16},{24,28},{28,24},{1,5},{5... | collective-permute-start | bytes 2654216 | tf_op jit(solution)/shard_map/ppermute | solution.py:29
  116.0 25.4 %collective-permute-start.24 = (bf16[3,192,768]{2,1,0:T(8,128)(2,1)S(1)}, bf16[3,192,768]{2,1,0:T(8,128)(2,1)S(1)}, u32[]{:S(2)}, u32[]{:S(2)}) collective-permute-start(bf16[3,192,768]{2,1,0:T(8,128)(2,1)S(1)} %collective-permute-done.19.refs_4_), channel_id=1, source_target_pairs={{0,4},{4,0},{8,12},{12,8},{16,20},{20,16},{24,28},{28,24},{1,5},{5... | collective-permute-start | bytes 2654216 | tf_op jit(solution)/shard_map/ppermute | solution.py:29
  116.2 25.8 %collective-permute-start.23 = (bf16[3,192,768]{2,1,0:T(8,128)(2,1)S(1)}, bf16[3,192,768]{2,1,0:T(8,128)(2,1)S(1)}, u32[]{:S(2)}, u32[]{:S(2)}) collective-permute-start(bf16[3,192,768]{2,1,0:T(8,128)(2,1)S(1)} %collective-permute-done.18.refs_3_), channel_id=1, source_target_pairs={{0,4},{4,0},{8,12},{12,8},{16,20},{20,16},{24,28},{28,24},{1,5},{5... | collective-permute-start | bytes 2654216 | tf_op jit(solution)/shard_map/ppermute | solution.py:29
  123.8 17.6 %collective-permute-start.25 = (bf16[3,96,768]{2,1,0:T(8,128)(2,1)S(1)}, bf16[3,96,768]{2,1,0:T(8,128)(2,1)S(1)}, u32[]{:S(2)}, u32[]{:S(2)}) collective-permute-start(bf16[3,96,768]{2,1,0:T(8,128)(2,1)S(1)} %collective-permute-done.20.refs_5_), channel_id=1, source_target_pairs={{0,4},{4,0},{8,12},{12,8},{16,20},{20,16},{24,28},{28,24},{1,5},{5... | collective-permute-start | bytes 1327112 | tf_op jit(solution)/shard_map/ppermute | solution.py:29
  124.4 17.5 %collective-permute-start.26 = (bf16[3,96,768]{2,1,0:T(8,128)(2,1)S(1)}, bf16[3,96,768]{2,1,0:T(8,128)(2,1)S(1)}, u32[]{:S(2)}, u32[]{:S(2)}) collective-permute-start(bf16[3,96,768]{2,1,0:T(8,128)(2,1)S(1)} %collective-permute-done.21.refs_6_), channel_id=1, source_target_pairs={{0,4},{4,0},{8,12},{12,8},{16,20},{20,16},{24,28},{28,24},{1,5},{5... | collective-permute-start | bytes 1327112 | tf_op jit(solution)/shard_map/ppermute | solution.py:29
  140.9 19.1 %collective-permute-start.42 = (bf16[3,96,768]{2,1,0:T(8,128)(2,1)S(1)}, bf16[3,96,768]{2,1,0:T(8,128)(2,1)S(1)}, u32[]{:S(2)}, u32[]{:S(2)}) collective-permute-start(bf16[3,96,768]{2,1,0:T(8,128)(2,1)S(1)} %pad_maximum_fusion.8.refs_3_), channel_id=1, source_target_pairs={{0,4},{4,0},{8,12},{12,8},{16,20},{20,16},{24,28},{28,24},{1,5},{5... | collective-permute-start | bytes 1327112 | tf_op jit(solution)/shard_map/ppermute | solution.py:29
  141.4 18.7 %collective-permute-start.44 = (bf16[3,96,768]{2,1,0:T(8,128)(2,1)S(1)}, bf16[3,96,768]{2,1,0:T(8,128)(2,1)S(1)}, u32[]{:S(2)}, u32[]{:S(2)}) collective-permute-start(bf16[3,96,768]{2,1,0:T(8,128)(2,1)S(1)} %collective-permute-done.39.refs_5_), channel_id=1, source_target_pairs={{0,4},{4,0},{8,12},{12,8},{16,20},{20,16},{24,28},{28,24},{1,5},{5... | collective-permute-start | bytes 1327112 | tf_op jit(solution)/shard_map/ppermute | solution.py:29
  141.5 18.6 %collective-permute-start.43 = (bf16[3,96,768]{2,1,0:T(8,128)(2,1)S(1)}, bf16[3,96,768]{2,1,0:T(8,128)(2,1)S(1)}, u32[]{:S(2)}, u32[]{:S(2)}) collective-permute-start(bf16[3,96,768]{2,1,0:T(8,128)(2,1)S(1)} %collective-permute-done.38.refs_4_), channel_id=1, source_target_pairs={{0,4},{4,0},{8,12},{12,8},{16,20},{20,16},{24,28},{28,24},{1,5},{5... | collective-permute-start | bytes 1327112 | tf_op jit(solution)/shard_map/ppermute | solution.py:29
  141.9 18.1 %collective-permute-start.45 = (bf16[3,48,768]{2,1,0:T(8,128)(2,1)S(1)}, bf16[3,48,768]{2,1,0:T(8,128)(2,1)S(1)}, u32[]{:S(2)}, u32[]{:S(2)}) collective-permute-start(bf16[3,48,768]{2,1,0:T(8,128)(2,1)S(1)} %collective-permute-done.40.refs_6_), channel_id=1, source_target_pairs={{0,4},{4,0},{8,12},{12,8},{16,20},{20,16},{24,28},{28,24},{1,5},{5... | collective-permute-start | bytes 663560 | tf_op jit(solution)/shard_map/ppermute | solution.py:29
  142.0 18.1 %collective-permute-start.46 = (bf16[3,48,768]{2,1,0:T(8,128)(2,1)S(1)}, bf16[3,48,768]{2,1,0:T(8,128)(2,1)S(1)}, u32[]{:S(2)}, u32[]{:S(2)}) collective-permute-start(bf16[3,48,768]{2,1,0:T(8,128)(2,1)S(1)} %collective-permute-done.41.refs_7_), channel_id=1, source_target_pairs={{0,4},{4,0},{8,12},{12,8},{16,20},{20,16},{24,28},{28,24},{1,5},{5... | collective-permute-start | bytes 663560 | tf_op jit(solution)/shard_map/ppermute | solution.py:29
  181.6 49.1 %collective-permute-start.29 = (bf16[256,768]{1,0:T(8,128)(2,1)S(1)}, bf16[256,768]{1,0:T(8,128)(2,1)S(1)}, u32[]{:S(2)}, u32[]{:S(2)}) collective-permute-start(bf16[256,768]{1,0:T(8,128)(2,1)S(1)} %get-tuple-element.84.memory_ref.refs_1_), channel_id=1, source_target_pairs={{0,3},{1,2},{2,1},{3,0},{4,7},{5,6},{6,5},{7,4},{8,11},{9,10},{10,... | collective-permute-start | bytes 1179656 | tf_op jit(solution)/shard_map/ppermute | solution.py:29
  184.4 41.3 %collective-permute-start.28 = (bf16[256,768]{1,0:T(8,128)(2,1)S(1)}, bf16[256,768]{1,0:T(8,128)(2,1)S(1)}, u32[]{:S(2)}, u32[]{:S(2)}) collective-permute-start(bf16[256,768]{1,0:T(8,128)(2,1)S(1)} %get-tuple-element.84.memory_ref.refs_1_), channel_id=1, source_target_pairs={{0,2},{1,3},{2,0},{3,1},{4,6},{5,7},{6,4},{7,5},{8,10},{9,11},{10,... | collective-permute-start | bytes 1179656 | tf_op jit(solution)/shard_map/ppermute | solution.py:29
  184.4 29.9 %collective-permute-start.27 = (bf16[256,768]{1,0:T(8,128)(2,1)S(1)}, bf16[256,768]{1,0:T(8,128)(2,1)S(1)}, u32[]{:S(2)}, u32[]{:S(2)}) collective-permute-start(bf16[256,768]{1,0:T(8,128)(2,1)S(1)} %get-tuple-element.84.memory_ref.refs_1_), channel_id=1, source_target_pairs={{0,1},{1,0},{2,3},{3,2},{4,5},{5,4},{6,7},{7,6},{8,9},{9,8},{10,11... | collective-permute-start | bytes 1179656 | tf_op jit(solution)/shard_map/ppermute | solution.py:29
  187.2 25.2 %collective-permute-start.50 = (f32[40,896]{1,0:T(8,128)S(1)}, f32[40,896]{1,0:T(8,128)S(1)}, u32[]{:S(2)}, u32[]{:S(2)}) collective-permute-start(f32[40,896]{1,0:T(8,128)S(1)} %merge_stats.6.one_ref), channel_id=1, source_target_pairs={{0,1},{1,0},{2,3},{3,2},{4,5},{5,4},{6,7},{7,6},{8,9},{9,8},{10,11... | collective-permute-start | bytes 430088 | tf_op jit(solution)/shard_map/ppermute | solution.py:29
  284.4 49.4 %collective-permute-start.63 = (bf16[256,768]{1,0:T(8,128)(2,1)S(1)}, bf16[256,768]{1,0:T(8,128)(2,1)S(1)}, u32[]{:S(2)}, u32[]{:S(2)}) collective-permute-start(bf16[256,768]{1,0:T(8,128)(2,1)S(1)} %get-tuple-element.113), channel_id=1, source_target_pairs={{0,3},{1,2},{2,1},{3,0},{4,7},{5,6},{6,5},{7,4},{8,11},{9,10},{10,... | collective-permute-start | bytes 1179656 | tf_op jit(solution)/shard_map/ppermute | solution.py:29
  285.9 48.5 %collective-permute-start.62 = (bf16[256,768]{1,0:T(8,128)(2,1)S(1)}, bf16[256,768]{1,0:T(8,128)(2,1)S(1)}, u32[]{:S(2)}, u32[]{:S(2)}) collective-permute-start(bf16[256,768]{1,0:T(8,128)(2,1)S(1)} %get-tuple-element.113), channel_id=1, source_target_pairs={{0,2},{1,3},{2,0},{3,1},{4,6},{5,7},{6,4},{7,5},{8,10},{9,11},{10,... | collective-permute-start | bytes 1179656 | tf_op jit(solution)/shard_map/ppermute | solution.py:29
  285.9 34.2 %collective-permute-start.61 = (bf16[256,768]{1,0:T(8,128)(2,1)S(1)}, bf16[256,768]{1,0:T(8,128)(2,1)S(1)}, u32[]{:S(2)}, u32[]{:S(2)}) collective-permute-start(bf16[256,768]{1,0:T(8,128)(2,1)S(1)} %get-tuple-element.113), channel_id=1, source_target_pairs={{0,1},{1,0},{2,3},{3,2},{4,5},{5,4},{6,7},{7,6},{8,9},{9,8},{10,11... | collective-permute-start | bytes 1179656 | tf_op jit(solution)/shard_map/ppermute | solution.py:29
  318.3 16.2 %collective-permute-start.70 = (bf16[4,96,768]{2,1,0:T(8,128)(2,1)S(1)}, bf16[4,96,768]{2,1,0:T(8,128)(2,1)S(1)}, u32[]{:S(2)}, u32[]{:S(2)}) collective-permute-start(bf16[4,96,768]{2,1,0:T(8,128)(2,1)S(1)} %get-tuple-element.122), channel_id=1, source_target_pairs={{0,4},{4,0},{8,12},{12,8},{16,20},{20,16},{24,28},{28,24},{1,5},{5... | collective-permute-start | bytes 1769480 | tf_op jit(solution)/shard_map/ppermute | solution.py:29
  319.7 48.4 %collective-permute-start.69 = (bf16[3,4,96,768]{3,2,1,0:T(8,128)(2,1)S(1)}, bf16[3,4,96,768]{3,2,1,0:T(8,128)(2,1)S(1)}, u32[]{:S(2)}, u32[]{:S(2)}) collective-permute-start(bf16[3,4,96,768]{3,2,1,0:T(8,128)(2,1)S(1)} %get-tuple-element.121), channel_id=1, source_target_pairs={{0,4},{4,0},{8,12},{12,8},{16,20},{20,16},{24,28},{28,24},{1,5},{5... | collective-permute-start | bytes 5308424 | tf_op jit(solution)/shard_map/ppermute | solution.py:29
  334.5 43.6 %collective-permute-start.78 = (bf16[3,4,96,768]{3,2,1,0:T(8,128)(2,1)S(1)}, bf16[3,4,96,768]{3,2,1,0:T(8,128)(2,1)S(1)}, u32[]{:S(2)}, u32[]{:S(2)}) collective-permute-start(bf16[3,4,96,768]{3,2,1,0:T(8,128)(2,1)S(1)} %get-tuple-element.126), channel_id=1, source_target_pairs={{0,4},{4,0},{8,12},{12,8},{16,20},{20,16},{24,28},{28,24},{1,5},{5... | collective-permute-start | bytes 5308424 | tf_op jit(solution)/shard_map/ppermute | solution.py:29
  342.3 46.8 %collective-permute-start.87 = (bf16[3,4,96,1152]{3,2,1,0:T(8,128)(2,1)S(1)}, bf16[3,4,96,1152]{3,2,1,0:T(8,128)(2,1)S(1)}, u32[]{:S(2)}, u32[]{:S(2)}) collective-permute-start(bf16[3,4,96,1152]{3,2,1,0:T(8,128)(2,1)S(1)} %get-tuple-element.132), channel_id=1, source_target_pairs={{0,4},{4,0},{8,12},{12,8},{16,20},{20,16},{24,28},{28,24},{1,5},{5... | collective-permute-start | bytes 7962632 | tf_op jit(solution)/shard_map/ppermute | solution.py:29
  342.5 14.3 %collective-permute-start.60 = (f32[80,768]{1,0:T(8,128)S(1)}, f32[80,768]{1,0:T(8,128)S(1)}, u32[]{:S(2)}, u32[]{:S(2)}) collective-permute-start(f32[80,768]{1,0:T(8,128)S(1)} %add.355.one_ref), channel_id=1, source_target_pairs={{0,2},{1,3},{2,0},{3,1},{4,6},{5,7},{6,4},{7,5},{8,10},{9,11},{10,... | collective-permute-start | bytes 737288 | tf_op jit(solution)/shard_map/ppermute | solution.py:29
  343.1 22.3 %collective-permute-start.71 = (bf16[2,96,768]{2,1,0:T(8,128)(2,1)S(1)}, bf16[2,96,768]{2,1,0:T(8,128)(2,1)S(1)}, u32[]{:S(2)}, u32[]{:S(2)}) collective-permute-start(bf16[2,96,768]{2,1,0:T(8,128)(2,1)S(1)} %get-tuple-element.210), channel_id=1, source_target_pairs={{0,16},{4,20},{8,24},{12,28},{16,0},{20,4},{24,8},{28,12},{1,17},{... | collective-permute-start | bytes 884744 | tf_op jit(solution)/shard_map/ppermute | solution.py:29
  368.2 16.5 %collective-permute-start.89 = (bf16[2,96,1152]{2,1,0:T(8,128)(2,1)S(1)}, bf16[2,96,1152]{2,1,0:T(8,128)(2,1)S(1)}, u32[]{:S(2)}, u32[]{:S(2)}) collective-permute-start(bf16[2,96,1152]{2,1,0:T(8,128)(2,1)S(1)} %get-tuple-element.198), channel_id=1, source_target_pairs={{0,16},{4,20},{8,24},{12,28},{16,0},{20,4},{24,8},{28,12},{1,17},{... | collective-permute-start | bytes 1327112 | tf_op jit(solution)/shard_map/ppermute | solution.py:29
  376.0 21.3 %collective-permute-start.74 = (bf16[4,96,768]{2,1,0:T(8,128)(2,1)S(1)}, bf16[4,96,768]{2,1,0:T(8,128)(2,1)S(1)}, u32[]{:S(2)}, u32[]{:S(2)}) collective-permute-start(bf16[4,96,768]{2,1,0:T(8,128)(2,1)S(1)} %pad_maximum_fusion.4), channel_id=1, source_target_pairs={{0,16},{4,20},{8,24},{12,28},{16,0},{20,4},{24,8},{28,12},{1,17},{... | collective-permute-start | bytes 1769480 | tf_op jit(solution)/shard_map/ppermute | solution.py:29
  378.1 22.9 %collective-permute-start.72 = (bf16[4,96,768]{2,1,0:T(8,128)(2,1)S(1)}, bf16[4,96,768]{2,1,0:T(8,128)(2,1)S(1)}, u32[]{:S(2)}, u32[]{:S(2)}) collective-permute-start(bf16[4,96,768]{2,1,0:T(8,128)(2,1)S(1)} %pad_maximum_fusion.3), channel_id=1, source_target_pairs={{0,8},{4,12},{8,0},{12,4},{16,24},{20,28},{24,16},{28,20},{1,9},{5... | collective-permute-start | bytes 1769480 | tf_op jit(solution)/shard_map/ppermute | solution.py:29
  384.7 25.3 %collective-permute-start.83 = (bf16[4,96,768]{2,1,0:T(8,128)(2,1)S(1)}, bf16[4,96,768]{2,1,0:T(8,128)(2,1)S(1)}, u32[]{:S(2)}, u32[]{:S(2)}) collective-permute-start(bf16[4,96,768]{2,1,0:T(8,128)(2,1)S(1)} %pad_maximum_fusion.6), channel_id=1, source_target_pairs={{0,16},{4,20},{8,24},{12,28},{16,0},{20,4},{24,8},{28,12},{1,17},{... | collective-permute-start | bytes 1769480 | tf_op jit(solution)/shard_map/ppermute | solution.py:29
  388.3 25.3 %collective-permute-start.81 = (bf16[4,96,768]{2,1,0:T(8,128)(2,1)S(1)}, bf16[4,96,768]{2,1,0:T(8,128)(2,1)S(1)}, u32[]{:S(2)}, u32[]{:S(2)}) collective-permute-start(bf16[4,96,768]{2,1,0:T(8,128)(2,1)S(1)} %pad_maximum_fusion.5), channel_id=1, source_target_pairs={{0,8},{4,12},{8,0},{12,4},{16,24},{20,28},{24,16},{28,20},{1,9},{5... | collective-permute-start | bytes 1769480 | tf_op jit(solution)/shard_map/ppermute | solution.py:29
  392.0 41.3 %collective-permute-start.92 = (bf16[4,96,1152]{2,1,0:T(8,128)(2,1)}, bf16[4,96,1152]{2,1,0:T(8,128)(2,1)}, u32[]{:S(2)}, u32[]{:S(2)}) collective-permute-start(bf16[4,96,1152]{2,1,0:T(8,128)(2,1)} %pad_maximum_fusion.2), channel_id=1, source_target_pairs={{0,16},{4,20},{8,24},{12,28},{16,0},{20,4},{24,8},{28,12},{1,17},{... | collective-permute-start | bytes 2654216 | tf_op jit(solution)/shard_map/ppermute | solution.py:29
  397.3 35.9 %collective-permute-start.90 = (bf16[4,96,1152]{2,1,0:T(8,128)(2,1)}, bf16[4,96,1152]{2,1,0:T(8,128)(2,1)}, u32[]{:S(2)}, u32[]{:S(2)}) collective-permute-start(bf16[4,96,1152]{2,1,0:T(8,128)(2,1)} %pad_maximum_fusion.1), channel_id=1, source_target_pairs={{0,8},{4,12},{8,0},{12,4},{16,24},{20,28},{24,16},{28,20},{1,9},{5... | collective-permute-start | bytes 2654216 | tf_op jit(solution)/shard_map/ppermute | solution.py:29
  414.6 26.2 %collective-permute-start.84 = (bf16[96,768]{1,0:T(8,128)(2,1)}, bf16[96,768]{1,0:T(8,128)(2,1)}, u32[]{:S(2)}, u32[]{:S(2)}) collective-permute-start(bf16[96,768]{1,0:T(8,128)(2,1)} %get-tuple-element.192), channel_id=1, source_target_pairs={{0,1},{1,0},{2,3},{3,2},{4,5},{5,4},{6,7},{7,6},{8,9},{9,8},{10,11... | collective-permute-start | bytes 442376 | tf_op jit(solution)/shard_map/ppermute | solution.py:29
  418.6 23.6 %collective-permute-start.86 = (bf16[96,768]{1,0:T(8,128)(2,1)}, bf16[96,768]{1,0:T(8,128)(2,1)}, u32[]{:S(2)}, u32[]{:S(2)}) collective-permute-start(bf16[96,768]{1,0:T(8,128)(2,1)} %get-tuple-element.193), channel_id=1, source_target_pairs={{0,3},{1,2},{2,1},{3,0},{4,7},{5,6},{6,5},{7,4},{8,11},{9,10},{10,... | collective-permute-start | bytes 442376 | tf_op jit(solution)/shard_map/ppermute | solution.py:29
  426.4 15.9 %collective-permute-start.85 = (bf16[96,768]{1,0:T(8,128)(2,1)}, bf16[96,768]{1,0:T(8,128)(2,1)}, u32[]{:S(2)}, u32[]{:S(2)}) collective-permute-start(bf16[96,768]{1,0:T(8,128)(2,1)} %get-tuple-element.194), channel_id=1, source_target_pairs={{0,2},{1,3},{2,0},{3,1},{4,6},{5,7},{6,4},{7,5},{8,10},{9,11},{10,... | collective-permute-start | bytes 442376 | tf_op jit(solution)/shard_map/ppermute | solution.py:29
  440.7 15.7 %collective-permute-start.94 = (bf16[96,1152]{1,0:T(8,128)(2,1)S(1)}, bf16[96,1152]{1,0:T(8,128)(2,1)S(1)}, u32[]{:S(2)}, u32[]{:S(2)}) collective-permute-start(bf16[96,1152]{1,0:T(8,128)(2,1)S(1)} %get-tuple-element.187), channel_id=1, source_target_pairs={{0,2},{1,3},{2,0},{3,1},{4,6},{5,7},{6,4},{7,5},{8,10},{9,11},{10,... | collective-permute-start | bytes 663560 | tf_op jit(solution)/shard_map/ppermute | solution.py:29
  (173 other events, 2743.7 us)
